TPU v7x, 32 devices: a whole 2x2x4 slice. The times are simulated.
32 devices in a mesh: colony: 8 (over z, y), fsdp: 4 (over x, core).
Axes of the slice: x: 2, y: 2, z: 4, core: 2. Of those that a mesh axis runs over, the one named last changes fastest.
Arguments:
- hidden_states: bfloat16 [8, 512, 4096], P('colony', 'fsdp'), may hold values from -40 to 40
- norm_gain: float32 [4096], replicated, may hold values from 0.25 to 1.75
- gate_weight: bfloat16 [4096, 7168], P(None, 'fsdp'), may hold values from -0.09375 to 0.09375
- up_weight: bfloat16 [4096, 7168], P(None, 'fsdp'), may hold values from -0.09375 to 0.09375
- hidden_grad: bfloat16 [8, 512, 7168], P('colony', 'fsdp'), may hold values from -2 to 2
- byz_order: int32 [8], replicated, may hold values from 0 to 7, each once
- byz_scale: float32 [3], replicated, may hold values from 2 to 6
Outputs:
- median_gate: float32 [4096, 7168], P('colony', 'fsdp')
- median_up: float32 [4096, 7168], P('colony', 'fsdp')
All inputs are finite; a program needn't handle non-finite values.
Results may differ from a plain program's by a relative error of at most 0.002.
The roundings to bfloat16 on the way count: a program that leaves them out, or rounds other values in their place, can miss the bound.
Values may be sent and summed in bfloat16 or wider, within the bound.
No kernel may reach another device: no remote copies, remote signals or barrier semaphores. Data moves between devices by JAX's collectives and lax.ppermute only.
A program may use at most 192 MiB of HBM per device.

v0:
```python
import jax
import jax.numpy as jnp
from jax import lax
from jax.sharding import PartitionSpec as P

NBYZ = 3
ITERS = 3


def backward_grads(normed_all, cotangent, gate_weight, up_weight):
    gate = jnp.dot(normed_all, gate_weight, preferred_element_type=jnp.float32)
    up = jnp.dot(normed_all, up_weight, preferred_element_type=jnp.float32)
    sig = jax.nn.sigmoid(gate)
    back = cotangent.astype(jnp.float32)
    d_up = (back * gate * sig).astype(jnp.bfloat16)
    d_gate = (back * up * sig * (1.0 + gate * (1.0 - sig))).astype(jnp.bfloat16)
    return (d_gate, d_up)


def token_contract(normed_all, delta):
    dims = (((0,), (0,)), ((), ()))
    return lax.dot_general(normed_all, delta, dims, preferred_element_type=jnp.float32).astype(
        jnp.bfloat16
    )


def on_device(hidden_states, norm_gain, gate_weight, up_weight, hidden_grad, byz_order, byz_scale):
    values = hidden_states[0].astype(jnp.float32)
    meansq = jnp.mean(values * values, axis=-1, keepdims=True)
    normed = (values * lax.rsqrt(meansq + 1e-05) * norm_gain).astype(jnp.bfloat16)
    normed_all = lax.all_gather(normed, "fsdp", axis=0, tiled=True)
    cotangent = lax.all_to_all(hidden_grad[0], "fsdp", split_axis=1, concat_axis=0, tiled=True)
    d_gate, d_up = backward_grads(normed_all, cotangent, gate_weight, up_weight)
    grad_gate = token_contract(normed_all, d_gate)
    grad_up = token_contract(normed_all, d_up)
    stacked = jnp.stack([grad_gate, grad_up])[None]
    pieces = lax.all_to_all(stacked, "colony", split_axis=2, concat_axis=0, tiled=True)
    count = lax.axis_size("colony")
    colonies = jnp.arange(count, dtype=jnp.int32)
    hits = byz_order[:NBYZ][:, None] == colonies[None, :]
    factor = 1.0 + jnp.sum(jnp.where(hits, -byz_scale[:, None] - 1.0, jnp.float32(0.0)), axis=0)

    def combine(coef):
        return jnp.sum(coef[:, None, None, None] * pieces.astype(jnp.float32), axis=0)

    median = combine(factor / count)
    for step in range(ITERS):
        diff = factor[:, None, None, None] * pieces.astype(jnp.float32) - median[None]
        partial_value = jnp.sum(diff * diff, axis=(1, 2, 3))
        dist = jnp.sqrt(lax.psum(partial_value, ("colony", "fsdp")) + 1e-06)
        weights = 1.0 / dist
        median = combine(weights * factor / jnp.sum(weights))
    return (median[0], median[1])


def solution(mesh):
    placed = (
        P("colony", "fsdp", None),
        P(),
        P(None, "fsdp"),
        P(None, "fsdp"),
        P("colony", "fsdp", None),
        P(),
        P(),
    )
    return jax.shard_map(
        on_device,
        mesh=mesh,
        in_specs=placed,
        out_specs=(P("colony", "fsdp"), P("colony", "fsdp")),
        check_vma=False,
    )
```

profile of v0, /device:TPU:0, one launch (start us, length us, event | category | flops | bytes accessed | tf_op | source)
XLA Modules:
  0.0 1383.3 jit_solution(15164193950256069921)
XLA Ops:
  7.2 0.0 all-gather.2.cloned.1.call-start
  7.2 1.5 fusion.20
  8.7 2.5 fusion.22
  11.3 0.0 all-gather.2.cloned.1.call-update
  11.3 3.6 all_to_all.7
  14.9 0.2 copy.14
  15.1 44.7 %all_to_all.22 = bf16[128,4,1792]{2,0,1:T(8,128)(2,1)S(1)} all-to-all(bf16[128,4,1792]{2,0,1:T(8,128)(2,1)S(1)} %copy.14), channel_id=1, replica_groups=mesh['colony'=8,'fsdp'=4] {'fsdp'}, dimensions={1} | all-to-all | bytes 3670016 | tf_op jit(solution)/shard_map/all_to_all | solution.py:32
  59.8 6.3 all-gather.2.cloned.1.call-done
  66.1 0.0 copy-start
  66.1 15.8 %fusion.19 = (bf16[512,1792]{1,0:T(8,128)(2,1)S(1)}, f32[512,1792]{1,0:T(8,128)S(1)}) fusion(bf16[128,4,1792]{2,0,1:T(8,128)(2,1)S(1)} %all_to_all.22, bf16[512,4096]{1,0:T(8,128)(2,1)} %all-gather.2.cloned.1.call-done, bf16[4096,1792]{1,0:T(8,128)(2,1)} %param.9), kind=kOutput, calls=%fused_computation.31 | convolution fusion | flops 7522615296 | bytes 26214400 | tf_op jit(solution)/shard_map/dot_general | solution.py:11
  81.9 0.0 copy-done
  81.9 12.9 fusion.17
  94.9 11.1 fusion.13
  105.9 11.4 fusion.14
  117.3 20.6 %maximum_bitcast_fusion = bf16[1,2,4096,1792]{3,2,1,0:T(8,128)(2,1)} fusion(bf16[1,4096,1792]{2,1,0:T(8,128)(2,1)} %fusion.14, bf16[1,4096,1792]{2,1,0:T(8,128)(2,1)} %fusion.13), kind=kLoop, calls=%fused_computation.18 | loop fusion | flops 14680064 | bytes 58720256 | tf_op jit(solution)/shard_map/broadcast_in_dim | solution.py:36
  137.9 53.1 %copy.15 = bf16[1,2,4096,1792]{3,1,0,2:T(2,128)(2,1)} copy(bf16[1,2,4096,1792]{3,2,1,0:T(8,128)(2,1)} %maximum_bitcast_fusion) | data formatting | bytes 58720256 | tf_op jit(solution)/shard_map/broadcast_in_dim | solution.py:36
  191.1 0.0 copy-start.1
  191.1 0.0 copy-start.2
  191.1 6.9 all-to-all-start.1
  198.0 0.0 copy-done.1
  198.0 0.0 copy-done.2
  198.0 0.1 select_reduce_fusion
  198.1 633.0 %all-to-all-done.1 = bf16[1,2,4096,1792]{3,1,0,2:T(2,128)(2,1)} async-done(((bf16[1,2,4096,1792]{3,1,0,2:T(2,128)(2,1)}), bf16[1,2,4096,1792]{3,1,0,2:T(2,128)(2,1)}, u32[]{:S(2)}, u32[]{:S(2)}) %all-to-all-start.1) | async-done | bytes 29360160 | tf_op jit(solution)/shard_map/all_to_all | solution.py:37
  831.2 60.1 %fusion.6 = f32[2,512,1792]{2,0,1:T(2,128)S(1)} fusion(bf16[1,2,8,512,1792]{4,1,3,2,0:T(2,128)(2,1)} %bitcast.11, f32[8]{0:T(128)S(1)} %get-tuple-element.4), kind=kLoop, calls=%fused_computation.11 | loop fusion | flops 42205184 | bytes 36700192 | tf_op jit(solution)/shard_map/reduce_sum | solution.py:44
  891.2 57.7 %fusion.12 = f32[8]{0:T(128)S(1)} fusion(bf16[1,2,8,512,1792]{4,1,3,2,0:T(2,128)(2,1)} %bitcast.11, f32[8]{0:T(128)S(1)} %get-tuple-element.5, f32[2,512,1792]{2,0,1:T(2,128)S(1)} %fusion.6), kind=kLoop, calls=%fused_computation.17 | loop fusion | flops 73400312 | bytes 36700224 | tf_op jit(solution)/shard_map/reduce_sum | solution.py:49
  949.0 38.1 %psum.21 = f32[8]{0:T(128)S(1)} all-reduce(f32[8]{0:T(128)S(1)} %fusion.12), channel_id=1, replica_groups=mesh['colony'=8,'fsdp'=4] {'colony','fsdp'}, use_global_device_ids=true, to_apply=%region_4.5 | all-reduce | flops 8 | bytes 64 | tf_op jit(solution)/shard_map/psum | solution.py:50
  987.0 0.6 fusion.23
  987.6 0.7 multiply_divide_fusion.2
  988.3 60.1 %fusion.7 = f32[2,512,1792]{2,0,1:T(2,128)S(1)} fusion(bf16[1,2,8,512,1792]{4,1,3,2,0:T(2,128)(2,1)} %bitcast.11, f32[8]{0:T(128)S(1)} %multiply_divide_fusion.2), kind=kLoop, calls=%fused_computation.12 | loop fusion | flops 42205184 | bytes 36700192 | tf_op jit(solution)/shard_map/reduce_sum | solution.py:44
  1048.4 57.7 %fusion.11 = f32[8]{0:T(128)S(1)} fusion(bf16[1,2,8,512,1792]{4,1,3,2,0:T(2,128)(2,1)} %bitcast.11, f32[8]{0:T(128)S(1)} %get-tuple-element.5, f32[2,512,1792]{2,0,1:T(2,128)S(1)} %fusion.7), kind=kLoop, calls=%fused_computation.16 | loop fusion | flops 73400312 | bytes 36700224 | tf_op jit(solution)/shard_map/reduce_sum | solution.py:49
  1106.1 41.7 %psum.22 = f32[8]{0:T(128)S(1)} all-reduce(f32[8]{0:T(128)S(1)} %fusion.11), channel_id=1, replica_groups=mesh['colony'=8,'fsdp'=4] {'colony','fsdp'}, use_global_device_ids=true, to_apply=%region_8.9 | all-reduce | flops 8 | bytes 64 | tf_op jit(solution)/shard_map/psum | solution.py:50
  1147.7 0.6 fusion.24
  1148.3 0.7 multiply_divide_fusion.1
  1149.0 60.1 %fusion.8 = f32[2,512,1792]{2,0,1:T(2,128)S(1)} fusion(bf16[1,2,8,512,1792]{4,1,3,2,0:T(2,128)(2,1)} %bitcast.11, f32[8]{0:T(128)S(1)} %multiply_divide_fusion.1), kind=kLoop, calls=%fused_computation.13 | loop fusion | flops 42205184 | bytes 36700192 | tf_op jit(solution)/shard_map/reduce_sum | solution.py:44
  1209.1 57.7 %fusion.10 = f32[8]{0:T(128)S(1)} fusion(bf16[1,2,8,512,1792]{4,1,3,2,0:T(2,128)(2,1)} %bitcast.11, f32[8]{0:T(128)S(1)} %get-tuple-element.5, f32[2,512,1792]{2,0,1:T(2,128)S(1)} %fusion.8), kind=kLoop, calls=%fused_computation.15 | loop fusion | flops 73400312 | bytes 36700224 | tf_op jit(solution)/shard_map/reduce_sum | solution.py:49
  1266.8 38.7 %psum.23 = f32[8]{0:T(128)S(1)} all-reduce(f32[8]{0:T(128)S(1)} %fusion.10), channel_id=1, replica_groups=mesh['colony'=8,'fsdp'=4] {'colony','fsdp'}, use_global_device_ids=true, to_apply=%region_12.13 | all-reduce | flops 8 | bytes 64 | tf_op jit(solution)/shard_map/psum | solution.py:50
  1305.5 0.6 fusion.25
  1306.1 0.7 multiply_divide_fusion
  1306.8 60.1 %fusion.9 = f32[2,512,1792]{2,0,1:T(2,128)S(1)} fusion(bf16[1,2,8,512,1792]{4,1,3,2,0:T(2,128)(2,1)} %bitcast.11, f32[8]{0:T(128)S(1)} %multiply_divide_fusion), kind=kLoop, calls=%fused_computation.14 | loop fusion | flops 42205184 | bytes 36700192 | tf_op jit(solution)/shard_map/reduce_sum | solution.py:44
  1366.9 5.8 fusion.26
  1372.7 3.5 copy_bitcast_fusion
  (3 shorter events, 0.0 us)
Async XLA Ops:
  7.2 58.9 %all-gather.2.cloned.1.call-start = ((), (), s32[]{:S(2)}) async-start(), calls=%async_computation.2 | async-start | bytes 5242880 | tf_op jit(solution)/shard_map/all_gather | solution.py:31
  66.1 15.8 %copy-start = (bf16[512,4096]{1,0:T(8,128)(2,1)S(1)}, bf16[512,4096]{1,0:T(8,128)(2,1)}, u32[]{:S(2)}) copy-start(bf16[512,4096]{1,0:T(8,128)(2,1)} %all-gather.2.cloned.1.call-done) | copy-start | bytes 12582916
  191.1 6.9 copy-start.1
  191.1 6.9 copy-start.2
  191.1 640.1 %all-to-all-start.1 = ((bf16[1,2,4096,1792]{3,1,0,2:T(2,128)(2,1)}), bf16[1,2,4096,1792]{3,1,0,2:T(2,128)(2,1)}, u32[]{:S(2)}, u32[]{:S(2)}) async-start(bf16[1,2,4096,1792]{3,1,0,2:T(2,128)(2,1)} %copy.15), calls=%async_computation.1 | async-start | bytes 58720256 | tf_op jit(solution)/shard_map/all_to_all | solution.py:37
Sparse Core Ops, SparseCore 0:
  11.4 54.6 all-gather.1
where the time goes:
time: 1400 us; the launch traced here: 1380 us
  waiting for transfers between devices  639 us (46%)
  other arithmetic  442 us (32%)
  blocking collectives  163 us (12%)
  local copies, waits for them, and re-layouts  66.3 us (5%)
  matrix products  51.2 us (4%)
  between operations  14.4 us (1%)
    all_to_all x1, waiting for transfers between devices, on_device(): lax.all_to_all(stacked, 'colony', split_axis=2, concat_axis=0, tiled=True)  633 us
    reduce_sum x4, other arithmetic, combine(): jnp.sum(coef[:, None, None, None] * pieces.astype(jnp.float32), axis=0)  240 us
    reduce_sum x3, other arithmetic, on_device(): partial_value = jnp.sum(diff * diff, axis=(1, 2, 3))  173 us
    psum x3, blocking collectives, on_device(): dist = jnp.sqrt(lax.psum(partial_value, ('colony', 'fsdp')) + 1e-06)  118 us
    broadcast_in_dim x1, local copies, waits for them, and re-layouts, on_device(): stacked = jnp.stack([grad_gate, grad_up])[None]  53.1 us
    all_to_all x1, blocking collectives, on_device(): lax.all_to_all(hidden_grad[0], 'fsdp', split_axis=1, concat_axis=0, tiled...  44.7 us
  transfers between devices with their start and end apart: 2, of which 2 were waited for; matrix products, arithmetic and copies ran while one was open for 0% of the time, Pallas kernels for 0%

commit v1 on v0

v1 whole, which is shorter than its diff:
```python
import functools

import jax
import jax.numpy as jnp
from jax import lax
from jax.experimental import pallas as pl
from jax.experimental.pallas import tpu as pltpu
from jax.sharding import PartitionSpec as P

NBYZ = 3
ITERS = 3
LINE = 4
AXES = ("colony", "fsdp")
MIB = 1024 * 1024


def ring_order(count):
    width = count // LINE
    if count % LINE or width % 2:
        return list(range(count))
    order = [(0, 0)]
    for y in range(width):
        column = list(range(1, LINE))
        order += [(z, y) for z in (column if y % 2 == 0 else column[::-1])]
    order += [(0, y) for y in range(width - 1, 0, -1)]
    return [z * width + y for z, y in order]


def slot_shifts(count):
    shifts = [0]
    for step in range(1, count // 2):
        shifts += [step, -step]
    return shifts + [count // 2]


def lane_sums(square):
    rows, lanes = square.shape
    total = square[:, :128]
    for at in range(128, lanes, 128):
        total = total + square[:, at : at + 128]
    return jnp.sum(total.reshape(rows // 8, 8, 128), axis=0)


def colony_kernel(slot, count, parts, share, n_cot, place_of, last, *refs):
    refs = list(refs)
    factor_ref = refs.pop(0)
    slots_ref = refs.pop(0)
    parts_refs = [refs.pop(0) for _ in parts]
    gate_ref, up_ref = refs.pop(0), refs.pop(0)
    cot_refs = [refs.pop(0) for _ in range(n_cot)]
    before = [refs.pop(0) for _ in range(slot)]
    earlier_ref = refs.pop(0) if last else None
    grad_ref = refs.pop(0)
    pair_ref = refs.pop(0) if slot else None
    tokens, rows_t, sems = refs[:3]
    acc = refs[3] if slot else None
    step = pl.program_id(0)
    steps = pl.num_programs(0)
    rows = rows_t.shape[0]

    @pl.when(step == 0)
    def _():
        copies = []
        for at, (ref, pieces) in enumerate(zip(parts_refs, parts)):
            for start, size, target in pieces:
                copies.append(
                    pltpu.make_async_copy(
                        ref.at[pl.ds(start, size)],
                        tokens.at[pl.ds(target, size)],
                        sems.at[len(copies)],
                    )
                )
        for copy in copies:
            copy.start()
        for copy in copies:
            copy.wait()
        first = pl.multiple_of(slots_ref[count] * rows, rows)
        rows_t[...] = tokens[:, pl.ds(first, rows)].T
        if slot:
            acc[...] = jnp.zeros_like(acc)

    gate = jnp.dot(tokens[...], gate_ref[...], preferred_element_type=jnp.float32)
    up = jnp.dot(tokens[...], up_ref[...], preferred_element_type=jnp.float32)
    sig = jax.nn.sigmoid(gate)
    cot = [ref[...] for ref in cot_refs]
    back = (cot[0] if n_cot == 1 else jnp.concatenate(cot, axis=0)).astype(jnp.float32)
    d_up = (back * gate * sig).astype(jnp.bfloat16)
    d_gate = (back * up * sig * (1.0 + gate * (1.0 - sig))).astype(jnp.bfloat16)
    turned = rows_t[...]
    grad_ref[0] = jnp.dot(turned, d_gate, preferred_element_type=jnp.float32).astype(jnp.bfloat16)
    grad_ref[1] = jnp.dot(turned, d_up, preferred_element_type=jnp.float32).astype(jnp.bfloat16)

    if slot:
        scales = [factor_ref[k] for k in range(slot + 1)]
        chunk = 32

        for matrix in range(2):

            def body(at, sums, matrix=matrix):
                span = pl.ds(pl.multiple_of(at * chunk, chunk), chunk)
                mine = scales[slot] * grad_ref[matrix, span, :].astype(jnp.float32)
                out = []
                for k in range(slot):
                    diff = mine - scales[k] * before[k][matrix, span, :].astype(jnp.float32)
                    out.append(sums[k] + lane_sums(diff * diff))
                return tuple(out)

            start = tuple(acc[k] for k in range(slot))
            done = lax.fori_loop(0, rows // chunk, body, start)
            for k in range(slot):
                acc[k] = done[k]

        @pl.when(step == steps - 1)
        def _():
            if not last:
                for k in range(slot):
                    pair_ref[k] = acc[k]
                return
            shape = pair_ref.shape
            row = lax.broadcasted_iota(jnp.int32, shape, 0)
            lane = lax.broadcasted_iota(jnp.int32, shape, 1)
            table = jnp.zeros(shape, jnp.float32)
            at = 0
            for one in range(1, count):
                for two in range(one):
                    part = acc[two] if one == slot else earlier_ref[at]
                    at += 1
                    a, b = slots_ref[one], slots_ref[two]
                    here = ((row == a) & (lane == b)) | ((row == b) & (lane == a))
                    table = table + jnp.where(here, jnp.sum(part), 0.0)
            pair_ref[...] = table


def combine_kernel(count, table_ref, factor_ref, slots_ref, *refs):
    grads = refs[:count]
    gate_out, up_out = refs[count : count + 2]
    coef = refs[count + 2]

    @pl.when(pl.program_id(0) == 0)
    def _():
        table = table_ref[...]
        shape = table.shape
        in_row = lax.broadcasted_iota(jnp.int32, (1, shape[1]), 1) < count
        in_column = lax.broadcasted_iota(jnp.int32, (shape[0], 1), 0) < count
        share_row = jnp.where(in_row, 1.0 / count, 0.0)
        share_column = jnp.where(in_column, 1.0 / count, 0.0)
        for _ in range(ITERS):
            by_row = table * share_row
            near_column = jnp.sum(by_row, axis=1, keepdims=True)
            near_row = jnp.sum(table * share_column, axis=0, keepdims=True)
            half = 0.5 * jnp.sum(near_column * share_column)
            dist_row = jnp.sqrt(jnp.maximum(near_row - half, 0.0) + 1e-06)
            dist_column = jnp.sqrt(jnp.maximum(near_column - half, 0.0) + 1e-06)
            weight_row = jnp.where(in_row, 1.0 / dist_row, 0.0)
            weight_column = jnp.where(in_column, 1.0 / dist_column, 0.0)
            share_row = weight_row / jnp.sum(weight_row)
            share_column = weight_column / jnp.sum(weight_column)
        lane = lax.broadcasted_iota(jnp.int32, (1, shape[1]), 1)
        for k in range(count):
            coef[k] = jnp.sum(jnp.where(lane == slots_ref[k], share_row, 0.0)) * factor_ref[k]

    scales = [coef[k] for k in range(count)]
    rows = gate_out.shape[0]
    chunk = 16
    for matrix, out in ((0, gate_out), (1, up_out)):

        def body(at, carry, matrix=matrix, out=out):
            span = pl.ds(pl.multiple_of(at * chunk, chunk), chunk)
            total = scales[0] * grads[0][matrix, span, :].astype(jnp.float32)
            for k in range(1, count):
                total = total + scales[k] * grads[k][matrix, span, :].astype(jnp.float32)
            out[span, :] = total
            return carry

        lax.fori_loop(0, rows // chunk, body, 0)


def on_device(order, hidden_states, norm_gain, gate_weight, up_weight, hidden_grad, byz_order, byz_scale):
    count, shards = len(order), lax.axis_size("fsdp")
    colony, shard = lax.axis_index("colony"), lax.axis_index("fsdp")
    width = gate_weight.shape[1]
    depth = hidden_states.shape[2]
    share = hidden_states.shape[1]
    half = share // 2
    rows = depth // count
    total_tokens = share * shards
    block = 256 if width % 256 == 0 else 128
    place = {c: at for at, c in enumerate(order)}
    shifts = slot_shifts(count)

    def hop(value, delta):
        pairs = []
        for c in range(count):
            to = order[(place[c] + delta) % count]
            pairs.append((c, to))
        return lax.ppermute(value, "colony", pairs)

    def swap(value, mask):
        return lax.ppermute(value, "fsdp", [(j, j ^ mask) for j in range(shards)])

    def spread(own):
        pieces = {0: own}
        bit = shards // 2
        while bit:
            for m in list(pieces):
                pieces[m | bit] = swap(pieces[m], bit)
            bit //= 2
        return [pieces[m] for m in range(shards)]

    values = hidden_states[0].astype(jnp.float32)
    meansq = jnp.mean(values * values, axis=-1, keepdims=True)
    normed = (values * lax.rsqrt(meansq + 1e-05) * norm_gain).astype(jnp.bfloat16)

    local_grad = hidden_grad[0]
    cuts = []
    for m in range(shards):
        columns = lax.dynamic_slice(local_grad, (0, (shard ^ m) * width), (share, width))
        cuts.append(columns if m == 0 else swap(columns, m))
    cot = jnp.concatenate([c[h * half : (h + 1) * half] for h in range(2) for c in cuts], axis=0)
    mid = total_tokens // 2

    tokens, cots = [None] * count, [None] * count
    tokens[0], cots[0] = spread(normed), [cot]
    ahead = {1: (normed, cot), -1: (normed, cot)}
    slot = 1
    for step in range(1, count // 2):
        for way in (1, -1):
            n, c = ahead[way]
            n, c = hop(n, way), hop(c, way)
            ahead[way] = (n, c)
            tokens[slot], cots[slot] = spread(n), [c]
            slot += 1
    halves = []
    last_cots = []
    for h, way in ((0, 1), (1, -1)):
        n, c = ahead[way]
        halves.append(spread(hop(n[h * half : (h + 1) * half], way)))
        last_cots.append(hop(c[h * mid : (h + 1) * mid], way))
    tokens[slot], cots[slot] = halves[0] + halves[1], last_cots

    ring = jnp.asarray(order, jnp.int32)
    at = jnp.asarray([place[c] for c in range(count)], jnp.int32)[colony]
    held = ring[(at - jnp.asarray(shifts, jnp.int32)) % count]
    slots = jnp.concatenate([held, colony[None].astype(jnp.int32)])
    hits = byz_order[:NBYZ][:, None] == held[None, :]
    factor = 1.0 + jnp.sum(jnp.where(hits, -byz_scale[:, None] - 1.0, jnp.float32(0.0)), axis=0)

    smem = pl.BlockSpec(memory_space=pltpu.SMEM)
    anywhere = pl.BlockSpec(memory_space=pl.ANY)
    table_shape = (max(8, count), 128)
    grads, pairs = [], []
    for k in range(count):
        last = k == count - 1
        if last:
            parts = [[(0, half, (h * shards + m) * half)] for h in range(2) for m in range(shards)]
        else:
            parts = [
                [(h * half, half, (h * shards + m) * half) for h in range(2)] for m in range(shards)
            ]
        column = pl.BlockSpec((depth, block), lambda b: (0, b))
        block_of_grad = pl.BlockSpec((2, rows, block), lambda b: (0, 0, b))
        in_specs = [smem, smem] + [anywhere] * len(parts) + [column, column]
        in_specs += [pl.BlockSpec((c.shape[0], block), lambda b: (0, b)) for c in cots[k]]
        in_specs += [block_of_grad] * k
        operands = [factor, slots, *tokens[k], gate_weight, up_weight, *cots[k], *grads]
        out_shape = [jax.ShapeDtypeStruct((2, rows, width), jnp.bfloat16)]
        out_specs = [block_of_grad]
        scratch = [
            pltpu.VMEM((total_tokens, depth), jnp.bfloat16),
            pltpu.VMEM((rows, total_tokens), jnp.bfloat16),
            pltpu.SemaphoreType.DMA((2 * shards,)),
        ]
        if last:
            earlier = jnp.concatenate(pairs, axis=0)
            operands.append(earlier)
            in_specs.append(pl.BlockSpec(earlier.shape, lambda b: (0, 0, 0)))
            out_shape.append(jax.ShapeDtypeStruct(table_shape, jnp.float32))
            out_specs.append(pl.BlockSpec(table_shape, lambda b: (0, 0)))
        elif k:
            out_shape.append(jax.ShapeDtypeStruct((k, 8, 128), jnp.float32))
            out_specs.append(pl.BlockSpec((k, 8, 128), lambda b: (0, 0, 0)))
        if k:
            scratch.append(pltpu.VMEM((k, 8, 128), jnp.float32))
        flops = 2 * total_tokens * width * 2 * (depth + rows)
        out = pl.pallas_call(
            functools.partial(colony_kernel, k, count, parts, share, len(cots[k]), place, last),
            grid=(width // block,),
            in_specs=in_specs,
            out_specs=out_specs,
            out_shape=out_shape,
            scratch_shapes=scratch,
            compiler_params=pltpu.CompilerParams(vmem_limit_bytes=40 * MIB),
            cost_estimate=pl.CostEstimate(
                flops=flops, bytes_accessed=4 * depth * width, transcendentals=total_tokens * width
            ),
        )(*operands)
        grads.append(out[0])
        if k:
            pairs.append(out[1])

    table = pairs[-1]
    devices = count * shards
    bit = 1
    while bit < devices:
        table = table + lax.ppermute(table, AXES, [(d, d ^ bit) for d in range(devices)])
        bit *= 2

    out_block = pl.BlockSpec((rows, block), lambda b: (0, b))
    return pl.pallas_call(
        functools.partial(combine_kernel, count),
        grid=(width // block,),
        in_specs=[pl.BlockSpec(table_shape, lambda b: (0, 0)), smem, smem]
        + [pl.BlockSpec((2, rows, block), lambda b: (0, 0, b))] * count,
        out_specs=[out_block, out_block],
        out_shape=[jax.ShapeDtypeStruct((rows, width), jnp.float32)] * 2,
        scratch_shapes=[pltpu.SMEM((count,), jnp.float32)],
        compiler_params=pltpu.CompilerParams(vmem_limit_bytes=40 * MIB),
    )(table, factor, slots, *grads)


def solution(mesh):
    placed = (
        P("colony", "fsdp", None),
        P(),
        P(None, "fsdp"),
        P(None, "fsdp"),
        P("colony", "fsdp", None),
        P(),
        P(),
    )
    return jax.shard_map(
        functools.partial(on_device, ring_order(mesh.shape["colony"])),
        mesh=mesh,
        in_specs=placed,
        out_specs=(P("colony", "fsdp"), P("colony", "fsdp")),
        check_vma=False,
    )
```

time: 1400 us -> 457 us (0.33); the launches traced: 1380 us -> 457 us
  waiting for transfers between devices: 639 us -> 119 us
  other arithmetic: 442 us -> 1.43 us
  Pallas kernels: 0 us -> 264 us
  blocking collectives: 163 us -> 0 us
  matrix products: 51.2 us -> 0 us
  local copies, waits for them, and re-layouts: 66.3 us -> 29.6 us
  starting transfers between devices: 6.93 us -> 41.9 us
    all_to_all x1 -> x0, waiting for transfers between devices: 633 us -> none  [on_device(): lax.all_to_all(stacked, 'colony', split_axis=2, concat_axis=0, tiled=True)]
    reduce_sum x10 -> x0, other arithmetic: 415 us -> none  [the longest x4 240 us: combine(): jnp.sum(coef[:, None, None, None] * pieces.astype(jnp.float32), axis=0)]
    pallas_call x0 -> x9, Pallas kernels: none -> 264 us  [the longest x8 248 us: on_device(): pl.pallas_call(functools.partial(colony_kernel, k, count, parts, share, l...]
    ppermute x0 -> x51, waiting for transfers between devices: none -> 119 us  [the longest x30 78.8 us: swap(): return lax.ppermute(value, 'fsdp', [(j, j ^ mask) for j in range(shards)])]
    psum x3 -> x0, blocking collectives: 118 us -> none  [on_device(): dist = jnp.sqrt(lax.psum(partial_value, ('colony', 'fsdp')) + 1e-06)]
    broadcast_in_dim x1 -> x0, local copies, waits for them, and re-layouts: 53.1 us -> none  [on_device(): stacked = jnp.stack([grad_gate, grad_up])[None]]
    dot_general x4 -> x0, matrix products: 51.2 us -> none  [the longest x2 22.5 us: token_contract(): lax.dot_general(normed_all, delta, dims, preferred_element_type=jnp.float32)]
    all_to_all x1 -> x0, blocking collectives: 44.7 us -> none  [on_device(): lax.all_to_all(hidden_grad[0], 'fsdp', split_axis=1, concat_axis=0, tiled...]
  transfers between devices with their start and end apart: 2 -> 51, of which waited for: 2 -> 13; matrix products, arithmetic and copies ran while one was open for 0% -> 1% of each run, Pallas kernels for 0% -> 46%
where the time goes in v1:
time: 457 us
  Pallas kernels  264 us (58%)
  waiting for transfers between devices  119 us (26%)
  starting transfers between devices  41.9 us (9%)
  local copies, waits for them, and re-layouts  29.6 us (6%)
    pallas_call x8, Pallas kernels, on_device(): pl.pallas_call(functools.partial(colony_kernel, k, count, parts, share, l...  248 us
    ppermute x30, waiting for transfers between devices, swap(): return lax.ppermute(value, 'fsdp', [(j, j ^ mask) for j in range(shards)])  78.8 us
    ppermute x16, waiting for transfers between devices, hop(): return lax.ppermute(value, 'colony', pairs)  30.8 us
    unnamed x76, local copies, waits for them, and re-layouts  24.7 us
    ppermute x16, starting transfers between devices, hop(): return lax.ppermute(value, 'colony', pairs)  18.9 us
    ppermute x30, starting transfers between devices, swap(): return lax.ppermute(value, 'fsdp', [(j, j ^ mask) for j in range(shards)])  15.7 us
    pallas_call x1, Pallas kernels, on_device(): pl.pallas_call(functools.partial(combine_kernel, count), grid=(width // b...  15.2 us
    ppermute x5, waiting for transfers between devices, on_device(): lax.ppermute(table, AXES, [(d, d ^ bit) for d in range(devices)])  9.21 us
  transfers between devices with their start and end apart: 51, of which 13 were waited for; matrix products, arithmetic and copies ran while one was open for 1% of the time, Pallas kernels for 46%

profile of v1, /device:TPU:0, one launch (start us, length us, event | category | flops | bytes accessed | tf_op | source)
XLA Modules:
  0.0 456.6 jit_solution(1222743586713018321)
XLA Ops:
  0.7 2.5 dynamic-slice_bitcast_fusion
  4.2 2.6 collective-permute-start.26
  7.0 1.6 collective-permute-start
  9.1 1.0 fusion.4
  10.5 29.9 %collective-permute-done.15 = bf16[128,1792]{1,0:T(8,128)(2,1)S(1)} collective-permute-done((bf16[128,1792]{1,0:T(8,128)(2,1)}, bf16[128,1792]{1,0:T(8,128)(2,1)S(1)}, u32[]{:S(2)}, u32[]{:S(2)}) %collective-permute-start.15) | collective-permute-done | bytes 458784 | tf_op jit(solution)/shard_map/ppermute | solution.py:199
  40.5 1.1 collective-permute-start.16
  41.6 11.6 %collective-permute-done.16 = bf16[128,1792]{1,0:T(8,128)(2,1)S(1)} collective-permute-done((bf16[128,1792]{1,0:T(8,128)(2,1)}, bf16[128,1792]{1,0:T(8,128)(2,1)S(1)}, u32[]{:S(2)}, u32[]{:S(2)}) %collective-permute-start.16) | collective-permute-done | bytes 458784 | tf_op jit(solution)/shard_map/ppermute | solution.py:199
  53.2 1.0 fusion.3
  54.2 2.0 collective-permute-start.29
  56.8 1.6 collective-permute-start.17
  59.0 1.6 collective-permute-done.27.refs_5_
  60.6 1.0 copy-done.13
  61.7 18.9 %collective-permute-done.29.refs_4_ = bf16[128,4096]{1,0:T(8,128)(2,1)} collective-permute-done((bf16[128,4096]{1,0:T(8,128)(2,1)}, bf16[128,4096]{1,0:T(8,128)(2,1)}, u32[]{:S(2)}, u32[]{:S(2)}) %collective-permute-start.29) | collective-permute-done | bytes 1048608 | tf_op jit(solution)/shard_map/ppermute | solution.py:199
  80.6 2.1 collective-permute-start.1
  82.7 1.0 copy-done.9
  85.7 16.7 %collective-permute-done.32.refs_4_ = bf16[128,4096]{1,0:T(8,128)(2,1)} collective-permute-done((bf16[128,4096]{1,0:T(8,128)(2,1)}, bf16[128,4096]{1,0:T(8,128)(2,1)}, u32[]{:S(2)}, u32[]{:S(2)}) %collective-permute-start.32) | collective-permute-done | bytes 1048608 | tf_op jit(solution)/shard_map/ppermute | solution.py:199
  102.4 1.9 collective-permute-start.21
  104.5 16.9 %collective-permute-done.1.refs_2_ = bf16[128,4096]{1,0:T(8,128)(2,1)} collective-permute-done((bf16[128,4096]{1,0:T(8,128)(2,1)}, bf16[128,4096]{1,0:T(8,128)(2,1)}, u32[]{:S(2)}, u32[]{:S(2)}) %collective-permute-start.1) | collective-permute-done | bytes 1048608 | tf_op jit(solution)/shard_map/ppermute | solution.py:196
  121.7 1.7 collective-permute-start.9
  123.5 1.2 copy-done.14
  124.7 24.2 %shard_map.113.refs_9_.refs_14_.refs_0_ = bf16[2,512,1792]{2,1,0:T(8,128)(2,1)S(1)} custom-call(f32[8]{0:T(128)S(1)} %broadcast_add_fusion.refs_0_.factor_ref, s32[9]{0:T(128)S(1)} %pad_add_fusion.refs_1_.slots_ref, bf16[128,4096]{1,0:T(8,128)(2,1)S(1)} %fusion.2.refs_2_, bf16[128,4096]{1,0:T(8,128)(2,1)} %collective-permute-done.25.refs_3_, ...), custom_call_target="tpu_custom_call" | custom-call | flops 16911433728 | bytes 29360128 | tf_op jit(solution)/shard_map/pallas_call | solution.py:285
  149.1 1.0 copy-done.17
  150.0 1.4 collective-permute-start.38
  151.4 1.0 copy-done.15
  152.4 1.3 collective-permute-start.2
  153.7 1.6 collective-permute-start.18
  155.2 13.7 %collective-permute-done.9.refs_2_ = bf16[128,4096]{1,0:T(8,128)(2,1)S(1)} collective-permute-done((bf16[128,4096]{1,0:T(8,128)(2,1)}, bf16[128,4096]{1,0:T(8,128)(2,1)S(1)}, u32[]{:S(2)}, u32[]{:S(2)}) %collective-permute-start.9) | collective-permute-done | bytes 1048608 | tf_op jit(solution)/shard_map/ppermute | solution.py:196
  169.2 1.2 copy-done.18
  170.4 27.6 %shard_map.114 = (bf16[2,512,1792]{2,1,0:T(8,128)(2,1)S(1)}, f32[1,8,128]{2,1,0:T(8,128)S(1)}) custom-call(f32[8]{0:T(128)S(1)} %broadcast_add_fusion.refs_0_.factor_ref, s32[9]{0:T(128)S(1)} %pad_add_fusion.refs_1_.slots_ref, bf16[128,4096]{1,0:T(8,128)(2,1)} %collective-permute-done.refs_2_, bf16[128,4096]{1,0:T(8,128)(2,1)S(1)} %copy-done.10, ...), custom_call_target="tpu_custom_call" | custom-call | flops 16911433728 | bytes 29360128 | tf_op jit(solution)/shard_map/pallas_call | solution.py:285
  198.1 1.8 copy-done
  200.1 1.7 collective-permute-start.10
  202.0 1.2 copy-done.16
  203.2 29.4 %shard_map.115 = (bf16[2,512,1792]{2,1,0:T(8,128)(2,1)S(1)}, f32[2,8,128]{2,1,0:T(8,128)S(1)}) custom-call(f32[8]{0:T(128)S(1)} %broadcast_add_fusion.refs_0_.factor_ref, s32[9]{0:T(128)S(1)} %pad_add_fusion.refs_1_.slots_ref, bf16[128,4096]{1,0:T(8,128)(2,1)} %collective-permute-done.7.refs_2_, bf16[128,4096]{1,0:T(8,128)(2,1)} %collective-permute-done.31.refs_3_, ...), custom_call_target="tpu_custom_call" | custom-call | flops 16911433728 | bytes 29360128 | tf_op jit(solution)/shard_map/pallas_call | solution.py:285
  232.6 1.8 copy-done.2
  235.0 1.3 collective-permute-start.41
  236.3 1.6 collective-permute-start.19
  238.4 31.0 %shard_map.116 = (bf16[2,512,1792]{2,1,0:T(8,128)(2,1)S(1)}, f32[3,8,128]{2,1,0:T(8,128)S(1)}) custom-call(f32[8]{0:T(128)S(1)} %broadcast_add_fusion.refs_0_.factor_ref, s32[9]{0:T(128)S(1)} %pad_add_fusion.refs_1_.slots_ref, bf16[128,4096]{1,0:T(8,128)(2,1)} %collective-permute-done.1.refs_2_, bf16[128,4096]{1,0:T(8,128)(2,1)} %collective-permute-done.34.refs_3_, ...), custom_call_target="tpu_custom_call" | custom-call | flops 16911433728 | bytes 29360128 | tf_op jit(solution)/shard_map/pallas_call | solution.py:285
  269.4 1.8 copy-done.4
  271.3 1.0 copy-done.19
  272.3 0.7 collective-permute-start.44
  273.2 1.2 copy-done.20
  274.4 32.5 %shard_map.117 = (bf16[2,512,1792]{2,1,0:T(8,128)(2,1)S(1)}, f32[4,8,128]{2,1,0:T(8,128)S(1)}) custom-call(f32[8]{0:T(128)S(1)} %broadcast_add_fusion.refs_0_.factor_ref, s32[9]{0:T(128)S(1)} %pad_add_fusion.refs_1_.slots_ref, bf16[128,4096]{1,0:T(8,128)(2,1)} %collective-permute-done.8.refs_2_, bf16[128,4096]{1,0:T(8,128)(2,1)} %collective-permute-done.37.refs_3_, ...), custom_call_target="tpu_custom_call" | custom-call | flops 16911433728 | bytes 29360128 | tf_op jit(solution)/shard_map/pallas_call | solution.py:285
  306.9 1.8 copy-done.5
  309.1 1.3 collective-permute-start.12
  310.4 0.8 collective-permute-start.5
  311.3 34.0 %shard_map.118 = (bf16[2,512,1792]{2,1,0:T(8,128)(2,1)S(1)}, f32[5,8,128]{2,1,0:T(8,128)S(1)}) custom-call(f32[8]{0:T(128)S(1)} %broadcast_add_fusion.refs_0_.factor_ref, s32[9]{0:T(128)S(1)} %pad_add_fusion.refs_1_.slots_ref, bf16[128,4096]{1,0:T(8,128)(2,1)S(1)} %collective-permute-done.2.refs_2_, bf16[128,4096]{1,0:T(8,128)(2,1)} %collective-permute-done.40.refs_3_, ...), custom_call_target="tpu_custom_call" | custom-call | flops 16911433728 | bytes 29360128 | tf_op jit(solution)/shard_map/pallas_call | solution.py:285
  345.4 1.1 slice.70
  347.2 0.8 copy-done.23
  348.3 1.7 collective-permute-start.20
  350.4 32.9 %shard_map.119 = (bf16[2,512,1792]{2,1,0:T(8,128)(2,1)S(1)}, f32[6,8,128]{2,1,0:T(8,128)S(1)}) custom-call(f32[8]{0:T(128)S(1)} %broadcast_add_fusion.refs_0_.factor_ref, s32[9]{0:T(128)S(1)} %pad_add_fusion.refs_1_.slots_ref, bf16[128,4096]{1,0:T(8,128)(2,1)S(1)} %collective-permute-done.9.refs_2_, bf16[128,4096]{1,0:T(8,128)(2,1)S(1)} %collective-permute-done.43.refs_3_, ...), custom_call_target="tpu_custom_call" | custom-call | flops 16911433728 | bytes 29360128 | tf_op jit(solution)/shard_map/pallas_call | solution.py:285
  383.3 1.8 copy-done.7
  385.1 1.0 copy-done.22
  386.2 36.8 %shard_map.120 = (bf16[2,512,1792]{2,1,0:T(8,128)(2,1)S(1)}, f32[8,128]{1,0:T(8,128)S(1)}) custom-call(f32[8]{0:T(128)S(1)} %broadcast_add_fusion.refs_0_.factor_ref, s32[9]{0:T(128)S(1)} %pad_add_fusion.refs_1_.slots_ref, bf16[64,4096]{1,0:T(8,128)(2,1)S(1)} %collective-permute-done.3.refs_2_, bf16[64,4096]{1,0:T(8,128)(2,1)S(1)} %collective-permute-done.4.refs_3_, ...), custom_call_target="tpu_custom_call" | custom-call | flops 16911433728 | bytes 29360128 | tf_op jit(solution)/shard_map/pallas_call | solution.py:285
  423.0 1.8 copy-done.8
  424.9 1.2 collective-permute-done.46
  426.0 1.3 collective-permute-start.47
  427.4 2.3 collective-permute-done.47
  429.6 1.6 collective-permute-start.48
  431.3 2.0 collective-permute-done.48
  433.3 1.7 collective-permute-start.49
  434.9 1.9 collective-permute-done.49
  436.9 2.7 collective-permute-start.50
  439.5 1.8 collective-permute-done.50
  441.4 15.2 %shard_map.121 = (f32[512,1792]{1,0:T(8,128)}, f32[512,1792]{1,0:T(8,128)}) custom-call(f32[8,128]{1,0:T(8,128)S(1)} %add.69.table_ref, f32[8]{0:T(128)S(1)} %broadcast_add_fusion.refs_0_.factor_ref, s32[9]{0:T(128)S(1)} %pad_add_fusion.refs_1_.slots_ref, bf16[2,512,1792]{2,1,0:T(8,128)(2,1)S(1)} %shard_map.113.refs_9_.refs_14_.refs_0_, ...), custom_call_target="tpu_custom_call" | custom-call | tf_op jit(solution)/shard_map/pallas_call | solution.py:309
  (146 shorter events, 9.9 us)
Async XLA Ops:
  3.2 6.9 %collective-permute-start.14 = (bf16[128,1792]{1,0:T(8,128)(2,1)}, bf16[128,1792]{1,0:T(8,128)(2,1)S(1)}, u32[]{:S(2)}, u32[]{:S(2)}) collective-permute-start(bf16[128,1792]{1,0:T(8,128)(2,1)} %get-tuple-element.31), channel_id=1, source_target_pairs={{0,1},{1,0},{2,3},{3,2},{4,5},{5,4},{6,7},{7,6},{8,9},{9,8},{10,11... | collective-permute-start | bytes 1376264 | tf_op jit(solution)/shard_map/ppermute | solution.py:199
  4.2 52.0 %collective-permute-start.26 = (bf16[128,4096]{1,0:T(8,128)(2,1)S(1)}, bf16[128,4096]{1,0:T(8,128)(2,1)}, u32[]{:S(2)}, u32[]{:S(2)}) collective-permute-start(bf16[128,4096]{1,0:T(8,128)(2,1)S(1)} %fusion.2.refs_2_), channel_id=1, source_target_pairs={{0,2},{1,3},{2,0},{3,1},{4,6},{5,7},{6,4},{7,5},{8,10},{9,11},{10,... | collective-permute-start | bytes 3145736 | tf_op jit(solution)/shard_map/ppermute | solution.py:199
  6.8 50.0 %collective-permute-start.25 = (bf16[128,4096]{1,0:T(8,128)(2,1)S(1)}, bf16[128,4096]{1,0:T(8,128)(2,1)}, u32[]{:S(2)}, u32[]{:S(2)}) collective-permute-start(bf16[128,4096]{1,0:T(8,128)(2,1)S(1)} %fusion.2.refs_2_), channel_id=1, source_target_pairs={{0,1},{1,0},{2,3},{3,2},{4,5},{5,4},{6,7},{7,6},{8,9},{9,8},{10,11... | collective-permute-start | bytes 3145736 | tf_op jit(solution)/shard_map/ppermute | solution.py:199
  7.0 47.2 %collective-permute-start = (bf16[128,4096]{1,0:T(8,128)(2,1)S(1)}, bf16[128,4096]{1,0:T(8,128)(2,1)}, u32[]{:S(2)}, u32[]{:S(2)}) collective-permute-start(bf16[128,4096]{1,0:T(8,128)(2,1)S(1)} %fusion.2.refs_2_), channel_id=1, source_target_pairs={{0,8},{4,0},{8,16},{12,4},{16,24},{20,12},{24,28},{28,20},{1,9},{5... | collective-permute-start | bytes 3145736 | tf_op jit(solution)/shard_map/ppermute | solution.py:196
  8.6 49.8 %collective-permute-start.7 = (bf16[128,4096]{1,0:T(8,128)(2,1)S(1)}, bf16[128,4096]{1,0:T(8,128)(2,1)}, u32[]{:S(2)}, u32[]{:S(2)}) collective-permute-start(bf16[128,4096]{1,0:T(8,128)(2,1)S(1)} %fusion.2.refs_2_), channel_id=1, source_target_pairs={{0,4},{4,12},{8,0},{12,20},{16,8},{20,28},{24,16},{28,24},{1,5},{5... | collective-permute-start | bytes 3145736 | tf_op jit(solution)/shard_map/ppermute | solution.py:196
  9.1 74.6 %copy-start.31 = (s32[8]{0:T(128)S(1)}, s32[8]{0:T(128)}, u32[]{:S(2)}) copy-start(s32[8]{0:T(128)} %constant.60.clone) | copy-start | bytes 100
  9.1 75.2 %copy-start.30 = (s32[8]{0:T(128)S(1)}, s32[8]{0:T(128)}, u32[]{:S(2)}) copy-start(s32[8]{0:T(128)} %constant.64) | copy-start | bytes 100
  9.1 75.9 %copy-start.25 = (s32[8]{0:T(128)S(1)}, s32[8]{0:T(128)}, u32[]{:S(2)}) copy-start(s32[8]{0:T(128)} %constant.59.clone) | copy-start | bytes 100
  10.1 75.5 %copy-start.29 = (f32[3]{0:T(128)S(1)}, f32[3]{0:T(128)}, u32[]{:S(2)}) copy-start(f32[3]{0:T(128)} %param.16) | copy-start | bytes 40
  10.1 75.5 %copy-start.28 = (s32[8]{0:T(128)S(1)}, s32[8]{0:T(128)}, u32[]{:S(2)}) copy-start(s32[8]{0:T(128)} %param.15) | copy-start | bytes 100
  10.1 30.4 %collective-permute-start.15 = (bf16[128,1792]{1,0:T(8,128)(2,1)}, bf16[128,1792]{1,0:T(8,128)(2,1)S(1)}, u32[]{:S(2)}, u32[]{:S(2)}) collective-permute-start(bf16[128,1792]{1,0:T(8,128)(2,1)} %get-tuple-element.32), channel_id=1, source_target_pairs={{0,2},{1,3},{2,0},{3,1},{4,6},{5,7},{6,4},{7,5},{8,10},{9,11},{10,... | collective-permute-start | bytes 1376264 | tf_op jit(solution)/shard_map/ppermute | solution.py:199
  40.5 12.7 %collective-permute-start.16 = (bf16[128,1792]{1,0:T(8,128)(2,1)}, bf16[128,1792]{1,0:T(8,128)(2,1)S(1)}, u32[]{:S(2)}, u32[]{:S(2)}) collective-permute-start(bf16[128,1792]{1,0:T(8,128)(2,1)} %get-tuple-element.30), channel_id=1, source_target_pairs={{0,3},{1,2},{2,1},{3,0},{4,7},{5,6},{6,5},{7,4},{8,11},{9,10},{10,... | collective-permute-start | bytes 1376264 | tf_op jit(solution)/shard_map/ppermute | solution.py:199
  54.2 26.4 %collective-permute-start.29 = (bf16[128,4096]{1,0:T(8,128)(2,1)}, bf16[128,4096]{1,0:T(8,128)(2,1)}, u32[]{:S(2)}, u32[]{:S(2)}) collective-permute-start(bf16[128,4096]{1,0:T(8,128)(2,1)} %collective-permute-done.refs_2_), channel_id=1, source_target_pairs={{0,2},{1,3},{2,0},{3,1},{4,6},{5,7},{6,4},{7,5},{8,10},{9,11},{10,... | collective-permute-start | bytes 3145736 | tf_op jit(solution)/shard_map/ppermute | solution.py:199
  56.3 26.5 %collective-permute-start.28 = (bf16[128,4096]{1,0:T(8,128)(2,1)}, bf16[128,4096]{1,0:T(8,128)(2,1)S(1)}, u32[]{:S(2)}, u32[]{:S(2)}) collective-permute-start(bf16[128,4096]{1,0:T(8,128)(2,1)} %collective-permute-done.refs_2_), channel_id=1, source_target_pairs={{0,1},{1,0},{2,3},{3,2},{4,5},{5,4},{6,7},{7,6},{8,9},{9,8},{10,11... | collective-permute-start | bytes 3145736 | tf_op jit(solution)/shard_map/ppermute | solution.py:199
  56.3 4.4 collective-permute-start.27
  56.8 64.9 %collective-permute-start.17 = (bf16[512,1792]{1,0:T(8,128)(2,1)S(1)}, bf16[512,1792]{1,0:T(8,128)(2,1)}, u32[]{:S(2)}, u32[]{:S(2)}) collective-permute-start(bf16[512,1792]{1,0:T(8,128)(2,1)S(1)} %slice_dynamic-update-slice_fusion.refs_8_), channel_id=1, source_target_pairs={{0,8},{4,0},{8,16},{12,4},{16,24},{20,12},{24,28},{28,20},{1,9},{5... | collective-permute-start | bytes 5505032 | tf_op jit(solution)/shard_map/ppermute | solution.py:196
  58.4 44.0 %collective-permute-start.32 = (bf16[128,4096]{1,0:T(8,128)(2,1)}, bf16[128,4096]{1,0:T(8,128)(2,1)}, u32[]{:S(2)}, u32[]{:S(2)}) collective-permute-start(bf16[128,4096]{1,0:T(8,128)(2,1)} %collective-permute-done.7.refs_2_), channel_id=1, source_target_pairs={{0,2},{1,3},{2,0},{3,1},{4,6},{5,7},{6,4},{7,5},{8,10},{9,11},{10,... | collective-permute-start | bytes 3145736 | tf_op jit(solution)/shard_map/ppermute | solution.py:199
  61.6 42.8 %collective-permute-start.31 = (bf16[128,4096]{1,0:T(8,128)(2,1)}, bf16[128,4096]{1,0:T(8,128)(2,1)}, u32[]{:S(2)}, u32[]{:S(2)}) collective-permute-start(bf16[128,4096]{1,0:T(8,128)(2,1)} %collective-permute-done.7.refs_2_), channel_id=1, source_target_pairs={{0,1},{1,0},{2,3},{3,2},{4,5},{5,4},{6,7},{7,6},{8,9},{9,8},{10,11... | collective-permute-start | bytes 3145736 | tf_op jit(solution)/shard_map/ppermute | solution.py:199
  80.6 40.7 %collective-permute-start.1 = (bf16[128,4096]{1,0:T(8,128)(2,1)}, bf16[128,4096]{1,0:T(8,128)(2,1)}, u32[]{:S(2)}, u32[]{:S(2)}) collective-permute-start(bf16[128,4096]{1,0:T(8,128)(2,1)} %collective-permute-done.refs_2_), channel_id=1, source_target_pairs={{0,8},{4,0},{8,16},{12,4},{16,24},{20,12},{24,28},{28,20},{1,9},{5... | collective-permute-start | bytes 3145736 | tf_op jit(solution)/shard_map/ppermute | solution.py:196
  83.7 37.7 %collective-permute-start.8 = (bf16[128,4096]{1,0:T(8,128)(2,1)}, bf16[128,4096]{1,0:T(8,128)(2,1)}, u32[]{:S(2)}, u32[]{:S(2)}) collective-permute-start(bf16[128,4096]{1,0:T(8,128)(2,1)} %collective-permute-done.7.refs_2_), channel_id=1, source_target_pairs={{0,4},{4,12},{8,0},{12,20},{16,8},{20,28},{24,16},{28,24},{1,5},{5... | collective-permute-start | bytes 3145736 | tf_op jit(solution)/shard_map/ppermute | solution.py:196
  102.4 46.7 %collective-permute-start.21 = (bf16[512,1792]{1,0:T(8,128)(2,1)S(1)}, bf16[512,1792]{1,0:T(8,128)(2,1)S(1)}, u32[]{:S(2)}, u32[]{:S(2)}) collective-permute-start(bf16[512,1792]{1,0:T(8,128)(2,1)S(1)} %slice_dynamic-update-slice_fusion.refs_8_), channel_id=1, source_target_pairs={{0,4},{4,12},{8,0},{12,20},{16,8},{20,28},{24,16},{28,24},{1,5},{5... | collective-permute-start | bytes 5505032 | tf_op jit(solution)/shard_map/ppermute | solution.py:196
  104.4 64.8 %copy-start.10 = (bf16[128,4096]{1,0:T(8,128)(2,1)S(1)}, bf16[128,4096]{1,0:T(8,128)(2,1)}, u32[]{:S(2)}) copy-start(bf16[128,4096]{1,0:T(8,128)(2,1)} %copy-done.9) | copy-start | bytes 3145732
  104.4 44.7 %collective-permute-start.30 = (bf16[128,4096]{1,0:T(8,128)(2,1)}, bf16[128,4096]{1,0:T(8,128)(2,1)S(1)}, u32[]{:S(2)}, u32[]{:S(2)}) collective-permute-start(bf16[128,4096]{1,0:T(8,128)(2,1)} %collective-permute-done.29.refs_4_), channel_id=1, source_target_pairs={{0,1},{1,0},{2,3},{3,2},{4,5},{5,4},{6,7},{7,6},{8,9},{9,8},{10,11... | collective-permute-start | bytes 3145736 | tf_op jit(solution)/shard_map/ppermute | solution.py:199
  121.3 30.0 %collective-permute-start.33 = (bf16[128,4096]{1,0:T(8,128)(2,1)}, bf16[128,4096]{1,0:T(8,128)(2,1)S(1)}, u32[]{:S(2)}, u32[]{:S(2)}) collective-permute-start(bf16[128,4096]{1,0:T(8,128)(2,1)} %collective-permute-done.32.refs_4_), channel_id=1, source_target_pairs={{0,1},{1,0},{2,3},{3,2},{4,5},{5,4},{6,7},{7,6},{8,9},{9,8},{10,11... | collective-permute-start | bytes 3145736 | tf_op jit(solution)/shard_map/ppermute | solution.py:199
  121.4 32.3 %collective-permute-start.35 = (bf16[128,4096]{1,0:T(8,128)(2,1)}, bf16[128,4096]{1,0:T(8,128)(2,1)S(1)}, u32[]{:S(2)}, u32[]{:S(2)}) collective-permute-start(bf16[128,4096]{1,0:T(8,128)(2,1)} %collective-permute-done.1.refs_2_), channel_id=1, source_target_pairs={{0,2},{1,3},{2,0},{3,1},{4,6},{5,7},{6,4},{7,5},{8,10},{9,11},{10,... | collective-permute-start | bytes 3145736 | tf_op jit(solution)/shard_map/ppermute | solution.py:199
  121.7 47.2 %collective-permute-start.9 = (bf16[128,4096]{1,0:T(8,128)(2,1)}, bf16[128,4096]{1,0:T(8,128)(2,1)S(1)}, u32[]{:S(2)}, u32[]{:S(2)}) collective-permute-start(bf16[128,4096]{1,0:T(8,128)(2,1)} %collective-permute-done.8.refs_2_), channel_id=1, source_target_pairs={{0,4},{4,12},{8,0},{12,20},{16,8},{20,28},{24,16},{28,24},{1,5},{5... | collective-permute-start | bytes 3145736 | tf_op jit(solution)/shard_map/ppermute | solution.py:196
  149.0 50.9 %collective-permute-start.34 = (bf16[128,4096]{1,0:T(8,128)(2,1)}, bf16[128,4096]{1,0:T(8,128)(2,1)}, u32[]{:S(2)}, u32[]{:S(2)}) collective-permute-start(bf16[128,4096]{1,0:T(8,128)(2,1)} %collective-permute-done.1.refs_2_), channel_id=1, source_target_pairs={{0,1},{1,0},{2,3},{3,2},{4,5},{5,4},{6,7},{7,6},{8,9},{9,8},{10,11... | collective-permute-start | bytes 3145736 | tf_op jit(solution)/shard_map/ppermute | solution.py:199
  150.0 50.0 %collective-permute-start.38 = (bf16[128,4096]{1,0:T(8,128)(2,1)}, bf16[128,4096]{1,0:T(8,128)(2,1)}, u32[]{:S(2)}, u32[]{:S(2)}) collective-permute-start(bf16[128,4096]{1,0:T(8,128)(2,1)} %collective-permute-done.8.refs_2_), channel_id=1, source_target_pairs={{0,2},{1,3},{2,0},{3,1},{4,6},{5,7},{6,4},{7,5},{8,10},{9,11},{10,... | collective-permute-start | bytes 3145736 | tf_op jit(solution)/shard_map/ppermute | solution.py:199
  152.4 49.4 %collective-permute-start.2 = (bf16[128,4096]{1,0:T(8,128)(2,1)}, bf16[128,4096]{1,0:T(8,128)(2,1)S(1)}, u32[]{:S(2)}, u32[]{:S(2)}) collective-permute-start(bf16[128,4096]{1,0:T(8,128)(2,1)} %collective-permute-done.1.refs_2_), channel_id=1, source_target_pairs={{0,8},{4,0},{8,16},{12,4},{16,24},{20,12},{24,28},{28,20},{1,9},{5... | collective-permute-start | bytes 3145736 | tf_op jit(solution)/shard_map/ppermute | solution.py:196
  153.7 48.1 %copy-start.11 = (bf16[128,4096]{1,0:T(8,128)(2,1)}, bf16[128,4096]{1,0:T(8,128)(2,1)S(1)}, u32[]{:S(2)}) copy-start(bf16[128,4096]{1,0:T(8,128)(2,1)S(1)} %collective-permute-done.35.refs_4_) | copy-start | bytes 3145732
  153.7 82.7 %collective-permute-start.18 = (bf16[512,1792]{1,0:T(8,128)(2,1)}, bf16[512,1792]{1,0:T(8,128)(2,1)S(1)}, u32[]{:S(2)}, u32[]{:S(2)}) collective-permute-start(bf16[512,1792]{1,0:T(8,128)(2,1)} %collective-permute-done.17.refs_8_), channel_id=1, source_target_pairs={{0,8},{4,0},{8,16},{12,4},{16,24},{20,12},{24,28},{28,20},{1,9},{5... | collective-permute-start | bytes 5505032 | tf_op jit(solution)/shard_map/ppermute | solution.py:196
  168.9 67.4 %collective-permute-start.22 = (bf16[512,1792]{1,0:T(8,128)(2,1)S(1)}, bf16[512,1792]{1,0:T(8,128)(2,1)S(1)}, u32[]{:S(2)}, u32[]{:S(2)}) collective-permute-start(bf16[512,1792]{1,0:T(8,128)(2,1)S(1)} %collective-permute-done.21.refs_8_), channel_id=1, source_target_pairs={{0,4},{4,12},{8,0},{12,20},{16,8},{20,28},{24,16},{28,24},{1,5},{5... | collective-permute-start | bytes 5505032 | tf_op jit(solution)/shard_map/ppermute | solution.py:196
  200.0 34.6 %collective-permute-start.37 = (bf16[128,4096]{1,0:T(8,128)(2,1)}, bf16[128,4096]{1,0:T(8,128)(2,1)}, u32[]{:S(2)}, u32[]{:S(2)}) collective-permute-start(bf16[128,4096]{1,0:T(8,128)(2,1)} %collective-permute-done.8.refs_2_), channel_id=1, source_target_pairs={{0,1},{1,0},{2,3},{3,2},{4,5},{5,4},{6,7},{7,6},{8,9},{9,8},{10,11... | collective-permute-start | bytes 3145736 | tf_op jit(solution)/shard_map/ppermute | solution.py:199
  200.1 35.0 %collective-permute-start.10 = (bf16[64,4096]{1,0:T(8,128)(2,1)S(1)}, bf16[64,4096]{1,0:T(8,128)(2,1)S(1)}, u32[]{:S(2)}, u32[]{:S(2)}) collective-permute-start(bf16[64,4096]{1,0:T(8,128)(2,1)S(1)} %slice.63), channel_id=1, source_target_pairs={{0,4},{4,12},{8,0},{12,20},{16,8},{20,28},{24,16},{28,24},{1,5},{5... | collective-permute-start | bytes 1572872 | tf_op jit(solution)/shard_map/ppermute | solution.py:196
  201.8 36.2 %collective-permute-start.36 = (bf16[128,4096]{1,0:T(8,128)(2,1)S(1)}, bf16[128,4096]{1,0:T(8,128)(2,1)}, u32[]{:S(2)}, u32[]{:S(2)}) collective-permute-start(bf16[128,4096]{1,0:T(8,128)(2,1)S(1)} %collective-permute-done.35.refs_4_), channel_id=1, source_target_pairs={{0,1},{1,0},{2,3},{3,2},{4,5},{5,4},{6,7},{7,6},{8,9},{9,8},{10,11... | collective-permute-start | bytes 3145736 | tf_op jit(solution)/shard_map/ppermute | solution.py:199
  203.2 35.3 %copy-start.12 = (bf16[128,4096]{1,0:T(8,128)(2,1)S(1)}, bf16[128,4096]{1,0:T(8,128)(2,1)}, u32[]{:S(2)}) copy-start(bf16[128,4096]{1,0:T(8,128)(2,1)} %copy-done.11) | copy-start | bytes 3145732
  234.5 36.7 %collective-permute-start.3 = (bf16[64,4096]{1,0:T(8,128)(2,1)S(1)}, bf16[64,4096]{1,0:T(8,128)(2,1)S(1)}, u32[]{:S(2)}, u32[]{:S(2)}) collective-permute-start(bf16[64,4096]{1,0:T(8,128)(2,1)S(1)} %slice.62), channel_id=1, source_target_pairs={{0,8},{4,0},{8,16},{12,4},{16,24},{20,12},{24,28},{28,20},{1,9},{5... | collective-permute-start | bytes 1572872 | tf_op jit(solution)/shard_map/ppermute | solution.py:196
  235.0 37.9 %collective-permute-start.41 = (bf16[128,4096]{1,0:T(8,128)(2,1)S(1)}, bf16[128,4096]{1,0:T(8,128)(2,1)}, u32[]{:S(2)}, u32[]{:S(2)}) collective-permute-start(bf16[128,4096]{1,0:T(8,128)(2,1)S(1)} %collective-permute-done.2.refs_2_), channel_id=1, source_target_pairs={{0,2},{1,3},{2,0},{3,1},{4,6},{5,7},{6,4},{7,5},{8,10},{9,11},{10,... | collective-permute-start | bytes 3145736 | tf_op jit(solution)/shard_map/ppermute | solution.py:199
  236.3 34.9 %collective-permute-start.39 = (bf16[128,4096]{1,0:T(8,128)(2,1)}, bf16[128,4096]{1,0:T(8,128)(2,1)S(1)}, u32[]{:S(2)}, u32[]{:S(2)}) collective-permute-start(bf16[128,4096]{1,0:T(8,128)(2,1)} %collective-permute-done.38.refs_4_), channel_id=1, source_target_pairs={{0,1},{1,0},{2,3},{3,2},{4,5},{5,4},{6,7},{7,6},{8,9},{9,8},{10,11... | collective-permute-start | bytes 3145736 | tf_op jit(solution)/shard_map/ppermute | solution.py:199
  236.3 74.1 %collective-permute-start.19 = (bf16[512,1792]{1,0:T(8,128)(2,1)S(1)}, bf16[512,1792]{1,0:T(8,128)(2,1)S(1)}, u32[]{:S(2)}, u32[]{:S(2)}) collective-permute-start(bf16[512,1792]{1,0:T(8,128)(2,1)S(1)} %collective-permute-done.18.refs_8_), channel_id=1, source_target_pairs={{0,8},{4,0},{8,16},{12,4},{16,24},{20,12},{24,28},{28,20},{1,9},{5... | collective-permute-start | bytes 5505032 | tf_op jit(solution)/shard_map/ppermute | solution.py:196
  238.0 73.2 %collective-permute-start.23 = (bf16[512,1792]{1,0:T(8,128)(2,1)S(1)}, bf16[512,1792]{1,0:T(8,128)(2,1)S(1)}, u32[]{:S(2)}, u32[]{:S(2)}) collective-permute-start(bf16[512,1792]{1,0:T(8,128)(2,1)S(1)} %collective-permute-done.22.refs_8_), channel_id=1, source_target_pairs={{0,4},{4,12},{8,0},{12,20},{16,8},{20,28},{24,16},{28,24},{1,5},{5... | collective-permute-start | bytes 5505032 | tf_op jit(solution)/shard_map/ppermute | solution.py:196
  271.3 37.5 %collective-permute-start.40 = (bf16[128,4096]{1,0:T(8,128)(2,1)S(1)}, bf16[128,4096]{1,0:T(8,128)(2,1)}, u32[]{:S(2)}, u32[]{:S(2)}) collective-permute-start(bf16[128,4096]{1,0:T(8,128)(2,1)S(1)} %collective-permute-done.2.refs_2_), channel_id=1, source_target_pairs={{0,1},{1,0},{2,3},{3,2},{4,5},{5,4},{6,7},{7,6},{8,9},{9,8},{10,11... | collective-permute-start | bytes 3145736 | tf_op jit(solution)/shard_map/ppermute | solution.py:199
  272.3 36.8 %collective-permute-start.44 = (bf16[128,4096]{1,0:T(8,128)(2,1)S(1)}, bf16[128,4096]{1,0:T(8,128)(2,1)S(1)}, u32[]{:S(2)}, u32[]{:S(2)}) collective-permute-start(bf16[128,4096]{1,0:T(8,128)(2,1)S(1)} %collective-permute-done.9.refs_2_), channel_id=1, source_target_pairs={{0,2},{1,3},{2,0},{3,1},{4,6},{5,7},{6,4},{7,5},{8,10},{9,11},{10,... | collective-permute-start | bytes 3145736 | tf_op jit(solution)/shard_map/ppermute | solution.py:199
  273.0 37.4 %collective-permute-start.42 = (bf16[128,4096]{1,0:T(8,128)(2,1)}, bf16[128,4096]{1,0:T(8,128)(2,1)}, u32[]{:S(2)}, u32[]{:S(2)}) collective-permute-start(bf16[128,4096]{1,0:T(8,128)(2,1)} %collective-permute-done.41.refs_4_), channel_id=1, source_target_pairs={{0,1},{1,0},{2,3},{3,2},{4,5},{5,4},{6,7},{7,6},{8,9},{9,8},{10,11... | collective-permute-start | bytes 3145736 | tf_op jit(solution)/shard_map/ppermute | solution.py:199
  308.8 39.6 %collective-permute-start.43 = (bf16[128,4096]{1,0:T(8,128)(2,1)S(1)}, bf16[128,4096]{1,0:T(8,128)(2,1)S(1)}, u32[]{:S(2)}, u32[]{:S(2)}) collective-permute-start(bf16[128,4096]{1,0:T(8,128)(2,1)S(1)} %collective-permute-done.9.refs_2_), channel_id=1, source_target_pairs={{0,1},{1,0},{2,3},{3,2},{4,5},{5,4},{6,7},{7,6},{8,9},{9,8},{10,11... | collective-permute-start | bytes 3145736 | tf_op jit(solution)/shard_map/ppermute | solution.py:199
  309.1 37.5 %collective-permute-start.12 = (bf16[64,4096]{1,0:T(8,128)(2,1)S(1)}, bf16[64,4096]{1,0:T(8,128)(2,1)S(1)}, u32[]{:S(2)}, u32[]{:S(2)}) collective-permute-start(bf16[64,4096]{1,0:T(8,128)(2,1)S(1)} %collective-permute-done.10.refs_6_), channel_id=1, source_target_pairs={{0,2},{1,3},{2,0},{3,1},{4,6},{5,7},{6,4},{7,5},{8,10},{9,11},{10,... | collective-permute-start | bytes 1572872 | tf_op jit(solution)/shard_map/ppermute | solution.py:199
  310.4 36.8 %collective-permute-start.11 = (bf16[64,4096]{1,0:T(8,128)(2,1)S(1)}, bf16[64,4096]{1,0:T(8,128)(2,1)S(1)}, u32[]{:S(2)}, u32[]{:S(2)}) collective-permute-start(bf16[64,4096]{1,0:T(8,128)(2,1)S(1)} %collective-permute-done.10.refs_6_), channel_id=1, source_target_pairs={{0,1},{1,0},{2,3},{3,2},{4,5},{5,4},{6,7},{7,6},{8,9},{9,8},{10,11... | collective-permute-start | bytes 1572872 | tf_op jit(solution)/shard_map/ppermute | solution.py:199
  310.4 36.6 %collective-permute-start.5 = (bf16[64,4096]{1,0:T(8,128)(2,1)S(1)}, bf16[64,4096]{1,0:T(8,128)(2,1)}, u32[]{:S(2)}, u32[]{:S(2)}) collective-permute-start(bf16[64,4096]{1,0:T(8,128)(2,1)S(1)} %collective-permute-done.3.refs_2_), channel_id=1, source_target_pairs={{0,2},{1,3},{2,0},{3,1},{4,6},{5,7},{6,4},{7,5},{8,10},{9,11},{10,... | collective-permute-start | bytes 1572872 | tf_op jit(solution)/shard_map/ppermute | solution.py:199
  311.2 38.8 %collective-permute-start.45 = (bf16[128,4096]{1,0:T(8,128)(2,1)S(1)}, bf16[128,4096]{1,0:T(8,128)(2,1)S(1)}, u32[]{:S(2)}, u32[]{:S(2)}) collective-permute-start(bf16[128,4096]{1,0:T(8,128)(2,1)S(1)} %collective-permute-done.44.refs_4_), channel_id=1, source_target_pairs={{0,1},{1,0},{2,3},{3,2},{4,5},{5,4},{6,7},{7,6},{8,9},{9,8},{10,11... | collective-permute-start | bytes 3145736 | tf_op jit(solution)/shard_map/ppermute | solution.py:199
  345.4 5.0 %copy-start.6 = (bf16[2,512,1792]{2,1,0:T(8,128)(2,1)}, bf16[2,512,1792]{2,1,0:T(8,128)(2,1)S(1)}, u32[]{:S(2)}) copy-start(bf16[2,512,1792]{2,1,0:T(8,128)(2,1)S(1)} %get-tuple-element.20.refs_14_.refs_19_.refs_5_) | copy-start | bytes 11010052
  346.6 36.7 %copy-start.21 = (bf16[64,4096]{1,0:T(8,128)(2,1)}, bf16[64,4096]{1,0:T(8,128)(2,1)S(1)}, u32[]{:S(2)}) copy-start(bf16[64,4096]{1,0:T(8,128)(2,1)S(1)} %collective-permute-done.12.refs_8_) | copy-start | bytes 1572868
  346.6 38.5 %collective-permute-start.4 = (bf16[64,4096]{1,0:T(8,128)(2,1)S(1)}, bf16[64,4096]{1,0:T(8,128)(2,1)S(1)}, u32[]{:S(2)}, u32[]{:S(2)}) collective-permute-start(bf16[64,4096]{1,0:T(8,128)(2,1)S(1)} %collective-permute-done.3.refs_2_), channel_id=1, source_target_pairs={{0,1},{1,0},{2,3},{3,2},{4,5},{5,4},{6,7},{7,6},{8,9},{9,8},{10,11... | collective-permute-start | bytes 1572872 | tf_op jit(solution)/shard_map/ppermute | solution.py:199
  347.0 38.1 %collective-permute-start.13 = (bf16[64,4096]{1,0:T(8,128)(2,1)S(1)}, bf16[64,4096]{1,0:T(8,128)(2,1)S(1)}, u32[]{:S(2)}, u32[]{:S(2)}) collective-permute-start(bf16[64,4096]{1,0:T(8,128)(2,1)S(1)} %collective-permute-done.12.refs_8_), channel_id=1, source_target_pairs={{0,1},{1,0},{2,3},{3,2},{4,5},{5,4},{6,7},{7,6},{8,9},{9,8},{10,11... | collective-permute-start | bytes 1572872 | tf_op jit(solution)/shard_map/ppermute | solution.py:199
  348.0 37.1 %collective-permute-start.6 = (bf16[64,4096]{1,0:T(8,128)(2,1)}, bf16[64,4096]{1,0:T(8,128)(2,1)S(1)}, u32[]{:S(2)}, u32[]{:S(2)}) collective-permute-start(bf16[64,4096]{1,0:T(8,128)(2,1)} %collective-permute-done.5.refs_4_), channel_id=1, source_target_pairs={{0,1},{1,0},{2,3},{3,2},{4,5},{5,4},{6,7},{7,6},{8,9},{9,8},{10,11... | collective-permute-start | bytes 1572872 | tf_op jit(solution)/shard_map/ppermute | solution.py:199
  348.3 36.8 %collective-permute-start.20 = (bf16[256,1792]{1,0:T(8,128)(2,1)}, bf16[256,1792]{1,0:T(8,128)(2,1)S(1)}, u32[]{:S(2)}, u32[]{:S(2)}) collective-permute-start(bf16[256,1792]{1,0:T(8,128)(2,1)} %slice.70), channel_id=1, source_target_pairs={{0,8},{4,0},{8,16},{12,4},{16,24},{20,12},{24,28},{28,20},{1,9},{5... | collective-permute-start | bytes 2752520 | tf_op jit(solution)/shard_map/ppermute | solution.py:196
  350.0 35.1 %collective-permute-start.24 = (bf16[256,1792]{1,0:T(8,128)(2,1)S(1)}, bf16[256,1792]{1,0:T(8,128)(2,1)S(1)}, u32[]{:S(2)}, u32[]{:S(2)}) collective-permute-start(bf16[256,1792]{1,0:T(8,128)(2,1)S(1)} %slice.71), channel_id=1, source_target_pairs={{0,4},{4,12},{8,0},{12,20},{16,8},{20,28},{24,16},{28,24},{1,5},{5... | collective-permute-start | bytes 2752520 | tf_op jit(solution)/shard_map/ppermute | solution.py:196
  350.4 34.8 %copy-start.24 = (bf16[64,4096]{1,0:T(8,128)(2,1)S(1)}, bf16[64,4096]{1,0:T(8,128)(2,1)}, u32[]{:S(2)}) copy-start(bf16[64,4096]{1,0:T(8,128)(2,1)} %copy-done.23) | copy-start | bytes 1572868
  386.2 55.2 %copy-start.1 = (bf16[2,512,1792]{2,1,0:T(8,128)(2,1)S(1)}, bf16[2,512,1792]{2,1,0:T(8,128)(2,1)}, u32[]{:S(2)}) copy-start(bf16[2,512,1792]{2,1,0:T(8,128)(2,1)} %copy-done) | copy-start | bytes 11010052
  386.2 55.2 %copy-start.3 = (bf16[2,512,1792]{2,1,0:T(8,128)(2,1)S(1)}, bf16[2,512,1792]{2,1,0:T(8,128)(2,1)}, u32[]{:S(2)}) copy-start(bf16[2,512,1792]{2,1,0:T(8,128)(2,1)} %copy-done.2) | copy-start | bytes 11010052
  424.9 1.2 collective-permute-start.46
  426.0 3.6 collective-permute-start.47
  429.6 3.6 collective-permute-start.48
  433.3 3.6 collective-permute-start.49
  436.9 4.5 collective-permute-start.50
  (19 other events, 28.9 us)

commit v2 on v1

v2 whole, which is shorter than its diff:
```python
import functools

import jax
import jax.numpy as jnp
from jax import lax
from jax.experimental import pallas as pl
from jax.experimental.pallas import tpu as pltpu
from jax.sharding import PartitionSpec as P

NBYZ = 3
ITERS = 3
LINE = 4
AXES = ("colony", "fsdp")
VMEM = 28 * 1024 * 1024


def ring_order(count):
    width = count // LINE
    if count % LINE or width % 2:
        return list(range(count))
    order = [(0, 0)]
    for y in range(width):
        column = list(range(1, LINE))
        order += [(z, y) for z in (column if y % 2 == 0 else column[::-1])]
    order += [(0, y) for y in range(width - 1, 0, -1)]
    return [z * width + y for z, y in order]


def slot_shifts(count):
    shifts = [0]
    for step in range(1, count // 2):
        shifts += [step, -step]
    return shifts + [count // 2]


def exact_dot(left, right):
    return jnp.dot(
        left, right, precision=lax.Precision.HIGHEST, preferred_element_type=jnp.float32
    )


def one_hot(shape, axis, sub, slots_ref, slots):
    piece = lax.broadcasted_iota(jnp.int32, shape, axis)
    colony = lax.broadcasted_iota(jnp.int32, shape, 1 - axis)
    result = jnp.zeros(shape, jnp.float32)
    for slot in slots:
        hit = (piece >= slot * sub) & (piece < (slot + 1) * sub) & (colony == slots_ref[slot])
        result = jnp.where(hit, 1.0, result)
    return result


def colony_kernel(slots, count, parts, n_parts, n_cot, *refs):
    refs = list(refs)
    last = slots[-1] == count - 1
    slots_ref = refs.pop(0)
    parts_refs = [refs.pop(0) for _ in range(n_parts)]
    gate_ref, up_ref = refs.pop(0), refs.pop(0)
    cot_refs = [[refs.pop(0) for _ in range(n_cot)] for _ in slots]
    before = [refs.pop(0) for _ in range(slots[0])] if last else []
    grad_refs = [refs.pop(0) for _ in slots]
    table_ref = refs.pop(0) if last else None
    tokens, rows_t, sems = refs[:3]
    gram = refs[3] if last else None
    step = pl.program_id(0)
    rows = rows_t.shape[1]

    copies = []
    for at, part in enumerate(parts):
        copies.append([])
        for which, start, size, target in part:
            copies[at].append(
                pltpu.make_async_copy(
                    parts_refs[which].at[pl.ds(start, size)],
                    tokens.at[at, pl.ds(target, size)],
                    sems.at[at, len(copies[at])],
                )
            )

    def arrive(at):
        for copy in copies[at]:
            copy.wait()
        if at + 1 < len(slots):
            for copy in copies[at + 1]:
                copy.start()
        first = pl.multiple_of(slots_ref[count] * rows, rows)
        rows_t[at] = tokens[at, :, pl.ds(first, rows)].T

    def gradients(at):
        gate = jnp.dot(tokens[at], gate_ref[...], preferred_element_type=jnp.float32)
        up = jnp.dot(tokens[at], up_ref[...], preferred_element_type=jnp.float32)
        sig = jax.nn.sigmoid(gate)
        cot = [ref[...] for ref in cot_refs[at]]
        back = (cot[0] if n_cot == 1 else jnp.concatenate(cot, axis=0)).astype(jnp.float32)
        d_up = (back * gate * sig).astype(jnp.bfloat16)
        d_gate = (back * up * sig * (1.0 + gate * (1.0 - sig))).astype(jnp.bfloat16)
        for matrix, delta in ((0, d_gate), (1, d_up)):
            grad_refs[at][matrix] = jnp.dot(
                rows_t[at], delta, preferred_element_type=jnp.float32
            ).astype(jnp.bfloat16)

    def products():
        every = before + grad_refs
        sub = gram.shape[0] // count
        wide = 8

        def add(at, carry):
            cut = []
            for part in range(wide):
                span = pl.ds(pl.multiple_of((at * wide + part) * sub, sub), sub)
                for matrix in range(2):
                    pieces = [ref[matrix, span, :] for ref in every]
                    cut.append(jnp.concatenate(pieces, axis=0))
            side = jnp.concatenate(cut, axis=1)
            gram[...] += lax.dot_general(
                side, side, (((1,), (1,)), ((), ())), preferred_element_type=jnp.float32
            )
            return carry

        lax.fori_loop(0, rows // (sub * wide), add, 0)

    @pl.when(step == 0)
    def _():
        for copy in copies[0]:
            copy.start()
        if last:
            gram[...] = jnp.zeros_like(gram)
        for at in range(len(slots)):
            arrive(at)
            gradients(at)

    @pl.when(step > 0)
    def _():
        for at in range(len(slots)):
            gradients(at)

    if last:
        products()

        @pl.when(step == pl.num_programs(0) - 1)
        def _():
            size = gram.shape[0]
            sub = size // count
            row = lax.broadcasted_iota(jnp.int32, gram.shape, 0)
            lane = lax.broadcasted_iota(jnp.int32, gram.shape, 1)
            kept = jnp.where((row & (sub - 1)) == (lane & (sub - 1)), gram[...], 0.0)
            left = one_hot((table_ref.shape[0], size), 1, sub, slots_ref, range(count))
            right = one_hot((size, table_ref.shape[1]), 0, sub, slots_ref, range(count))
            table_ref[...] = exact_dot(exact_dot(left, kept), right)


def combine_kernel(count, table_ref, factors_ref, factor_ref, slots_ref, *refs):
    grads = refs[:count]
    gate_out, up_out = refs[count : count + 2]
    coef = refs[count + 2]

    @pl.when(pl.program_id(0) == 0)
    def _():
        table = table_ref[...] * factors_ref[...]
        shape = table.shape
        row = lax.broadcasted_iota(jnp.int32, shape, 0)
        lane = lax.broadcasted_iota(jnp.int32, shape, 1)
        one = jnp.where(row == lane, 1.0, 0.0)
        in_row = lax.broadcasted_iota(jnp.int32, (1, shape[1]), 1) < count
        in_column = lax.broadcasted_iota(jnp.int32, (shape[0], 1), 0) < count
        share_row = jnp.where(in_row, 1.0 / count, 0.0)
        share_column = jnp.where(in_column, 1.0 / count, 0.0)
        for _ in range(ITERS):
            to_row = jnp.sum(table * share_column, axis=0, keepdims=True)
            to_column = jnp.sum(table * share_row, axis=1, keepdims=True)
            near_column = jnp.sum((table - to_row) * (one - share_row), axis=1, keepdims=True)
            near_row = jnp.sum((table - to_column) * (one - share_column), axis=0, keepdims=True)
            dist_row = jnp.sqrt(jnp.maximum(near_row, 0.0) + 1e-06)
            dist_column = jnp.sqrt(jnp.maximum(near_column, 0.0) + 1e-06)
            weight_row = jnp.where(in_row, 1.0 / dist_row, 0.0)
            weight_column = jnp.where(in_column, 1.0 / dist_column, 0.0)
            share_row = weight_row / jnp.sum(weight_row)
            share_column = weight_column / jnp.sum(weight_column)
        mine = share_row * factor_ref[...]
        lanes = lax.broadcasted_iota(jnp.int32, (1, shape[1]), 1)
        for k in range(count):
            coef[k] = jnp.sum(jnp.where(lanes == slots_ref[k], mine, 0.0))

    scales = [coef[k] for k in range(count)]
    rows = gate_out.shape[0]
    chunk = 16
    for matrix, out in ((0, gate_out), (1, up_out)):

        def body(at, carry, matrix=matrix, out=out):
            span = pl.ds(pl.multiple_of(at * chunk, chunk), chunk)
            total = scales[0] * grads[0][matrix, span, :].astype(jnp.float32)
            for k in range(1, count):
                total = total + scales[k] * grads[k][matrix, span, :].astype(jnp.float32)
            out[span, :] = total
            return carry

        lax.fori_loop(0, rows // chunk, body, 0)


def on_device(order, hidden_states, norm_gain, gate_weight, up_weight, hidden_grad, byz_order, byz_scale):
    count, shards = len(order), lax.axis_size("fsdp")
    colony, shard = lax.axis_index("colony"), lax.axis_index("fsdp")
    width = gate_weight.shape[1]
    depth = hidden_states.shape[2]
    share = hidden_states.shape[1]
    half = share // 2
    rows = depth // count
    total_tokens = share * shards
    block = 256 if width % 256 == 0 else 128
    place = {c: at for at, c in enumerate(order)}
    shifts = slot_shifts(count)

    def hop(value, delta):
        pairs = []
        for c in range(count):
            to = order[(place[c] + delta) % count]
            pairs.append((c, to))
        return lax.ppermute(value, "colony", pairs)

    def swap(value, mask):
        return lax.ppermute(value, "fsdp", [(j, j ^ mask) for j in range(shards)])

    def spread_chips(own):
        pieces = {0: own}
        bit = shards // 2
        while bit > 1:
            for m in list(pieces):
                pieces[m | bit] = swap(pieces[m], bit)
            bit //= 2
        return pieces

    def spread_cores(pieces):
        every = dict(pieces)
        for m, piece in pieces.items():
            every[m | 1] = swap(piece, 1)
        return [every[m] for m in range(shards)]

    values = hidden_states[0].astype(jnp.float32)
    meansq = jnp.mean(values * values, axis=-1, keepdims=True)
    normed = (values * lax.rsqrt(meansq + 1e-05) * norm_gain).astype(jnp.bfloat16)

    local_grad = hidden_grad[0]
    cuts = []
    for m in range(shards):
        columns = lax.dynamic_slice(local_grad, (0, (shard ^ m) * width), (share, width))
        cuts.append(columns if m == 0 else swap(columns, m))
    cot = jnp.concatenate([c[h * half : (h + 1) * half] for h in range(2) for c in cuts], axis=0)
    mid = total_tokens // 2

    ring = jnp.asarray(order, jnp.int32)
    at = jnp.asarray([place[c] for c in range(count)], jnp.int32)[colony]
    held = ring[(at - jnp.asarray(shifts, jnp.int32)) % count]
    slots = jnp.concatenate([held, colony[None].astype(jnp.int32)])
    table_shape = (max(8, count), 128)
    lanes = jnp.arange(128, dtype=jnp.int32)
    hits = byz_order[:NBYZ][:, None] == lanes[None, :]
    factor = 1.0 + jnp.sum(jnp.where(hits, -byz_scale[:, None] - 1.0, jnp.float32(0.0)), axis=0)
    factor = jnp.where(lanes < count, factor, 0.0)
    factors = factor[: table_shape[0], None] * factor[None, :]

    smem = pl.BlockSpec(memory_space=pltpu.SMEM)
    anywhere = pl.BlockSpec(memory_space=pl.ANY)
    column = pl.BlockSpec((depth, block), lambda b: (0, b))
    block_of_grad = pl.BlockSpec((2, rows, block), lambda b: (0, 0, b))

    def colonies(group, tokens, cots, before):
        if n_pieces := len(cots[0]) - 1:
            parts = [
                [(m, h * half, half, (h * shards + m) * half) for h in range(2) for m in range(shards)]
            ]
        else:
            parts = [
                [
                    (m, at * share + h * half, half, (h * shards + m) * half)
                    for h in range(2)
                    for m in range(shards)
                ]
                for at in range(len(group))
            ]
        n_cot = n_pieces + 1
        last = group[-1] == count - 1
        in_specs = [smem] + [anywhere] * shards + [column, column]
        in_specs += [pl.BlockSpec((c.shape[0], block), lambda b: (0, b)) for c in sum(cots, [])]
        out_shape = [jax.ShapeDtypeStruct((2, rows, width), jnp.bfloat16)] * len(group)
        out_specs = [block_of_grad] * len(group)
        scratch = [
            pltpu.VMEM((len(group), total_tokens, depth), jnp.bfloat16),
            pltpu.VMEM((len(group), rows, total_tokens), jnp.bfloat16),
            pltpu.SemaphoreType.DMA((len(group), 2 * shards)),
        ]
        operands = [slots, *tokens, gate_weight, up_weight, *sum(cots, [])]
        if last:
            in_specs += [block_of_grad] * len(before)
            operands += before
            out_shape.append(jax.ShapeDtypeStruct(table_shape, jnp.float32))
            out_specs.append(pl.BlockSpec(table_shape, lambda b: (0, 0)))
            scratch.append(pltpu.VMEM((256, 256), jnp.float32))
        flops = len(group) * 2 * total_tokens * width * 2 * (depth + rows)
        return pl.pallas_call(
            functools.partial(colony_kernel, group, count, parts, shards, n_cot),
            grid=(width // block,),
            in_specs=in_specs,
            out_specs=out_specs,
            out_shape=out_shape,
            scratch_shapes=scratch,
            compiler_params=pltpu.CompilerParams(vmem_limit_bytes=VMEM),
            cost_estimate=pl.CostEstimate(
                flops=flops, bytes_accessed=4 * depth * width, transcendentals=total_tokens * width
            ),
        )(*operands)

    ways = (1, -1)
    far = count // 2
    n_at = {(0, way): normed for way in ways}
    c_at = {(0, way): cot for way in ways}

    def send_tokens(step):
        for h, way in enumerate(ways):
            value = n_at[step - 1, way]
            if step == far:
                value = value[h * half : (h + 1) * half]
            n_at[step, way] = hop(value, way)

    def send_cot(step):
        for h, way in enumerate(ways):
            value = c_at[step - 1, way]
            if step == far:
                value = value[h * mid : (h + 1) * mid]
            c_at[step, way] = hop(value, way)

    def both(step):
        return jnp.concatenate([n_at[step, way] for way in ways], axis=0)

    def fence():
        nonlocal n_at, c_at, chips, grads
        n_at, c_at, chips, grads = lax.optimization_barrier((n_at, c_at, chips, grads))

    grads, chips = [], {0: normed}
    send_tokens(1)
    fence()
    chips[0] = spread_chips(chips[0])
    send_tokens(2)
    fence()
    for step in range(far + 1):
        cores = spread_cores(chips[step])
        if step + 1 <= far:
            send_cot(step + 1)
            chips[step + 1] = spread_chips(both(step + 1))
        if 0 < step <= far - 2:
            send_tokens(step + 2)
        if step == 0:
            group, cots = [0], [[c_at[0, 1]]]
        elif step < far:
            group, cots = [2 * step - 1, 2 * step], [[c_at[step, way]] for way in ways]
        else:
            group, cots = [count - 1], [[c_at[far, way] for way in ways]]
        grads = [*grads, *colonies(group, cores, cots, grads)]
        if step < far:
            fence()
    table = grads.pop()
    devices = count * shards
    bit = 1
    while bit < devices:
        table = table + lax.ppermute(table, AXES, [(d, d ^ bit) for d in range(devices)])
        bit *= 2

    cut = min(64, rows)
    whole = pl.BlockSpec(table_shape, lambda b: (0, 0))
    out_block = pl.BlockSpec((cut, width), lambda b: (b, 0))
    return pl.pallas_call(
        functools.partial(combine_kernel, count),
        grid=(rows // cut,),
        in_specs=[whole, whole, pl.BlockSpec((1, 128), lambda b: (0, 0)), smem]
        + [pl.BlockSpec((2, cut, width), lambda b: (0, b, 0))] * count,
        out_specs=[out_block, out_block],
        out_shape=[jax.ShapeDtypeStruct((rows, width), jnp.float32)] * 2,
        scratch_shapes=[pltpu.SMEM((count,), jnp.float32)],
        compiler_params=pltpu.CompilerParams(vmem_limit_bytes=VMEM),
    )(table, factors, factor[None], slots, *grads)


def solution(mesh):
    placed = (
        P("colony", "fsdp", None),
        P(),
        P(None, "fsdp"),
        P(None, "fsdp"),
        P("colony", "fsdp", None),
        P(),
        P(),
    )
    return jax.shard_map(
        functools.partial(on_device, ring_order(mesh.shape["colony"])),
        mesh=mesh,
        in_specs=placed,
        out_specs=(P("colony", "fsdp"), P("colony", "fsdp")),
        check_vma=False,
    )
```

time: 457 us -> 371 us (0.81); the launches traced: 457 us -> 365 us
  Pallas kernels: 264 us -> 197 us
  waiting for transfers between devices: 119 us -> 88.1 us
  local copies, waits for them, and re-layouts: 29.6 us -> 42.8 us
  starting transfers between devices: 41.9 us -> 33.8 us
    pallas_call x9 -> x6, Pallas kernels: 264 us -> 197 us  [the longest x5 186 us: colonies(): pl.pallas_call(functools.partial(colony_kernel, group, count, parts, shar...]
    ppermute x30 -> x18, waiting for transfers between devices: 78.8 us -> 28.5 us  [swap(): return lax.ppermute(value, 'fsdp', [(j, j ^ mask) for j in range(shards)])]
    ppermute x16, waiting for transfers between devices: 30.8 us -> 47.9 us  [hop(): return lax.ppermute(value, 'colony', pairs)]
    unnamed x76 -> x81, local copies, waits for them, and re-layouts: 24.7 us -> 35.4 us
    ppermute x30 -> x18, starting transfers between devices: 15.7 us -> 11.2 us  [swap(): return lax.ppermute(value, 'fsdp', [(j, j ^ mask) for j in range(shards)])]
  transfers between devices with their start and end apart: 51 -> 39, of which waited for: 13 -> 19; matrix products, arithmetic and copies ran while one was open for 1% -> 4% of each run, Pallas kernels for 46% -> 41%
where the time goes in v2:
time: 371 us; the launch traced here: 365 us
  Pallas kernels  197 us (53%)
  waiting for transfers between devices  88.1 us (24%)
  local copies, waits for them, and re-layouts  42.8 us (12%)
  starting transfers between devices  33.8 us (9%)
    pallas_call x5, Pallas kernels, colonies(): pl.pallas_call(functools.partial(colony_kernel, group, count, parts, shar...  186 us
    ppermute x16, waiting for transfers between devices, hop(): return lax.ppermute(value, 'colony', pairs)  47.9 us
    unnamed x81, local copies, waits for them, and re-layouts  35.4 us
    ppermute x18, waiting for transfers between devices, swap(): return lax.ppermute(value, 'fsdp', [(j, j ^ mask) for j in range(shards)])  28.5 us
    ppermute x16, starting transfers between devices, hop(): return lax.ppermute(value, 'colony', pairs)  17.9 us
    ppermute x5, waiting for transfers between devices, on_device(): lax.ppermute(table, AXES, [(d, d ^ bit) for d in range(devices)])  11.7 us
    ppermute x18, starting transfers between devices, swap(): return lax.ppermute(value, 'fsdp', [(j, j ^ mask) for j in range(shards)])  11.2 us
    pallas_call x1, Pallas kernels, on_device(): pl.pallas_call(functools.partial(combine_kernel, count), grid=(rows // cu...  11.1 us
  transfers between devices with their start and end apart: 39, of which 19 were waited for; matrix products, arithmetic and copies ran while one was open for 4% of the time, Pallas kernels for 41%

profile of v2, /device:TPU:0, one launch (start us, length us, event | category | flops | bytes accessed | tf_op | source)
XLA Modules:
  0.0 364.8 jit_solution(2708507450530127138)
XLA Ops:
  0.7 2.5 dynamic-slice_bitcast_fusion
  4.3 2.6 collective-permute-start
  7.0 1.9 collective-permute-start.3
  8.8 1.0 fusion.4
  9.8 10.8 %collective-permute-done.3 = bf16[128,1792]{1,0:T(8,128)(2,1)} collective-permute-done((bf16[128,1792]{1,0:T(8,128)(2,1)}, bf16[128,1792]{1,0:T(8,128)(2,1)}, u32[]{:S(2)}, u32[]{:S(2)}) %collective-permute-start.3) | collective-permute-done | bytes 458784 | tf_op jit(solution)/shard_map/ppermute | solution.py:220
  21.6 7.5 %collective-permute-done.4 = bf16[128,1792]{1,0:T(8,128)(2,1)} collective-permute-done((bf16[128,1792]{1,0:T(8,128)(2,1)}, bf16[128,1792]{1,0:T(8,128)(2,1)}, u32[]{:S(2)}, u32[]{:S(2)}) %collective-permute-start.4) | collective-permute-done | bytes 458784 | tf_op jit(solution)/shard_map/ppermute | solution.py:220
  30.0 1.0 fusion.3
  31.0 1.0 slice_dynamic-update-slice_fusion.1
  32.0 1.0 slice_dynamic-update-slice_fusion.refs_7_
  33.0 1.4 collective-permute-start.5
  35.1 1.3 collective-permute-start.7
  36.3 22.8 %collective-permute-done.5 = bf16[128,4096]{1,0:T(8,128)(2,1)S(1)} collective-permute-done((bf16[128,4096]{1,0:T(8,128)(2,1)}, bf16[128,4096]{1,0:T(8,128)(2,1)S(1)}, u32[]{:S(2)}, u32[]{:S(2)}) %collective-permute-start.5) | collective-permute-done | bytes 1048608 | tf_op jit(solution)/shard_map/ppermute | solution.py:217
  59.1 1.3 collective-permute-done.6
  61.5 1.3 constant_dynamic-update-slice_fusion.1
  62.8 1.3 constant_dynamic-update-slice_fusion.refs_1_
  64.1 1.6 collective-permute-start.10
  66.4 1.6 collective-permute-start.8
  69.9 1.5 copy-done.14
  71.4 5.2 %copy-done.15 = bf16[4096,1792]{1,0:T(8,128)(2,1)S(1)} copy-done((bf16[4096,1792]{1,0:T(8,128)(2,1)S(1)}, bf16[4096,1792]{1,0:T(8,128)(2,1)}, u32[]{:S(2)}) %copy-start.15) | copy-done | bytes 14680088
  76.6 24.4 %shard_map.113.refs_9_.refs_0_ = bf16[2,512,1792]{2,1,0:T(8,128)(2,1)S(1)} custom-call(s32[9]{0:T(128)S(1)} %pad_add_fusion.refs_0_.slots_ref, bf16[128,4096]{1,0:T(8,128)(2,1)S(1)} %fusion.2.refs_1_, bf16[128,4096]{1,0:T(8,128)(2,1)} %collective-permute-done.11.refs_2_, bf16[128,4096]{1,0:T(8,128)(2,1)} %collective-permute-done.7.refs_3_, ...), custom_call_target="tpu_custom_call" | custom-call | flops 16911433728 | bytes 29360128 | tf_op jit(solution)/shard_map/pallas_call | solution.py:298
  101.0 7.8 %collective-permute-done.8.refs_8_ = bf16[512,1792]{1,0:T(8,128)(2,1)} collective-permute-done((bf16[512,1792]{1,0:T(8,128)(2,1)}, bf16[512,1792]{1,0:T(8,128)(2,1)}, u32[]{:S(2)}, u32[]{:S(2)}) %collective-permute-start.8) | collective-permute-done | bytes 1835040 | tf_op jit(solution)/shard_map/ppermute | solution.py:217
  108.8 1.3 collective-permute-done.9.refs_7_
  110.1 2.2 collective-permute-done.10.refs_3_
  112.8 1.6 collective-permute-start.13
  115.0 1.6 collective-permute-start.17
  116.6 2.1 collective-permute-done.18.refs_2_
  118.7 1.6 collective-permute-start.15
  121.2 42.7 %shard_map.114 = (bf16[2,512,1792]{2,1,0:T(8,128)(2,1)S(1)}, bf16[2,512,1792]{2,1,0:T(8,128)(2,1)S(1)}) custom-call(s32[9]{0:T(128)S(1)} %pad_add_fusion.refs_0_.slots_ref, bf16[256,4096]{1,0:T(8,128)(2,1)S(1)} %copy-done.10, bf16[256,4096]{1,0:T(8,128)(2,1)S(1)} %collective-permute-done.18.refs_2_, bf16[256,4096]{1,0:T(8,128)(2,1)} %collective-permute-done.10.refs_3_, ...), custom_call_target="tpu_custom_call" | custom-call | flops 33822867456 | bytes 29360128 | tf_op jit(solution)/shard_map/pallas_call | solution.py:298
  164.0 13.4 %collective-permute-done.15.refs_8_ = bf16[512,1792]{1,0:T(8,128)(2,1)} collective-permute-done((bf16[512,1792]{1,0:T(8,128)(2,1)}, bf16[512,1792]{1,0:T(8,128)(2,1)}, u32[]{:S(2)}, u32[]{:S(2)}) %collective-permute-start.15) | collective-permute-done | bytes 1835040 | tf_op jit(solution)/shard_map/ppermute | solution.py:217
  177.3 1.3 collective-permute-done.16.refs_7_
  179.2 1.0 slice.58
  180.4 1.6 collective-permute-start.24
  182.0 1.6 collective-permute-start.22
  184.0 1.3 copy-done.18
  185.3 1.6 collective-permute-start.20
  186.9 1.3 copy-done.20
  188.8 1.6 copy-done.17
  190.4 1.6 copy-done.19
  192.0 1.6 copy-done.21
  193.6 41.1 %shard_map.115 = (bf16[2,512,1792]{2,1,0:T(8,128)(2,1)S(1)}, bf16[2,512,1792]{2,1,0:T(8,128)(2,1)S(1)}) custom-call(s32[9]{0:T(128)S(1)} %pad_add_fusion.refs_0_.slots_ref, bf16[256,4096]{1,0:T(8,128)(2,1)S(1)} %constant_dynamic-update-slice_fusion.2.refs_1_, bf16[256,4096]{1,0:T(8,128)(2,1)S(1)} %copy-done.19, bf16[256,4096]{1,0:T(8,128)(2,1)S(1)} %copy-done.17, ...), custom_call_target="tpu_custom_call" | custom-call | flops 33822867456 | bytes 29360128 | tf_op jit(solution)/shard_map/pallas_call | solution.py:298
  234.8 1.8 copy-done.2
  237.2 1.5 constant_dynamic-update-slice_fusion.7
  239.4 1.6 collective-permute-start.27
  241.8 1.3 collective-permute-done.30.refs_2_
  243.1 1.0 collective-permute-done.31.refs_4_
  244.1 42.5 %shard_map.116 = (bf16[2,512,1792]{2,1,0:T(8,128)(2,1)S(1)}, bf16[2,512,1792]{2,1,0:T(8,128)(2,1)S(1)}) custom-call(s32[9]{0:T(128)S(1)} %pad_add_fusion.refs_0_.slots_ref, bf16[256,4096]{1,0:T(8,128)(2,1)S(1)} %constant_dynamic-update-slice_fusion.4.refs_1_, bf16[256,4096]{1,0:T(8,128)(2,1)S(1)} %collective-permute-done.30.refs_2_, ...), custom_call_target="tpu_custom_call" | custom-call | flops 33822867456 | bytes 29360128 | tf_op jit(solution)/shard_map/pallas_call | solution.py:298
  286.6 1.8 copy-done.4
  288.4 1.8 copy-done.6
  291.8 2.1 collective-permute-done.32.refs_2_
  293.9 1.5 collective-permute-done.33.refs_4_
  295.4 2.0 copy-done.1
  297.5 1.2 copy-done.12
  298.7 1.2 copy-done.23
  299.9 35.2 %shard_map.117 = (bf16[2,512,1792]{2,1,0:T(8,128)(2,1)S(1)}, f32[8,128]{1,0:T(8,128)S(1)}) custom-call(s32[9]{0:T(128)S(1)} %pad_add_fusion.refs_0_.slots_ref, bf16[128,4096]{1,0:T(8,128)(2,1)S(1)} %copy-done.12, bf16[128,4096]{1,0:T(8,128)(2,1)S(1)} %collective-permute-done.32.refs_2_, bf16[128,4096]{1,0:T(8,128)(2,1)S(1)} %collective-permute-done.29.refs_3_, ...), custom_call_target="tpu_custom_call" | custom-call | flops 16911433728 | bytes 29360128 | tf_op jit(solution)/shard_map/pallas_call | solution.py:298
  335.0 1.8 copy-done.8
  337.0 1.0 collective-permute-done.34
  338.6 3.0 collective-permute-done.35
  341.6 1.6 collective-permute-start.36
  343.2 2.0 collective-permute-done.36
  345.2 1.1 collective-permute-start.37
  346.5 2.4 collective-permute-done.37
  348.9 1.3 collective-permute-start.38
  350.2 3.2 collective-permute-done.38
  353.4 11.1 %shard_map.118 = (f32[512,1792]{1,0:T(8,128)}, f32[512,1792]{1,0:T(8,128)}) custom-call(f32[8,128]{1,0:T(8,128)S(1)} %add.82.table_ref, f32[8,128]{1,0:T(8,128)S(1)} %broadcast_multiply_fusion.factors_ref, f32[1,128]{1,0:T(1,128)S(1)} %compare_select_fusion.3.factor_ref, s32[9]{0:T(128)S(1)} %pad_add_fusion.refs_0_.slots_ref, ...), custom_call_target="tpu_custom_call" | custom-call | tf_op jit(solution)/shard_map/pallas_call | solution.py:369
  (129 shorter events, 15.8 us)
Async XLA Ops:
  0.6 3.0 copy-start.25
  0.6 3.3 copy-start.30
  3.2 6.6 %collective-permute-start.2 = (bf16[128,1792]{1,0:T(8,128)(2,1)}, bf16[128,1792]{1,0:T(8,128)(2,1)S(1)}, u32[]{:S(2)}, u32[]{:S(2)}) collective-permute-start(bf16[128,1792]{1,0:T(8,128)(2,1)} %get-tuple-element.121), channel_id=1, source_target_pairs={{0,1},{1,0},{2,3},{3,2},{4,5},{5,4},{6,7},{7,6},{8,9},{9,8},{10,11... | collective-permute-start | bytes 1376264 | tf_op jit(solution)/shard_map/ppermute | solution.py:220
  4.3 28.7 %collective-permute-start = (bf16[128,4096]{1,0:T(8,128)(2,1)S(1)}, bf16[128,4096]{1,0:T(8,128)(2,1)}, u32[]{:S(2)}, u32[]{:S(2)}) collective-permute-start(bf16[128,4096]{1,0:T(8,128)(2,1)S(1)} %fusion.2.refs_1_), channel_id=1, source_target_pairs={{0,4},{4,12},{8,0},{12,20},{16,8},{20,28},{24,16},{28,24},{1,5},{5... | collective-permute-start | bytes 3145736 | tf_op jit(solution)/shard_map/ppermute | solution.py:217
  6.8 26.1 %collective-permute-start.1 = (bf16[128,4096]{1,0:T(8,128)(2,1)S(1)}, bf16[128,4096]{1,0:T(8,128)(2,1)}, u32[]{:S(2)}, u32[]{:S(2)}) collective-permute-start(bf16[128,4096]{1,0:T(8,128)(2,1)S(1)} %fusion.2.refs_1_), channel_id=1, source_target_pairs={{0,8},{4,0},{8,16},{12,4},{16,24},{20,12},{24,28},{28,20},{1,9},{5... | collective-permute-start | bytes 3145736 | tf_op jit(solution)/shard_map/ppermute | solution.py:217
  7.0 13.7 %collective-permute-start.3 = (bf16[128,1792]{1,0:T(8,128)(2,1)}, bf16[128,1792]{1,0:T(8,128)(2,1)}, u32[]{:S(2)}, u32[]{:S(2)}) collective-permute-start(bf16[128,1792]{1,0:T(8,128)(2,1)} %get-tuple-element.122), channel_id=1, source_target_pairs={{0,2},{1,3},{2,0},{3,1},{4,6},{5,7},{6,4},{7,5},{8,10},{9,11},{10,... | collective-permute-start | bytes 1376264 | tf_op jit(solution)/shard_map/ppermute | solution.py:220
  8.8 20.2 %collective-permute-start.4 = (bf16[128,1792]{1,0:T(8,128)(2,1)}, bf16[128,1792]{1,0:T(8,128)(2,1)}, u32[]{:S(2)}, u32[]{:S(2)}) collective-permute-start(bf16[128,1792]{1,0:T(8,128)(2,1)} %get-tuple-element.120), channel_id=1, source_target_pairs={{0,3},{1,2},{2,1},{3,0},{4,7},{5,6},{6,5},{7,4},{8,11},{9,10},{10,... | collective-permute-start | bytes 1376264 | tf_op jit(solution)/shard_map/ppermute | solution.py:220
  32.9 27.6 %copy-start.13 = (bf16[512,1792]{1,0:T(8,128)(2,1)}, bf16[512,1792]{1,0:T(8,128)(2,1)S(1)}, u32[]{:S(2)}) copy-start(bf16[512,1792]{1,0:T(8,128)(2,1)S(1)} %slice_dynamic-update-slice_fusion.refs_7_) | copy-start | bytes 5505028
  32.9 32.8 %copy-start.34 = (s32[8]{0:T(128)S(1)}, s32[8]{0:T(128)}, u32[]{:S(2)}) copy-start(s32[8]{0:T(128)} %constant.61.clone) | copy-start | bytes 100
  32.9 35.5 %copy-start.33 = (s32[8]{0:T(128)S(1)}, s32[8]{0:T(128)}, u32[]{:S(2)}) copy-start(s32[8]{0:T(128)} %constant.65) | copy-start | bytes 100
  32.9 36.2 %copy-start.24 = (s32[8]{0:T(128)S(1)}, s32[8]{0:T(128)}, u32[]{:S(2)}) copy-start(s32[8]{0:T(128)} %constant.60.clone) | copy-start | bytes 100
  33.0 26.1 %collective-permute-start.5 = (bf16[128,4096]{1,0:T(8,128)(2,1)}, bf16[128,4096]{1,0:T(8,128)(2,1)S(1)}, u32[]{:S(2)}, u32[]{:S(2)}) collective-permute-start(bf16[128,4096]{1,0:T(8,128)(2,1)} %collective-permute-done), channel_id=1, source_target_pairs={{0,4},{4,12},{8,0},{12,20},{16,8},{20,28},{24,16},{28,24},{1,5},{5... | collective-permute-start | bytes 3145736 | tf_op jit(solution)/shard_map/ppermute | solution.py:217
  34.4 26.1 %collective-permute-start.6 = (bf16[128,4096]{1,0:T(8,128)(2,1)}, bf16[128,4096]{1,0:T(8,128)(2,1)S(1)}, u32[]{:S(2)}, u32[]{:S(2)}) collective-permute-start(bf16[128,4096]{1,0:T(8,128)(2,1)} %collective-permute-done.1), channel_id=1, source_target_pairs={{0,8},{4,0},{8,16},{12,4},{16,24},{20,12},{24,28},{28,20},{1,9},{5... | collective-permute-start | bytes 3145736 | tf_op jit(solution)/shard_map/ppermute | solution.py:217
  35.1 25.4 %collective-permute-start.7 = (bf16[128,4096]{1,0:T(8,128)(2,1)S(1)}, bf16[128,4096]{1,0:T(8,128)(2,1)}, u32[]{:S(2)}, u32[]{:S(2)}) collective-permute-start(bf16[128,4096]{1,0:T(8,128)(2,1)S(1)} %fusion.2.refs_1_), channel_id=1, source_target_pairs={{0,2},{1,3},{2,0},{3,1},{4,6},{5,7},{6,4},{7,5},{8,10},{9,11},{10,... | collective-permute-start | bytes 3145736 | tf_op jit(solution)/shard_map/ppermute | solution.py:220
  60.5 9.4 %collective-permute-start.11 = (bf16[128,4096]{1,0:T(8,128)(2,1)S(1)}, bf16[128,4096]{1,0:T(8,128)(2,1)}, u32[]{:S(2)}, u32[]{:S(2)}) collective-permute-start(bf16[128,4096]{1,0:T(8,128)(2,1)S(1)} %fusion.2.refs_1_), channel_id=1, source_target_pairs={{0,1},{1,0},{2,3},{3,2},{4,5},{5,4},{6,7},{7,6},{8,9},{9,8},{10,11... | collective-permute-start | bytes 3145736 | tf_op jit(solution)/shard_map/ppermute | solution.py:220
  61.4 8.4 %collective-permute-start.12 = (bf16[128,4096]{1,0:T(8,128)(2,1)}, bf16[128,4096]{1,0:T(8,128)(2,1)}, u32[]{:S(2)}, u32[]{:S(2)}) collective-permute-start(bf16[128,4096]{1,0:T(8,128)(2,1)} %collective-permute-done.7.refs_3_), channel_id=1, source_target_pairs={{0,1},{1,0},{2,3},{3,2},{4,5},{5,4},{6,7},{7,6},{8,9},{9,8},{10,11... | collective-permute-start | bytes 3145736 | tf_op jit(solution)/shard_map/ppermute | solution.py:220
  64.1 48.2 %copy-start.9 = (bf16[256,4096]{1,0:T(8,128)(2,1)}, bf16[256,4096]{1,0:T(8,128)(2,1)S(1)}, u32[]{:S(2)}) copy-start(bf16[256,4096]{1,0:T(8,128)(2,1)S(1)} %constant_dynamic-update-slice_fusion.refs_1_) | copy-start | bytes 6291460
  64.1 48.1 %collective-permute-start.10 = (bf16[256,4096]{1,0:T(8,128)(2,1)S(1)}, bf16[256,4096]{1,0:T(8,128)(2,1)}, u32[]{:S(2)}, u32[]{:S(2)}) collective-permute-start(bf16[256,4096]{1,0:T(8,128)(2,1)S(1)} %constant_dynamic-update-slice_fusion.refs_1_), channel_id=1, source_target_pairs={{0,2},{1,3},{2,0},{3,1},{4,6},{5,7},{6,4},{7,5},{8,10},{9,11},{10,... | collective-permute-start | bytes 6291464 | tf_op jit(solution)/shard_map/ppermute | solution.py:220
  66.4 42.4 %collective-permute-start.8 = (bf16[512,1792]{1,0:T(8,128)(2,1)}, bf16[512,1792]{1,0:T(8,128)(2,1)}, u32[]{:S(2)}, u32[]{:S(2)}) collective-permute-start(bf16[512,1792]{1,0:T(8,128)(2,1)} %copy-done.13), channel_id=1, source_target_pairs={{0,4},{4,12},{8,0},{12,20},{16,8},{20,28},{24,16},{28,24},{1,5},{5... | collective-permute-start | bytes 5505032 | tf_op jit(solution)/shard_map/ppermute | solution.py:217
  68.0 42.1 %collective-permute-start.9 = (bf16[512,1792]{1,0:T(8,128)(2,1)}, bf16[512,1792]{1,0:T(8,128)(2,1)}, u32[]{:S(2)}, u32[]{:S(2)}) collective-permute-start(bf16[512,1792]{1,0:T(8,128)(2,1)} %copy-done.13), channel_id=1, source_target_pairs={{0,8},{4,0},{8,16},{12,4},{16,24},{20,12},{24,28},{28,20},{1,9},{5... | collective-permute-start | bytes 5505032 | tf_op jit(solution)/shard_map/ppermute | solution.py:217
  71.4 5.2 %copy-start.15 = (bf16[4096,1792]{1,0:T(8,128)(2,1)S(1)}, bf16[4096,1792]{1,0:T(8,128)(2,1)}, u32[]{:S(2)}) copy-start(bf16[4096,1792]{1,0:T(8,128)(2,1)} %refs_5_.9) | copy-start | bytes 44040196
  76.6 36.2 %copy-start.27 = (bf16[128,4096]{1,0:T(8,128)(2,1)S(1)}, bf16[128,4096]{1,0:T(8,128)(2,1)}, u32[]{:S(2)}) copy-start(bf16[128,4096]{1,0:T(8,128)(2,1)} %copy-done.26) | copy-start | bytes 3145732
  76.6 37.8 %copy-start.29 = (bf16[128,4096]{1,0:T(8,128)(2,1)S(1)}, bf16[128,4096]{1,0:T(8,128)(2,1)}, u32[]{:S(2)}) copy-start(bf16[128,4096]{1,0:T(8,128)(2,1)} %copy-done.28) | copy-start | bytes 3145732
  112.3 6.4 %collective-permute-start.18 = (bf16[256,4096]{1,0:T(8,128)(2,1)S(1)}, bf16[256,4096]{1,0:T(8,128)(2,1)S(1)}, u32[]{:S(2)}, u32[]{:S(2)}) collective-permute-start(bf16[256,4096]{1,0:T(8,128)(2,1)S(1)} %constant_dynamic-update-slice_fusion.refs_1_), channel_id=1, source_target_pairs={{0,1},{1,0},{2,3},{3,2},{4,5},{5,4},{6,7},{7,6},{8,9},{9,8},{10,11... | collective-permute-start | bytes 6291464 | tf_op jit(solution)/shard_map/ppermute | solution.py:220
  112.3 9.0 %copy-start.10 = (bf16[256,4096]{1,0:T(8,128)(2,1)S(1)}, bf16[256,4096]{1,0:T(8,128)(2,1)}, u32[]{:S(2)}) copy-start(bf16[256,4096]{1,0:T(8,128)(2,1)} %copy-done.9) | copy-start | bytes 6291460
  112.3 8.0 %collective-permute-start.19 = (bf16[256,4096]{1,0:T(8,128)(2,1)}, bf16[256,4096]{1,0:T(8,128)(2,1)S(1)}, u32[]{:S(2)}, u32[]{:S(2)}) collective-permute-start(bf16[256,4096]{1,0:T(8,128)(2,1)} %collective-permute-done.10.refs_3_), channel_id=1, source_target_pairs={{0,1},{1,0},{2,3},{3,2},{4,5},{5,4},{6,7},{7,6},{8,9},{9,8},{10,11... | collective-permute-start | bytes 6291464 | tf_op jit(solution)/shard_map/ppermute | solution.py:220
  112.8 51.2 %collective-permute-start.13 = (bf16[128,4096]{1,0:T(8,128)(2,1)S(1)}, bf16[128,4096]{1,0:T(8,128)(2,1)S(1)}, u32[]{:S(2)}, u32[]{:S(2)}) collective-permute-start(bf16[128,4096]{1,0:T(8,128)(2,1)S(1)} %copy-done.27), channel_id=1, source_target_pairs={{0,4},{4,12},{8,0},{12,20},{16,8},{20,28},{24,16},{28,24},{1,5},{5... | collective-permute-start | bytes 3145736 | tf_op jit(solution)/shard_map/ppermute | solution.py:217
  114.4 49.6 %collective-permute-start.14 = (bf16[128,4096]{1,0:T(8,128)(2,1)S(1)}, bf16[128,4096]{1,0:T(8,128)(2,1)S(1)}, u32[]{:S(2)}, u32[]{:S(2)}) collective-permute-start(bf16[128,4096]{1,0:T(8,128)(2,1)S(1)} %copy-done.29), channel_id=1, source_target_pairs={{0,8},{4,0},{8,16},{12,4},{16,24},{20,12},{24,28},{28,20},{1,9},{5... | collective-permute-start | bytes 3145736 | tf_op jit(solution)/shard_map/ppermute | solution.py:217
  115.0 63.6 %collective-permute-start.17 = (bf16[256,4096]{1,0:T(8,128)(2,1)S(1)}, bf16[256,4096]{1,0:T(8,128)(2,1)S(1)}, u32[]{:S(2)}, u32[]{:S(2)}) collective-permute-start(bf16[256,4096]{1,0:T(8,128)(2,1)S(1)} %constant_dynamic-update-slice_fusion.2.refs_1_), channel_id=1, source_target_pairs={{0,2},{1,3},{2,0},{3,1},{4,6},{5,7},{6,4},{7,5},{8,10},{9,11},{10,... | collective-permute-start | bytes 6291464 | tf_op jit(solution)/shard_map/ppermute | solution.py:220
  118.7 58.6 %collective-permute-start.15 = (bf16[512,1792]{1,0:T(8,128)(2,1)}, bf16[512,1792]{1,0:T(8,128)(2,1)}, u32[]{:S(2)}, u32[]{:S(2)}) collective-permute-start(bf16[512,1792]{1,0:T(8,128)(2,1)} %collective-permute-done.8.refs_8_), channel_id=1, source_target_pairs={{0,4},{4,12},{8,0},{12,20},{16,8},{20,28},{24,16},{28,24},{1,5},{5... | collective-permute-start | bytes 5505032 | tf_op jit(solution)/shard_map/ppermute | solution.py:217
  120.3 58.4 %collective-permute-start.16 = (bf16[512,1792]{1,0:T(8,128)(2,1)}, bf16[512,1792]{1,0:T(8,128)(2,1)}, u32[]{:S(2)}, u32[]{:S(2)}) collective-permute-start(bf16[512,1792]{1,0:T(8,128)(2,1)} %collective-permute-done.9.refs_7_), channel_id=1, source_target_pairs={{0,8},{4,0},{8,16},{12,4},{16,24},{20,12},{24,28},{28,20},{1,9},{5... | collective-permute-start | bytes 5505032 | tf_op jit(solution)/shard_map/ppermute | solution.py:217
  178.7 1.6 copy-start.16
  178.7 5.3 %collective-permute-start.25 = (bf16[256,4096]{1,0:T(8,128)(2,1)S(1)}, bf16[256,4096]{1,0:T(8,128)(2,1)S(1)}, u32[]{:S(2)}, u32[]{:S(2)}) collective-permute-start(bf16[256,4096]{1,0:T(8,128)(2,1)S(1)} %constant_dynamic-update-slice_fusion.2.refs_1_), channel_id=1, source_target_pairs={{0,1},{1,0},{2,3},{3,2},{4,5},{5,4},{6,7},{7,6},{8,9},{9,8},{10,11... | collective-permute-start | bytes 6291464 | tf_op jit(solution)/shard_map/ppermute | solution.py:220
  178.7 8.2 %collective-permute-start.26 = (bf16[256,4096]{1,0:T(8,128)(2,1)S(1)}, bf16[256,4096]{1,0:T(8,128)(2,1)S(1)}, u32[]{:S(2)}, u32[]{:S(2)}) collective-permute-start(bf16[256,4096]{1,0:T(8,128)(2,1)S(1)} %collective-permute-done.17.refs_3_), channel_id=1, source_target_pairs={{0,1},{1,0},{2,3},{3,2},{4,5},{5,4},{6,7},{7,6},{8,9},{9,8},{10,11... | collective-permute-start | bytes 6291464 | tf_op jit(solution)/shard_map/ppermute | solution.py:220
  180.4 56.3 %collective-permute-start.24 = (bf16[256,4096]{1,0:T(8,128)(2,1)S(1)}, bf16[256,4096]{1,0:T(8,128)(2,1)}, u32[]{:S(2)}, u32[]{:S(2)}) collective-permute-start(bf16[256,4096]{1,0:T(8,128)(2,1)S(1)} %constant_dynamic-update-slice_fusion.4.refs_1_), channel_id=1, source_target_pairs={{0,2},{1,3},{2,0},{3,1},{4,6},{5,7},{6,4},{7,5},{8,10},{9,11},{10,... | collective-permute-start | bytes 6291464 | tf_op jit(solution)/shard_map/ppermute | solution.py:220
  182.0 54.7 %collective-permute-start.22 = (bf16[512,1792]{1,0:T(8,128)(2,1)}, bf16[512,1792]{1,0:T(8,128)(2,1)S(1)}, u32[]{:S(2)}, u32[]{:S(2)}) collective-permute-start(bf16[512,1792]{1,0:T(8,128)(2,1)} %collective-permute-done.15.refs_8_), channel_id=1, source_target_pairs={{0,4},{4,12},{8,0},{12,20},{16,8},{20,28},{24,16},{28,24},{1,5},{5... | collective-permute-start | bytes 5505032 | tf_op jit(solution)/shard_map/ppermute | solution.py:217
  183.5 53.1 %collective-permute-start.23 = (bf16[512,1792]{1,0:T(8,128)(2,1)}, bf16[512,1792]{1,0:T(8,128)(2,1)S(1)}, u32[]{:S(2)}, u32[]{:S(2)}) collective-permute-start(bf16[512,1792]{1,0:T(8,128)(2,1)} %collective-permute-done.16.refs_7_), channel_id=1, source_target_pairs={{0,8},{4,0},{8,16},{12,4},{16,24},{20,12},{24,28},{28,20},{1,9},{5... | collective-permute-start | bytes 5505032 | tf_op jit(solution)/shard_map/ppermute | solution.py:217
  185.3 51.3 %collective-permute-start.20 = (bf16[64,4096]{1,0:T(8,128)(2,1)}, bf16[64,4096]{1,0:T(8,128)(2,1)S(1)}, u32[]{:S(2)}, u32[]{:S(2)}) collective-permute-start(bf16[64,4096]{1,0:T(8,128)(2,1)} %slice.58), channel_id=1, source_target_pairs={{0,4},{4,12},{8,0},{12,20},{16,8},{20,28},{24,16},{28,24},{1,5},{5... | collective-permute-start | bytes 1572872 | tf_op jit(solution)/shard_map/ppermute | solution.py:217
  188.2 48.4 %collective-permute-start.21 = (bf16[64,4096]{1,0:T(8,128)(2,1)S(1)}, bf16[64,4096]{1,0:T(8,128)(2,1)}, u32[]{:S(2)}, u32[]{:S(2)}) collective-permute-start(bf16[64,4096]{1,0:T(8,128)(2,1)S(1)} %slice.59), channel_id=1, source_target_pairs={{0,8},{4,0},{8,16},{12,4},{16,24},{20,12},{24,28},{28,20},{1,9},{5... | collective-permute-start | bytes 1572872 | tf_op jit(solution)/shard_map/ppermute | solution.py:217
  188.8 1.6 copy-start.17
  234.8 1.8 copy-start.2
  236.6 4.5 %copy-start = (bf16[2,512,1792]{2,1,0:T(8,128)(2,1)}, bf16[2,512,1792]{2,1,0:T(8,128)(2,1)S(1)}, u32[]{:S(2)}) copy-start(bf16[2,512,1792]{2,1,0:T(8,128)(2,1)S(1)} %get-tuple-element.114.refs_12_.refs_3_) | copy-start | bytes 11010052
  236.6 6.4 %collective-permute-start.30 = (bf16[256,4096]{1,0:T(8,128)(2,1)S(1)}, bf16[256,4096]{1,0:T(8,128)(2,1)S(1)}, u32[]{:S(2)}, u32[]{:S(2)}) collective-permute-start(bf16[256,4096]{1,0:T(8,128)(2,1)S(1)} %constant_dynamic-update-slice_fusion.4.refs_1_), channel_id=1, source_target_pairs={{0,1},{1,0},{2,3},{3,2},{4,5},{5,4},{6,7},{7,6},{8,9},{9,8},{10,11... | collective-permute-start | bytes 6291464 | tf_op jit(solution)/shard_map/ppermute | solution.py:220
  236.7 7.4 %collective-permute-start.31 = (bf16[256,4096]{1,0:T(8,128)(2,1)}, bf16[256,4096]{1,0:T(8,128)(2,1)S(1)}, u32[]{:S(2)}, u32[]{:S(2)}) collective-permute-start(bf16[256,4096]{1,0:T(8,128)(2,1)} %collective-permute-done.24.refs_3_), channel_id=1, source_target_pairs={{0,1},{1,0},{2,3},{3,2},{4,5},{5,4},{6,7},{7,6},{8,9},{9,8},{10,11... | collective-permute-start | bytes 6291464 | tf_op jit(solution)/shard_map/ppermute | solution.py:220
  238.7 52.5 %copy-start.11 = (bf16[128,4096]{1,0:T(8,128)(2,1)}, bf16[128,4096]{1,0:T(8,128)(2,1)S(1)}, u32[]{:S(2)}) copy-start(bf16[128,4096]{1,0:T(8,128)(2,1)S(1)} %constant_dynamic-update-slice_fusion.6.refs_1_) | copy-start | bytes 3145732
  238.7 52.4 %collective-permute-start.29 = (bf16[128,4096]{1,0:T(8,128)(2,1)S(1)}, bf16[128,4096]{1,0:T(8,128)(2,1)S(1)}, u32[]{:S(2)}, u32[]{:S(2)}) collective-permute-start(bf16[128,4096]{1,0:T(8,128)(2,1)S(1)} %constant_dynamic-update-slice_fusion.6.refs_1_), channel_id=1, source_target_pairs={{0,2},{1,3},{2,0},{3,1},{4,6},{5,7},{6,4},{7,5},{8,10},{9,11},{10,... | collective-permute-start | bytes 3145736 | tf_op jit(solution)/shard_map/ppermute | solution.py:220
  239.4 50.9 %collective-permute-start.27 = (bf16[256,1792]{1,0:T(8,128)(2,1)S(1)}, bf16[256,1792]{1,0:T(8,128)(2,1)S(1)}, u32[]{:S(2)}, u32[]{:S(2)}) collective-permute-start(bf16[256,1792]{1,0:T(8,128)(2,1)S(1)} %slice.60), channel_id=1, source_target_pairs={{0,4},{4,12},{8,0},{12,20},{16,8},{20,28},{24,16},{28,24},{1,5},{5... | collective-permute-start | bytes 2752520 | tf_op jit(solution)/shard_map/ppermute | solution.py:217
  241.1 49.2 %collective-permute-start.28 = (bf16[256,1792]{1,0:T(8,128)(2,1)S(1)}, bf16[256,1792]{1,0:T(8,128)(2,1)S(1)}, u32[]{:S(2)}, u32[]{:S(2)}) collective-permute-start(bf16[256,1792]{1,0:T(8,128)(2,1)S(1)} %slice.61), channel_id=1, source_target_pairs={{0,8},{4,0},{8,16},{12,4},{16,24},{20,12},{24,28},{28,20},{1,9},{5... | collective-permute-start | bytes 2752520 | tf_op jit(solution)/shard_map/ppermute | solution.py:217
  286.6 1.8 copy-start.4
  288.4 1.8 copy-start.6
  291.2 45.8 %copy-start.31 = (f32[3]{0:T(128)S(1)}, f32[3]{0:T(128)}, u32[]{:S(2)}) copy-start(f32[3]{0:T(128)} %param.16) | copy-start | bytes 40
  291.2 47.3 %copy-start.32 = (s32[8]{0:T(128)S(1)}, s32[8]{0:T(128)}, u32[]{:S(2)}) copy-start(s32[8]{0:T(128)} %param.15) | copy-start | bytes 100
  291.2 2.7 collective-permute-start.32
  291.4 4.0 %collective-permute-start.33 = (bf16[128,4096]{1,0:T(8,128)(2,1)S(1)}, bf16[128,4096]{1,0:T(8,128)(2,1)S(1)}, u32[]{:S(2)}, u32[]{:S(2)}) collective-permute-start(bf16[128,4096]{1,0:T(8,128)(2,1)S(1)} %collective-permute-done.29.refs_3_), channel_id=1, source_target_pairs={{0,1},{1,0},{2,3},{3,2},{4,5},{5,4},{6,7},{7,6},{8,9},{9,8},{10,11... | collective-permute-start | bytes 3145736 | tf_op jit(solution)/shard_map/ppermute | solution.py:220
  295.4 2.0 copy-start.1
  299.9 53.5 %copy-start.3 = (bf16[2,512,1792]{2,1,0:T(8,128)(2,1)S(1)}, bf16[2,512,1792]{2,1,0:T(8,128)(2,1)}, u32[]{:S(2)}) copy-start(bf16[2,512,1792]{2,1,0:T(8,128)(2,1)} %copy-done.2) | copy-start | bytes 11010052
  299.9 53.5 %copy-start.5 = (bf16[2,512,1792]{2,1,0:T(8,128)(2,1)S(1)}, bf16[2,512,1792]{2,1,0:T(8,128)(2,1)}, u32[]{:S(2)}) copy-start(bf16[2,512,1792]{2,1,0:T(8,128)(2,1)} %copy-done.4) | copy-start | bytes 11010052
  299.9 53.5 %copy-start.7 = (bf16[2,512,1792]{2,1,0:T(8,128)(2,1)S(1)}, bf16[2,512,1792]{2,1,0:T(8,128)(2,1)}, u32[]{:S(2)}) copy-start(bf16[2,512,1792]{2,1,0:T(8,128)(2,1)} %copy-done.6) | copy-start | bytes 11010052
  335.0 1.8 copy-start.8
  336.8 1.2 collective-permute-start.34
  338.0 3.6 collective-permute-start.35
  341.6 3.6 collective-permute-start.36
  345.2 3.6 collective-permute-start.37
  348.9 4.5 %collective-permute-start.38 = (f32[8,128]{1,0:T(8,128)S(1)}, f32[8,128]{1,0:T(8,128)S(1)}, u32[]{:S(2)}, u32[]{:S(2)}) collective-permute-start(f32[8,128]{1,0:T(8,128)S(1)} %add.81), channel_id=1, source_target_pairs={{0,16},{1,17},{2,18},{3,19},{4,20},{5,21},{6,22},{7,23},{8,24},{9,... | collective-permute-start | bytes 12296 | tf_op jit(solution)/shard_map/ppermute | solution.py:363
  (10 other events, 13.1 us)

commit v3 on v2

--- a/solution.py
+++ b/solution.py
@@ -12,6 +12,7 @@
 LINE = 4
 AXES = ("colony", "fsdp")
 VMEM = 28 * 1024 * 1024
+VMEM_FIRST = 50 * 1024 * 1024
 
 
 def ring_order(count):
@@ -258,7 +259,7 @@
     factors = factor[: table_shape[0], None] * factor[None, :]
 
     smem = pl.BlockSpec(memory_space=pltpu.SMEM)
-    anywhere = pl.BlockSpec(memory_space=pl.ANY)
+    main = pl.BlockSpec(memory_space=pltpu.HBM)
     column = pl.BlockSpec((depth, block), lambda b: (0, b))
     block_of_grad = pl.BlockSpec((2, rows, block), lambda b: (0, 0, b))
 
@@ -278,7 +279,7 @@
             ]
         n_cot = n_pieces + 1
         last = group[-1] == count - 1
-        in_specs = [smem] + [anywhere] * shards + [column, column]
+        in_specs = [smem] + [main] * shards + [column, column]
         in_specs += [pl.BlockSpec((c.shape[0], block), lambda b: (0, b)) for c in sum(cots, [])]
         out_shape = [jax.ShapeDtypeStruct((2, rows, width), jnp.bfloat16)] * len(group)
         out_specs = [block_of_grad] * len(group)
@@ -287,7 +288,10 @@
             pltpu.VMEM((len(group), rows, total_tokens), jnp.bfloat16),
             pltpu.SemaphoreType.DMA((len(group), 2 * shards)),
         ]
-        operands = [slots, *tokens, gate_weight, up_weight, *sum(cots, [])]
+        held = functools.partial(pltpu.with_memory_space_constraint, memory_space=pltpu.HBM)
+        tokens = [held(piece) for piece in tokens]
+        cots = [[held(piece) for piece in pieces] for pieces in cots]
+        operands = [slots, *tokens, held(gate_weight), held(up_weight), *sum(cots, [])]
         if last:
             in_specs += [block_of_grad] * len(before)
             operands += before
@@ -302,7 +306,9 @@
             out_specs=out_specs,
             out_shape=out_shape,
             scratch_shapes=scratch,
-            compiler_params=pltpu.CompilerParams(vmem_limit_bytes=VMEM),
+            compiler_params=pltpu.CompilerParams(
+                vmem_limit_bytes=VMEM if group[0] else VMEM_FIRST
+            ),
             cost_estimate=pl.CostEstimate(
                 flops=flops, bytes_accessed=4 * depth * width, transcendentals=total_tokens * width
             ),
@@ -331,20 +337,27 @@
         return jnp.concatenate([n_at[step, way] for way in ways], axis=0)
 
     def fence():
-        nonlocal n_at, c_at, chips, grads
-        n_at, c_at, chips, grads = lax.optimization_barrier((n_at, c_at, chips, grads))
-
-    grads, chips = [], {0: normed}
+        nonlocal n_at, c_at, chips, grads, joined
+        n_at, c_at, chips, grads, joined = lax.optimization_barrier(
+            (n_at, c_at, chips, grads, joined)
+        )
+
+    grads, chips, joined = [], {0: normed}, {}
     send_tokens(1)
     fence()
     chips[0] = spread_chips(chips[0])
     send_tokens(2)
+    joined[1] = both(1)
     fence()
     for step in range(far + 1):
         cores = spread_cores(chips[step])
         if step + 1 <= far:
             send_cot(step + 1)
-            chips[step + 1] = spread_chips(both(step + 1))
+            if step + 1 not in joined:
+                joined[step + 1] = both(step + 1)
+            chips[step + 1] = spread_chips(joined.pop(step + 1))
+        if step == 0:
+            joined[2] = both(2)
         if 0 < step <= far - 2:
             send_tokens(step + 2)
         if step == 0:

time: 371 us -> 364 us (0.981)
  local copies, waits for them, and re-layouts: 42.8 us -> 13.6 us
  waiting for transfers between devices: 88.1 us -> 99.5 us
  Pallas kernels: 197 us -> 204 us
  other arithmetic: 1.59 us -> 6.3 us
    unnamed x81 -> x71, local copies, waits for them, and re-layouts: 35.4 us -> 9.53 us
    ppermute x16, waiting for transfers between devices: 47.9 us -> 55 us  [hop(): return lax.ppermute(value, 'colony', pairs)]
    pallas_call x5, Pallas kernels: 186 us -> 193 us  [colonies(): pl.pallas_call(functools.partial(colony_kernel, group, count, parts, shar...]
    concatenate x0 -> x2, other arithmetic: none -> 4.78 us  [both(): return jnp.concatenate([n_at[step, way] for way in ways], axis=0)]
  transfers between devices with their start and end apart: 39 -> 39, of which waited for: 19 -> 24; matrix products, arithmetic and copies ran while one was open for 4% -> 3% of each run, Pallas kernels for 41% -> 43%
where the time goes in v3:
time: 364 us; the launch traced here: 359 us
  Pallas kernels  204 us (56%)
  waiting for transfers between devices  99.5 us (27%)
  starting transfers between devices  34.2 us (9%)
  local copies, waits for them, and re-layouts  13.6 us (4%)
  other arithmetic  6.3 us (2%)
    pallas_call x5, Pallas kernels, colonies(): pl.pallas_call(functools.partial(colony_kernel, group, count, parts, shar...  193 us
    ppermute x16, waiting for transfers between devices, hop(): return lax.ppermute(value, 'colony', pairs)  55 us
    ppermute x18, waiting for transfers between devices, swap(): return lax.ppermute(value, 'fsdp', [(j, j ^ mask) for j in range(shards)])  32.2 us
    ppermute x16, starting transfers between devices, hop(): return lax.ppermute(value, 'colony', pairs)  18.4 us
    ppermute x5, waiting for transfers between devices, on_device(): lax.ppermute(table, AXES, [(d, d ^ bit) for d in range(devices)])  12.3 us
    ppermute x18, starting transfers between devices, swap(): return lax.ppermute(value, 'fsdp', [(j, j ^ mask) for j in range(shards)])  11.8 us
    pallas_call x1, Pallas kernels, on_device(): pl.pallas_call(functools.partial(combine_kernel, count), grid=(rows // cu...  11.1 us
    unnamed x71, local copies, waits for them, and re-layouts  9.53 us
  transfers between devices with their start and end apart: 39, of which 24 were waited for; matrix products, arithmetic and copies ran while one was open for 3% of the time, Pallas kernels for 43%

profile of v3, /device:TPU:0, one launch (start us, length us, event | category | flops | bytes accessed | tf_op | source)
XLA Modules:
  0.0 358.7 jit_solution(2556943479113559717)
XLA Ops:
  0.7 2.5 dynamic-slice_bitcast_fusion
  4.3 2.6 collective-permute-start
  7.0 1.9 collective-permute-start.3
  8.8 1.0 fusion.4
  9.8 10.7 %collective-permute-done.3 = bf16[128,1792]{1,0:T(8,128)(2,1)S(1)} collective-permute-done((bf16[128,1792]{1,0:T(8,128)(2,1)}, bf16[128,1792]{1,0:T(8,128)(2,1)S(1)}, u32[]{:S(2)}, u32[]{:S(2)}) %collective-permute-start.3) | collective-permute-done | bytes 458784 | tf_op jit(solution)/shard_map/ppermute | solution.py:221
  20.5 8.4 %collective-permute-done.4 = bf16[128,1792]{1,0:T(8,128)(2,1)S(1)} collective-permute-done((bf16[128,1792]{1,0:T(8,128)(2,1)}, bf16[128,1792]{1,0:T(8,128)(2,1)S(1)}, u32[]{:S(2)}, u32[]{:S(2)}) %collective-permute-start.4) | collective-permute-done | bytes 458784 | tf_op jit(solution)/shard_map/ppermute | solution.py:221
  29.0 1.0 fusion.3
  30.1 0.8 collective-permute-done
  30.8 1.4 collective-permute-done.1
  32.2 1.6 collective-permute-start.5
  34.3 1.5 collective-permute-start.7
  35.8 1.7 pad_maximum_fusion.refs_1_
  37.4 19.6 %collective-permute-done.5 = bf16[128,4096]{1,0:T(8,128)(2,1)} collective-permute-done((bf16[128,4096]{1,0:T(8,128)(2,1)}, bf16[128,4096]{1,0:T(8,128)(2,1)}, u32[]{:S(2)}, u32[]{:S(2)}) %collective-permute-start.5) | collective-permute-done | bytes 1048608 | tf_op jit(solution)/shard_map/ppermute | solution.py:218
  57.0 1.3 collective-permute-done.6
  58.3 0.5 collective-permute-start.12
  58.8 0.6 dynamic_slice.21
  59.4 0.6 compare_select_fusion
  60.1 0.6 gather_fusion
  60.8 1.6 collective-permute-start.10
  62.4 1.6 collective-permute-start.8
  64.4 3.1 pad_maximum_fusion.1.refs_1_
  67.5 24.8 %shard_map.113.refs_9_.refs_0_ = bf16[2,512,1792]{2,1,0:T(8,128)(2,1)S(1)} custom-call(s32[9]{0:T(128)S(1)} %pad_add_fusion.refs_0_.slots_ref, bf16[128,4096]{1,0:T(8,128)(2,1)} %copy-done.6, bf16[128,4096]{1,0:T(8,128)(2,1)} %collective-permute-done.11.refs_2_, bf16[128,4096]{1,0:T(8,128)(2,1)} %collective-permute-done.7.refs_3_, ...), custom_call_target="tpu_custom_call" | custom-call | flops 16911433728 | bytes 29360128 | tf_op jit(solution)/shard_map/pallas_call | solution.py:302
  92.3 12.0 %collective-permute-done.8.refs_8_ = bf16[512,1792]{1,0:T(8,128)(2,1)S(1)} collective-permute-done((bf16[512,1792]{1,0:T(8,128)(2,1)}, bf16[512,1792]{1,0:T(8,128)(2,1)S(1)}, u32[]{:S(2)}, u32[]{:S(2)}) %collective-permute-start.8) | collective-permute-done | bytes 1835040 | tf_op jit(solution)/shard_map/ppermute | solution.py:218
  104.3 1.3 collective-permute-done.9.refs_7_
  105.6 2.8 collective-permute-done.10.refs_3_
  109.0 1.5 collective-permute-start.17
  110.5 1.6 collective-permute-start.15
  112.7 1.6 collective-permute-start.13
  114.2 1.4 collective-permute-done.19.refs_4_
  115.7 1.5 collective-permute-start.14
  117.2 43.4 %shard_map.114 = (bf16[2,512,1792]{2,1,0:T(8,128)(2,1)S(1)}, bf16[2,512,1792]{2,1,0:T(8,128)(2,1)S(1)}) custom-call(s32[9]{0:T(128)S(1)} %pad_add_fusion.refs_0_.slots_ref, bf16[256,4096]{1,0:T(8,128)(2,1)} %copy-done.5, bf16[256,4096]{1,0:T(8,128)(2,1)} %copy-done.19, bf16[256,4096]{1,0:T(8,128)(2,1)} %copy-done.15, bf16[256,4096]{1,0:T(8,128)(2,1)} %copy-done.21, ...), custom_call_target="tpu_custom_call" | custom-call | flops 33822867456 | bytes 29360128 | tf_op jit(solution)/shard_map/pallas_call | solution.py:302
  160.6 14.1 %collective-permute-done.13 = bf16[128,4096]{1,0:T(8,128)(2,1)S(1)} collective-permute-done((bf16[128,4096]{1,0:T(8,128)(2,1)}, bf16[128,4096]{1,0:T(8,128)(2,1)S(1)}, u32[]{:S(2)}, u32[]{:S(2)}) %collective-permute-start.13) | collective-permute-done | bytes 1048608 | tf_op jit(solution)/shard_map/ppermute | solution.py:218
  174.7 1.5 collective-permute-done.14
  176.3 0.5 collective-permute-start.26
  177.0 0.6 copy-done.13
  177.6 0.6 collective-permute-start.24
  178.2 1.6 collective-permute-start.22
  180.3 2.6 collective-permute-done.25.refs_2_
  182.9 1.6 collective-permute-start.20
  184.5 0.6 collective-permute-start.21
  185.1 0.8 copy-done.17
  185.8 43.4 %shard_map.115 = (bf16[2,512,1792]{2,1,0:T(8,128)(2,1)S(1)}, bf16[2,512,1792]{2,1,0:T(8,128)(2,1)S(1)}) custom-call(s32[9]{0:T(128)S(1)} %pad_add_fusion.refs_0_.slots_ref, bf16[256,4096]{1,0:T(8,128)(2,1)} %pad_maximum_fusion.1.refs_1_, bf16[256,4096]{1,0:T(8,128)(2,1)} %copy-done.16, bf16[256,4096]{1,0:T(8,128)(2,1)} %copy-done.13, ...), custom_call_target="tpu_custom_call" | custom-call | flops 33822867456 | bytes 29360128 | tf_op jit(solution)/shard_map/pallas_call | solution.py:302
  229.2 1.7 collective-permute-done.20
  230.9 1.3 collective-permute-done.21
  232.9 1.6 collective-permute-start.29
  234.5 1.5 collective-permute-start.27
  236.1 0.8 collective-permute-start.28
  236.9 2.5 collective-permute-done.31.refs_4_
  239.4 1.3 copy-done.20
  240.8 43.4 %shard_map.116 = (bf16[2,512,1792]{2,1,0:T(8,128)(2,1)S(1)}, bf16[2,512,1792]{2,1,0:T(8,128)(2,1)S(1)}) custom-call(s32[9]{0:T(128)S(1)} %pad_add_fusion.refs_0_.slots_ref, bf16[256,4096]{1,0:T(8,128)(2,1)} %copy-done.7, bf16[256,4096]{1,0:T(8,128)(2,1)} %copy-done.18, bf16[256,4096]{1,0:T(8,128)(2,1)} %copy-done.14, bf16[256,4096]{1,0:T(8,128)(2,1)} %copy-done.20, ...), custom_call_target="tpu_custom_call" | custom-call | flops 33822867456 | bytes 29360128 | tf_op jit(solution)/shard_map/pallas_call | solution.py:302
  284.2 1.8 copy-done
  286.6 2.1 collective-permute-done.32.refs_2_
  288.8 1.5 collective-permute-done.33.refs_4_
  290.3 1.0 copy-done.26
  291.3 37.7 %shard_map.117 = (bf16[2,512,1792]{2,1,0:T(8,128)(2,1)S(1)}, f32[8,128]{1,0:T(8,128)S(1)}) custom-call(s32[9]{0:T(128)S(1)} %pad_add_fusion.refs_0_.slots_ref, bf16[128,4096]{1,0:T(8,128)(2,1)} %copy-done.10, bf16[128,4096]{1,0:T(8,128)(2,1)} %copy-done.25, bf16[128,4096]{1,0:T(8,128)(2,1)} %copy-done.24, bf16[128,4096]{1,0:T(8,128)(2,1)} %copy-done.26, ...), custom_call_target="tpu_custom_call" | custom-call | flops 16911433728 | bytes 29360128 | tf_op jit(solution)/shard_map/pallas_call | solution.py:302
  329.0 1.8 copy-done.2
  330.9 1.0 collective-permute-done.34
  331.9 1.5 collective-permute-start.35
  333.5 2.0 collective-permute-done.35
  335.6 1.5 collective-permute-start.36
  337.0 2.1 collective-permute-done.36
  339.7 3.1 collective-permute-done.37
  343.2 4.1 %collective-permute-done.38 = f32[8,128]{1,0:T(8,128)S(1)} collective-permute-done((f32[8,128]{1,0:T(8,128)S(1)}, f32[8,128]{1,0:T(8,128)S(1)}, u32[]{:S(2)}, u32[]{:S(2)}) %collective-permute-start.38) | collective-permute-done | bytes 4128 | tf_op jit(solution)/shard_map/ppermute | solution.py:376
  347.3 11.1 %shard_map.118 = (f32[512,1792]{1,0:T(8,128)}, f32[512,1792]{1,0:T(8,128)}) custom-call(f32[8,128]{1,0:T(8,128)S(1)} %add.82.table_ref, f32[8,128]{1,0:T(8,128)S(1)} %broadcast_multiply_fusion.factors_ref, f32[1,128]{1,0:T(1,128)S(1)} %compare_select_fusion.3.factor_ref, s32[9]{0:T(128)S(1)} %pad_add_fusion.refs_0_.slots_ref, ...), custom_call_target="tpu_custom_call" | custom-call | tf_op jit(solution)/shard_map/pallas_call | solution.py:382
  (119 shorter events, 6.9 us)
Async XLA Ops:
  0.6 3.0 copy-start.4
  0.6 3.3 copy-start.12
  3.2 6.6 %collective-permute-start.2 = (bf16[128,1792]{1,0:T(8,128)(2,1)}, bf16[128,1792]{1,0:T(8,128)(2,1)S(1)}, u32[]{:S(2)}, u32[]{:S(2)}) collective-permute-start(bf16[128,1792]{1,0:T(8,128)(2,1)} %get-tuple-element.121), channel_id=1, source_target_pairs={{0,1},{1,0},{2,3},{3,2},{4,5},{5,4},{6,7},{7,6},{8,9},{9,8},{10,11... | collective-permute-start | bytes 1376264 | tf_op jit(solution)/shard_map/ppermute | solution.py:221
  4.3 54.1 %copy-start.6 = (bf16[128,4096]{1,0:T(8,128)(2,1)}, bf16[128,4096]{1,0:T(8,128)(2,1)S(1)}, u32[]{:S(2)}) copy-start(bf16[128,4096]{1,0:T(8,128)(2,1)S(1)} %fusion.2.refs_1_) | copy-start | bytes 3145732
  4.3 26.6 %collective-permute-start = (bf16[128,4096]{1,0:T(8,128)(2,1)S(1)}, bf16[128,4096]{1,0:T(8,128)(2,1)}, u32[]{:S(2)}, u32[]{:S(2)}) collective-permute-start(bf16[128,4096]{1,0:T(8,128)(2,1)S(1)} %fusion.2.refs_1_), channel_id=1, source_target_pairs={{0,4},{4,12},{8,0},{12,20},{16,8},{20,28},{24,16},{28,24},{1,5},{5... | collective-permute-start | bytes 3145736 | tf_op jit(solution)/shard_map/ppermute | solution.py:218
  6.8 25.4 %collective-permute-start.1 = (bf16[128,4096]{1,0:T(8,128)(2,1)S(1)}, bf16[128,4096]{1,0:T(8,128)(2,1)}, u32[]{:S(2)}, u32[]{:S(2)}) collective-permute-start(bf16[128,4096]{1,0:T(8,128)(2,1)S(1)} %fusion.2.refs_1_), channel_id=1, source_target_pairs={{0,8},{4,0},{8,16},{12,4},{16,24},{20,12},{24,28},{28,20},{1,9},{5... | collective-permute-start | bytes 3145736 | tf_op jit(solution)/shard_map/ppermute | solution.py:218
  7.0 13.6 %collective-permute-start.3 = (bf16[128,1792]{1,0:T(8,128)(2,1)}, bf16[128,1792]{1,0:T(8,128)(2,1)S(1)}, u32[]{:S(2)}, u32[]{:S(2)}) collective-permute-start(bf16[128,1792]{1,0:T(8,128)(2,1)} %get-tuple-element.122), channel_id=1, source_target_pairs={{0,2},{1,3},{2,0},{3,1},{4,6},{5,7},{6,4},{7,5},{8,10},{9,11},{10,... | collective-permute-start | bytes 1376264 | tf_op jit(solution)/shard_map/ppermute | solution.py:221
  8.8 20.1 %collective-permute-start.4 = (bf16[128,1792]{1,0:T(8,128)(2,1)}, bf16[128,1792]{1,0:T(8,128)(2,1)S(1)}, u32[]{:S(2)}, u32[]{:S(2)}) collective-permute-start(bf16[128,1792]{1,0:T(8,128)(2,1)} %get-tuple-element.120), channel_id=1, source_target_pairs={{0,3},{1,2},{2,1},{3,0},{4,7},{5,6},{6,5},{7,4},{8,11},{9,10},{10,... | collective-permute-start | bytes 1376264 | tf_op jit(solution)/shard_map/ppermute | solution.py:221
  30.0 4.3 %copy-start.11 = (bf16[512,1792]{1,0:T(8,128)(2,1)}, bf16[512,1792]{1,0:T(8,128)(2,1)S(1)}, u32[]{:S(2)}) copy-start(bf16[512,1792]{1,0:T(8,128)(2,1)S(1)} %slice_dynamic-update-slice_fusion.refs_7_) | copy-start | bytes 5505028
  30.0 28.8 %copy-start.30 = (s32[8]{0:T(128)S(1)}, s32[8]{0:T(128)}, u32[]{:S(2)}) copy-start(s32[8]{0:T(128)} %constant.61.clone) | copy-start | bytes 100
  30.0 29.4 %copy-start.29 = (s32[8]{0:T(128)S(1)}, s32[8]{0:T(128)}, u32[]{:S(2)}) copy-start(s32[8]{0:T(128)} %constant.65) | copy-start | bytes 100
  30.0 30.1 %copy-start.3 = (s32[8]{0:T(128)S(1)}, s32[8]{0:T(128)}, u32[]{:S(2)}) copy-start(s32[8]{0:T(128)} %constant.60.clone) | copy-start | bytes 100
  32.2 24.8 %collective-permute-start.5 = (bf16[128,4096]{1,0:T(8,128)(2,1)}, bf16[128,4096]{1,0:T(8,128)(2,1)}, u32[]{:S(2)}, u32[]{:S(2)}) collective-permute-start(bf16[128,4096]{1,0:T(8,128)(2,1)} %collective-permute-done), channel_id=1, source_target_pairs={{0,4},{4,12},{8,0},{12,20},{16,8},{20,28},{24,16},{28,24},{1,5},{5... | collective-permute-start | bytes 3145736 | tf_op jit(solution)/shard_map/ppermute | solution.py:218
  33.8 24.5 %collective-permute-start.6 = (bf16[128,4096]{1,0:T(8,128)(2,1)}, bf16[128,4096]{1,0:T(8,128)(2,1)}, u32[]{:S(2)}, u32[]{:S(2)}) collective-permute-start(bf16[128,4096]{1,0:T(8,128)(2,1)} %collective-permute-done.1), channel_id=1, source_target_pairs={{0,8},{4,0},{8,16},{12,4},{16,24},{20,12},{24,28},{28,20},{1,9},{5... | collective-permute-start | bytes 3145736 | tf_op jit(solution)/shard_map/ppermute | solution.py:218
  34.3 24.1 %collective-permute-start.7 = (bf16[128,4096]{1,0:T(8,128)(2,1)S(1)}, bf16[128,4096]{1,0:T(8,128)(2,1)}, u32[]{:S(2)}, u32[]{:S(2)}) collective-permute-start(bf16[128,4096]{1,0:T(8,128)(2,1)S(1)} %fusion.2.refs_1_), channel_id=1, source_target_pairs={{0,2},{1,3},{2,0},{3,1},{4,6},{5,7},{6,4},{7,5},{8,10},{9,11},{10,... | collective-permute-start | bytes 3145736 | tf_op jit(solution)/shard_map/ppermute | solution.py:221
  37.4 71.0 %copy-start.5 = (bf16[256,4096]{1,0:T(8,128)(2,1)}, bf16[256,4096]{1,0:T(8,128)(2,1)S(1)}, u32[]{:S(2)}) copy-start(bf16[256,4096]{1,0:T(8,128)(2,1)S(1)} %pad_maximum_fusion.refs_1_) | copy-start | bytes 6291460
  58.3 9.2 %collective-permute-start.11 = (bf16[128,4096]{1,0:T(8,128)(2,1)S(1)}, bf16[128,4096]{1,0:T(8,128)(2,1)}, u32[]{:S(2)}, u32[]{:S(2)}) collective-permute-start(bf16[128,4096]{1,0:T(8,128)(2,1)S(1)} %fusion.2.refs_1_), channel_id=1, source_target_pairs={{0,1},{1,0},{2,3},{3,2},{4,5},{5,4},{6,7},{7,6},{8,9},{9,8},{10,11... | collective-permute-start | bytes 3145736 | tf_op jit(solution)/shard_map/ppermute | solution.py:221
  58.3 9.2 %collective-permute-start.12 = (bf16[128,4096]{1,0:T(8,128)(2,1)}, bf16[128,4096]{1,0:T(8,128)(2,1)}, u32[]{:S(2)}, u32[]{:S(2)}) collective-permute-start(bf16[128,4096]{1,0:T(8,128)(2,1)} %collective-permute-done.7.refs_3_), channel_id=1, source_target_pairs={{0,1},{1,0},{2,3},{3,2},{4,5},{5,4},{6,7},{7,6},{8,9},{9,8},{10,11... | collective-permute-start | bytes 3145736 | tf_op jit(solution)/shard_map/ppermute | solution.py:221
  60.8 47.7 %collective-permute-start.10 = (bf16[256,4096]{1,0:T(8,128)(2,1)S(1)}, bf16[256,4096]{1,0:T(8,128)(2,1)S(1)}, u32[]{:S(2)}, u32[]{:S(2)}) collective-permute-start(bf16[256,4096]{1,0:T(8,128)(2,1)S(1)} %pad_maximum_fusion.refs_1_), channel_id=1, source_target_pairs={{0,2},{1,3},{2,0},{3,1},{4,6},{5,7},{6,4},{7,5},{8,10},{9,11},{10,... | collective-permute-start | bytes 6291464 | tf_op jit(solution)/shard_map/ppermute | solution.py:221
  62.4 41.9 %collective-permute-start.8 = (bf16[512,1792]{1,0:T(8,128)(2,1)}, bf16[512,1792]{1,0:T(8,128)(2,1)S(1)}, u32[]{:S(2)}, u32[]{:S(2)}) collective-permute-start(bf16[512,1792]{1,0:T(8,128)(2,1)} %copy-done.11), channel_id=1, source_target_pairs={{0,4},{4,12},{8,0},{12,20},{16,8},{20,28},{24,16},{28,24},{1,5},{5... | collective-permute-start | bytes 5505032 | tf_op jit(solution)/shard_map/ppermute | solution.py:218
  64.0 41.6 %collective-permute-start.9 = (bf16[512,1792]{1,0:T(8,128)(2,1)}, bf16[512,1792]{1,0:T(8,128)(2,1)S(1)}, u32[]{:S(2)}, u32[]{:S(2)}) collective-permute-start(bf16[512,1792]{1,0:T(8,128)(2,1)} %copy-done.11), channel_id=1, source_target_pairs={{0,8},{4,0},{8,16},{12,4},{16,24},{20,12},{24,28},{28,20},{1,9},{5... | collective-permute-start | bytes 5505032 | tf_op jit(solution)/shard_map/ppermute | solution.py:218
  104.3 12.8 %copy-start.22 = (bf16[512,1792]{1,0:T(8,128)(2,1)}, bf16[512,1792]{1,0:T(8,128)(2,1)S(1)}, u32[]{:S(2)}) copy-start(bf16[512,1792]{1,0:T(8,128)(2,1)S(1)} %collective-permute-done.8.refs_8_) | copy-start | bytes 5505028
  105.6 2.8 copy-start.23
  108.4 8.7 %copy-start.15 = (bf16[256,4096]{1,0:T(8,128)(2,1)}, bf16[256,4096]{1,0:T(8,128)(2,1)S(1)}, u32[]{:S(2)}) copy-start(bf16[256,4096]{1,0:T(8,128)(2,1)S(1)} %collective-permute-done.10.refs_3_) | copy-start | bytes 6291460
  108.4 4.2 %collective-permute-start.18 = (bf16[256,4096]{1,0:T(8,128)(2,1)S(1)}, bf16[256,4096]{1,0:T(8,128)(2,1)S(1)}, u32[]{:S(2)}, u32[]{:S(2)}) collective-permute-start(bf16[256,4096]{1,0:T(8,128)(2,1)S(1)} %pad_maximum_fusion.refs_1_), channel_id=1, source_target_pairs={{0,1},{1,0},{2,3},{3,2},{4,5},{5,4},{6,7},{7,6},{8,9},{9,8},{10,11... | collective-permute-start | bytes 6291464 | tf_op jit(solution)/shard_map/ppermute | solution.py:221
  108.5 7.1 %collective-permute-start.19 = (bf16[256,4096]{1,0:T(8,128)(2,1)S(1)}, bf16[256,4096]{1,0:T(8,128)(2,1)S(1)}, u32[]{:S(2)}, u32[]{:S(2)}) collective-permute-start(bf16[256,4096]{1,0:T(8,128)(2,1)S(1)} %collective-permute-done.10.refs_3_), channel_id=1, source_target_pairs={{0,1},{1,0},{2,3},{3,2},{4,5},{5,4},{6,7},{7,6},{8,9},{9,8},{10,11... | collective-permute-start | bytes 6291464 | tf_op jit(solution)/shard_map/ppermute | solution.py:221
  109.0 67.2 %collective-permute-start.17 = (bf16[256,4096]{1,0:T(8,128)(2,1)}, bf16[256,4096]{1,0:T(8,128)(2,1)S(1)}, u32[]{:S(2)}, u32[]{:S(2)}) collective-permute-start(bf16[256,4096]{1,0:T(8,128)(2,1)} %pad_maximum_fusion.1.refs_1_), channel_id=1, source_target_pairs={{0,2},{1,3},{2,0},{3,1},{4,6},{5,7},{6,4},{7,5},{8,10},{9,11},{10,... | collective-permute-start | bytes 6291464 | tf_op jit(solution)/shard_map/ppermute | solution.py:221
  110.5 65.7 %collective-permute-start.15 = (bf16[512,1792]{1,0:T(8,128)(2,1)S(1)}, bf16[512,1792]{1,0:T(8,128)(2,1)}, u32[]{:S(2)}, u32[]{:S(2)}) collective-permute-start(bf16[512,1792]{1,0:T(8,128)(2,1)S(1)} %collective-permute-done.8.refs_8_), channel_id=1, source_target_pairs={{0,4},{4,12},{8,0},{12,20},{16,8},{20,28},{24,16},{28,24},{1,5},{5... | collective-permute-start | bytes 5505032 | tf_op jit(solution)/shard_map/ppermute | solution.py:218
  112.1 64.1 %collective-permute-start.16 = (bf16[512,1792]{1,0:T(8,128)(2,1)}, bf16[512,1792]{1,0:T(8,128)(2,1)}, u32[]{:S(2)}, u32[]{:S(2)}) collective-permute-start(bf16[512,1792]{1,0:T(8,128)(2,1)} %copy-done.23), channel_id=1, source_target_pairs={{0,8},{4,0},{8,16},{12,4},{16,24},{20,12},{24,28},{28,20},{1,9},{5... | collective-permute-start | bytes 5505032 | tf_op jit(solution)/shard_map/ppermute | solution.py:218
  112.7 4.5 %copy-start.19 = (bf16[256,4096]{1,0:T(8,128)(2,1)}, bf16[256,4096]{1,0:T(8,128)(2,1)S(1)}, u32[]{:S(2)}) copy-start(bf16[256,4096]{1,0:T(8,128)(2,1)S(1)} %collective-permute-done.18.refs_2_) | copy-start | bytes 6291460
  112.7 62.0 %collective-permute-start.13 = (bf16[128,4096]{1,0:T(8,128)(2,1)}, bf16[128,4096]{1,0:T(8,128)(2,1)S(1)}, u32[]{:S(2)}, u32[]{:S(2)}) collective-permute-start(bf16[128,4096]{1,0:T(8,128)(2,1)} %collective-permute-done.5), channel_id=1, source_target_pairs={{0,4},{4,12},{8,0},{12,20},{16,8},{20,28},{24,16},{28,24},{1,5},{5... | collective-permute-start | bytes 3145736 | tf_op jit(solution)/shard_map/ppermute | solution.py:218
  115.7 60.5 %collective-permute-start.14 = (bf16[128,4096]{1,0:T(8,128)(2,1)}, bf16[128,4096]{1,0:T(8,128)(2,1)S(1)}, u32[]{:S(2)}, u32[]{:S(2)}) collective-permute-start(bf16[128,4096]{1,0:T(8,128)(2,1)} %collective-permute-done.6), channel_id=1, source_target_pairs={{0,8},{4,0},{8,16},{12,4},{16,24},{20,12},{24,28},{28,20},{1,9},{5... | collective-permute-start | bytes 3145736 | tf_op jit(solution)/shard_map/ppermute | solution.py:218
  176.2 6.7 %collective-permute-start.25 = (bf16[256,4096]{1,0:T(8,128)(2,1)}, bf16[256,4096]{1,0:T(8,128)(2,1)S(1)}, u32[]{:S(2)}, u32[]{:S(2)}) collective-permute-start(bf16[256,4096]{1,0:T(8,128)(2,1)} %pad_maximum_fusion.1.refs_1_), channel_id=1, source_target_pairs={{0,1},{1,0},{2,3},{3,2},{4,5},{5,4},{6,7},{7,6},{8,9},{9,8},{10,11... | collective-permute-start | bytes 6291464 | tf_op jit(solution)/shard_map/ppermute | solution.py:221
  176.3 8.2 %collective-permute-start.26 = (bf16[256,4096]{1,0:T(8,128)(2,1)S(1)}, bf16[256,4096]{1,0:T(8,128)(2,1)S(1)}, u32[]{:S(2)}, u32[]{:S(2)}) collective-permute-start(bf16[256,4096]{1,0:T(8,128)(2,1)S(1)} %collective-permute-done.17.refs_3_), channel_id=1, source_target_pairs={{0,1},{1,0},{2,3},{3,2},{4,5},{5,4},{6,7},{7,6},{8,9},{9,8},{10,11... | collective-permute-start | bytes 6291464 | tf_op jit(solution)/shard_map/ppermute | solution.py:221
  177.6 54.6 %copy-start.7 = (bf16[256,4096]{1,0:T(8,128)(2,1)}, bf16[256,4096]{1,0:T(8,128)(2,1)S(1)}, u32[]{:S(2)}) copy-start(bf16[256,4096]{1,0:T(8,128)(2,1)S(1)} %constant_dynamic-update-slice_fusion.refs_1_) | copy-start | bytes 6291460
  177.6 54.5 %collective-permute-start.24 = (bf16[256,4096]{1,0:T(8,128)(2,1)S(1)}, bf16[256,4096]{1,0:T(8,128)(2,1)S(1)}, u32[]{:S(2)}, u32[]{:S(2)}) collective-permute-start(bf16[256,4096]{1,0:T(8,128)(2,1)S(1)} %constant_dynamic-update-slice_fusion.refs_1_), channel_id=1, source_target_pairs={{0,2},{1,3},{2,0},{3,1},{4,6},{5,7},{6,4},{7,5},{8,10},{9,11},{10,... | collective-permute-start | bytes 6291464 | tf_op jit(solution)/shard_map/ppermute | solution.py:221
  178.2 53.9 %collective-permute-start.22 = (bf16[512,1792]{1,0:T(8,128)(2,1)}, bf16[512,1792]{1,0:T(8,128)(2,1)S(1)}, u32[]{:S(2)}, u32[]{:S(2)}) collective-permute-start(bf16[512,1792]{1,0:T(8,128)(2,1)} %collective-permute-done.15.refs_8_), channel_id=1, source_target_pairs={{0,4},{4,12},{8,0},{12,20},{16,8},{20,28},{24,16},{28,24},{1,5},{5... | collective-permute-start | bytes 5505032 | tf_op jit(solution)/shard_map/ppermute | solution.py:218
  179.8 52.3 %collective-permute-start.23 = (bf16[512,1792]{1,0:T(8,128)(2,1)}, bf16[512,1792]{1,0:T(8,128)(2,1)S(1)}, u32[]{:S(2)}, u32[]{:S(2)}) collective-permute-start(bf16[512,1792]{1,0:T(8,128)(2,1)} %collective-permute-done.16.refs_7_), channel_id=1, source_target_pairs={{0,8},{4,0},{8,16},{12,4},{16,24},{20,12},{24,28},{28,20},{1,9},{5... | collective-permute-start | bytes 5505032 | tf_op jit(solution)/shard_map/ppermute | solution.py:218
  182.9 2.2 copy-start.16
  182.9 48.0 %collective-permute-start.20 = (bf16[64,4096]{1,0:T(8,128)(2,1)S(1)}, bf16[64,4096]{1,0:T(8,128)(2,1)S(1)}, u32[]{:S(2)}, u32[]{:S(2)}) collective-permute-start(bf16[64,4096]{1,0:T(8,128)(2,1)S(1)} %slice.58), channel_id=1, source_target_pairs={{0,4},{4,12},{8,0},{12,20},{16,8},{20,28},{24,16},{28,24},{1,5},{5... | collective-permute-start | bytes 1572872 | tf_op jit(solution)/shard_map/ppermute | solution.py:218
  184.5 47.7 %collective-permute-start.21 = (bf16[64,4096]{1,0:T(8,128)(2,1)S(1)}, bf16[64,4096]{1,0:T(8,128)(2,1)S(1)}, u32[]{:S(2)}, u32[]{:S(2)}) collective-permute-start(bf16[64,4096]{1,0:T(8,128)(2,1)S(1)} %slice.59), channel_id=1, source_target_pairs={{0,8},{4,0},{8,16},{12,4},{16,24},{20,12},{24,28},{28,20},{1,9},{5... | collective-permute-start | bytes 1572872 | tf_op jit(solution)/shard_map/ppermute | solution.py:218
  232.2 3.9 %copy-start.8 = (bf16[512,1792]{1,0:T(8,128)(2,1)}, bf16[512,1792]{1,0:T(8,128)(2,1)S(1)}, u32[]{:S(2)}) copy-start(bf16[512,1792]{1,0:T(8,128)(2,1)S(1)} %collective-permute-done.22.refs_8_) | copy-start | bytes 5505028
  232.2 3.9 %copy-start.9 = (bf16[512,1792]{1,0:T(8,128)(2,1)}, bf16[512,1792]{1,0:T(8,128)(2,1)S(1)}, u32[]{:S(2)}) copy-start(bf16[512,1792]{1,0:T(8,128)(2,1)S(1)} %collective-permute-done.23.refs_7_) | copy-start | bytes 5505028
  232.2 3.9 %copy-start.14 = (bf16[256,4096]{1,0:T(8,128)(2,1)}, bf16[256,4096]{1,0:T(8,128)(2,1)S(1)}, u32[]{:S(2)}) copy-start(bf16[256,4096]{1,0:T(8,128)(2,1)S(1)} %collective-permute-done.24.refs_3_) | copy-start | bytes 6291460
  232.2 4.7 %collective-permute-start.30 = (bf16[256,4096]{1,0:T(8,128)(2,1)S(1)}, bf16[256,4096]{1,0:T(8,128)(2,1)S(1)}, u32[]{:S(2)}, u32[]{:S(2)}) collective-permute-start(bf16[256,4096]{1,0:T(8,128)(2,1)S(1)} %constant_dynamic-update-slice_fusion.refs_1_), channel_id=1, source_target_pairs={{0,1},{1,0},{2,3},{3,2},{4,5},{5,4},{6,7},{7,6},{8,9},{9,8},{10,11... | collective-permute-start | bytes 6291464 | tf_op jit(solution)/shard_map/ppermute | solution.py:221
  232.3 7.1 %collective-permute-start.31 = (bf16[256,4096]{1,0:T(8,128)(2,1)S(1)}, bf16[256,4096]{1,0:T(8,128)(2,1)S(1)}, u32[]{:S(2)}, u32[]{:S(2)}) collective-permute-start(bf16[256,4096]{1,0:T(8,128)(2,1)S(1)} %collective-permute-done.24.refs_3_), channel_id=1, source_target_pairs={{0,1},{1,0},{2,3},{3,2},{4,5},{5,4},{6,7},{7,6},{8,9},{9,8},{10,11... | collective-permute-start | bytes 6291464 | tf_op jit(solution)/shard_map/ppermute | solution.py:221
  232.9 53.1 %copy-start.10 = (bf16[128,4096]{1,0:T(8,128)(2,1)}, bf16[128,4096]{1,0:T(8,128)(2,1)S(1)}, u32[]{:S(2)}) copy-start(bf16[128,4096]{1,0:T(8,128)(2,1)S(1)} %constant_dynamic-update-slice_fusion.2.refs_1_) | copy-start | bytes 3145732
  232.9 53.1 %collective-permute-start.29 = (bf16[128,4096]{1,0:T(8,128)(2,1)S(1)}, bf16[128,4096]{1,0:T(8,128)(2,1)S(1)}, u32[]{:S(2)}, u32[]{:S(2)}) collective-permute-start(bf16[128,4096]{1,0:T(8,128)(2,1)S(1)} %constant_dynamic-update-slice_fusion.2.refs_1_), channel_id=1, source_target_pairs={{0,2},{1,3},{2,0},{3,1},{4,6},{5,7},{6,4},{7,5},{8,10},{9,11},{10,... | collective-permute-start | bytes 3145736 | tf_op jit(solution)/shard_map/ppermute | solution.py:221
  234.5 51.5 %collective-permute-start.27 = (bf16[256,1792]{1,0:T(8,128)(2,1)S(1)}, bf16[256,1792]{1,0:T(8,128)(2,1)}, u32[]{:S(2)}, u32[]{:S(2)}) collective-permute-start(bf16[256,1792]{1,0:T(8,128)(2,1)S(1)} %slice.60), channel_id=1, source_target_pairs={{0,4},{4,12},{8,0},{12,20},{16,8},{20,28},{24,16},{28,24},{1,5},{5... | collective-permute-start | bytes 2752520 | tf_op jit(solution)/shard_map/ppermute | solution.py:218
  236.1 49.9 %collective-permute-start.28 = (bf16[256,1792]{1,0:T(8,128)(2,1)S(1)}, bf16[256,1792]{1,0:T(8,128)(2,1)}, u32[]{:S(2)}, u32[]{:S(2)}) collective-permute-start(bf16[256,1792]{1,0:T(8,128)(2,1)S(1)} %slice.61), channel_id=1, source_target_pairs={{0,8},{4,0},{8,16},{12,4},{16,24},{20,12},{24,28},{28,20},{1,9},{5... | collective-permute-start | bytes 2752520 | tf_op jit(solution)/shard_map/ppermute | solution.py:218
  236.9 2.5 copy-start.18
  284.2 1.8 copy-start
  286.0 4.3 %copy-start.24 = (bf16[128,4096]{1,0:T(8,128)(2,1)}, bf16[128,4096]{1,0:T(8,128)(2,1)S(1)}, u32[]{:S(2)}) copy-start(bf16[128,4096]{1,0:T(8,128)(2,1)S(1)} %collective-permute-done.29.refs_3_) | copy-start | bytes 3145732
  286.0 44.9 %copy-start.27 = (f32[3]{0:T(128)S(1)}, f32[3]{0:T(128)}, u32[]{:S(2)}) copy-start(f32[3]{0:T(128)} %param.16) | copy-start | bytes 40
  286.0 47.4 %copy-start.28 = (s32[8]{0:T(128)S(1)}, s32[8]{0:T(128)}, u32[]{:S(2)}) copy-start(s32[8]{0:T(128)} %param.15) | copy-start | bytes 100
  286.0 2.7 collective-permute-start.32
  286.3 4.0 %collective-permute-start.33 = (bf16[128,4096]{1,0:T(8,128)(2,1)S(1)}, bf16[128,4096]{1,0:T(8,128)(2,1)S(1)}, u32[]{:S(2)}, u32[]{:S(2)}) collective-permute-start(bf16[128,4096]{1,0:T(8,128)(2,1)S(1)} %collective-permute-done.29.refs_3_), channel_id=1, source_target_pairs={{0,1},{1,0},{2,3},{3,2},{4,5},{5,4},{6,7},{7,6},{8,9},{9,8},{10,11... | collective-permute-start | bytes 3145736 | tf_op jit(solution)/shard_map/ppermute | solution.py:221
  291.3 56.0 %copy-start.1 = (bf16[2,512,1792]{2,1,0:T(8,128)(2,1)S(1)}, bf16[2,512,1792]{2,1,0:T(8,128)(2,1)}, u32[]{:S(2)}) copy-start(bf16[2,512,1792]{2,1,0:T(8,128)(2,1)} %copy-done) | copy-start | bytes 11010052
  329.0 1.8 copy-start.2
  330.8 1.2 collective-permute-start.34
  331.9 3.6 %collective-permute-start.35 = (f32[8,128]{1,0:T(8,128)S(1)}, f32[8,128]{1,0:T(8,128)S(1)}, u32[]{:S(2)}, u32[]{:S(2)}) collective-permute-start(f32[8,128]{1,0:T(8,128)S(1)} %add.78), channel_id=1, source_target_pairs={{0,2},{1,3},{2,0},{3,1},{4,6},{5,7},{6,4},{7,5},{8,10},{9,11},{10,... | collective-permute-start | bytes 12296 | tf_op jit(solution)/shard_map/ppermute | solution.py:376
  335.6 3.6 %collective-permute-start.36 = (f32[8,128]{1,0:T(8,128)S(1)}, f32[8,128]{1,0:T(8,128)S(1)}, u32[]{:S(2)}, u32[]{:S(2)}) collective-permute-start(f32[8,128]{1,0:T(8,128)S(1)} %add.79), channel_id=1, source_target_pairs={{0,4},{1,5},{2,6},{3,7},{4,0},{5,1},{6,2},{7,3},{8,12},{9,13},{10,... | collective-permute-start | bytes 12296 | tf_op jit(solution)/shard_map/ppermute | solution.py:376
  339.2 3.6 %collective-permute-start.37 = (f32[8,128]{1,0:T(8,128)S(1)}, f32[8,128]{1,0:T(8,128)S(1)}, u32[]{:S(2)}, u32[]{:S(2)}) collective-permute-start(f32[8,128]{1,0:T(8,128)S(1)} %add.80), channel_id=1, source_target_pairs={{0,8},{1,9},{2,10},{3,11},{4,12},{5,13},{6,14},{7,15},{8,0},{9,1},... | collective-permute-start | bytes 12296 | tf_op jit(solution)/shard_map/ppermute | solution.py:376
  342.8 4.5 %collective-permute-start.38 = (f32[8,128]{1,0:T(8,128)S(1)}, f32[8,128]{1,0:T(8,128)S(1)}, u32[]{:S(2)}, u32[]{:S(2)}) collective-permute-start(f32[8,128]{1,0:T(8,128)S(1)} %add.81), channel_id=1, source_target_pairs={{0,16},{1,17},{2,18},{3,19},{4,20},{5,21},{6,22},{7,23},{8,24},{9,... | collective-permute-start | bytes 12296 | tf_op jit(solution)/shard_map/ppermute | solution.py:376
  (6 other events, 8.0 us)

commit v4 on v3

--- a/solution.py
+++ b/solution.py
@@ -11,7 +11,7 @@
 ITERS = 3
 LINE = 4
 AXES = ("colony", "fsdp")
-VMEM = 28 * 1024 * 1024
+VMEM = 24 * 1024 * 1024
 VMEM_FIRST = 50 * 1024 * 1024
 
 
@@ -152,10 +152,9 @@
 def combine_kernel(count, table_ref, factors_ref, factor_ref, slots_ref, *refs):
     grads = refs[:count]
     gate_out, up_out = refs[count : count + 2]
-    coef = refs[count + 2]
-
-    @pl.when(pl.program_id(0) == 0)
-    def _():
+    coef, held, sems = refs[count + 2 :]
+
+    def weigh():
         table = table_ref[...] * factors_ref[...]
         shape = table.shape
         row = lax.broadcasted_iota(jnp.int32, shape, 0)
@@ -181,20 +180,34 @@
         for k in range(count):
             coef[k] = jnp.sum(jnp.where(lanes == slots_ref[k], mine, 0.0))
 
+    weigh()
     scales = [coef[k] for k in range(count)]
     rows = gate_out.shape[0]
-    chunk = 16
-    for matrix, out in ((0, gate_out), (1, up_out)):
-
-        def body(at, carry, matrix=matrix, out=out):
-            span = pl.ds(pl.multiple_of(at * chunk, chunk), chunk)
-            total = scales[0] * grads[0][matrix, span, :].astype(jnp.float32)
-            for k in range(1, count):
-                total = total + scales[k] * grads[k][matrix, span, :].astype(jnp.float32)
-            out[span, :] = total
-            return carry
-
-        lax.fori_loop(0, rows // chunk, body, 0)
+    slots, cut, chunk = held.shape[0], held.shape[1], 16
+    copies = []
+    for first in range(0, rows, cut):
+        for matrix, out in ((0, gate_out), (1, up_out)):
+            slot = len(copies) % slots
+            if len(copies) >= slots:
+                copies[-slots].wait()
+
+            def body(at, carry, matrix=matrix, first=first, slot=slot):
+                start = pl.multiple_of(at * chunk, chunk)
+                span = pl.ds(first + start, chunk)
+                total = scales[0] * grads[0][matrix, span, :].astype(jnp.float32)
+                for k in range(1, count):
+                    total = total + scales[k] * grads[k][matrix, span, :].astype(jnp.float32)
+                held[slot, pl.ds(start, chunk), :] = total
+                return carry
+
+            lax.fori_loop(0, cut // chunk, body, 0)
+            copy = pltpu.make_async_copy(
+                held.at[slot], out.at[pl.ds(first, cut)], sems.at[slot]
+            )
+            copy.start()
+            copies.append(copy)
+    for copy in copies[-slots:]:
+        copy.wait()
 
 
 def on_device(order, hidden_states, norm_gain, gate_weight, up_weight, hidden_grad, byz_order, byz_scale):
@@ -377,18 +390,21 @@
         bit *= 2
 
     cut = min(64, rows)
-    whole = pl.BlockSpec(table_shape, lambda b: (0, 0))
-    out_block = pl.BlockSpec((cut, width), lambda b: (b, 0))
+    vmem = pl.BlockSpec(memory_space=pltpu.VMEM)
+    main = pl.BlockSpec(memory_space=pltpu.HBM)
+    near = [pltpu.with_memory_space_constraint(grad, pltpu.VMEM) for grad in grads]
     return pl.pallas_call(
         functools.partial(combine_kernel, count),
-        grid=(rows // cut,),
-        in_specs=[whole, whole, pl.BlockSpec((1, 128), lambda b: (0, 0)), smem]
-        + [pl.BlockSpec((2, cut, width), lambda b: (0, b, 0))] * count,
-        out_specs=[out_block, out_block],
+        in_specs=[vmem, vmem, vmem, smem] + [vmem] * count,
+        out_specs=[main, main],
         out_shape=[jax.ShapeDtypeStruct((rows, width), jnp.float32)] * 2,
-        scratch_shapes=[pltpu.SMEM((count,), jnp.float32)],
+        scratch_shapes=[
+            pltpu.SMEM((count,), jnp.float32),
+            pltpu.VMEM((4, cut, width), jnp.float32),
+            pltpu.SemaphoreType.DMA((4,)),
+        ],
         compiler_params=pltpu.CompilerParams(vmem_limit_bytes=VMEM),
-    )(table, factors, factor[None], slots, *grads)
+    )(table, factors, factor[None], slots, *near)
 
 
 def solution(mesh):

time: 364 us -> 357 us (0.981)
  Pallas kernels: 204 us -> 200 us
  transfers between devices with their start and end apart: 39 -> 39, of which waited for: 24 -> 24; matrix products, arithmetic and copies ran while one was open for 3% -> 3% of each run, Pallas kernels for 43% -> 44%
where the time goes in v4:
time: 357 us; the launch traced here: 352 us
  Pallas kernels  200 us (56%)
  waiting for transfers between devices  99.4 us (28%)
  starting transfers between devices  34.2 us (10%)
  local copies, waits for them, and re-layouts  10 us (3%)
  other arithmetic  6.3 us (2%)
    pallas_call x5, Pallas kernels, colonies(): pl.pallas_call(functools.partial(colony_kernel, group, count, parts, shar...  192 us
    ppermute x16, waiting for transfers between devices, hop(): return lax.ppermute(value, 'colony', pairs)  55 us
    ppermute x18, waiting for transfers between devices, swap(): return lax.ppermute(value, 'fsdp', [(j, j ^ mask) for j in range(shards)])  32.2 us
    ppermute x16, starting transfers between devices, hop(): return lax.ppermute(value, 'colony', pairs)  18.4 us
    ppermute x5, waiting for transfers between devices, on_device(): lax.ppermute(table, AXES, [(d, d ^ bit) for d in range(devices)])  12.3 us
    ppermute x18, starting transfers between devices, swap(): return lax.ppermute(value, 'fsdp', [(j, j ^ mask) for j in range(shards)])  11.7 us
    pallas_call x1, Pallas kernels, on_device(): pl.pallas_call(functools.partial(combine_kernel, count), in_specs=[vmem,...  8.12 us
  transfers between devices with their start and end apart: 39, of which 24 were waited for; matrix products, arithmetic and copies ran while one was open for 3% of the time, Pallas kernels for 44%

profile of v4, /device:TPU:0, one launch (start us, length us, event | category | flops | bytes accessed | tf_op | source)
XLA Modules:
  0.0 351.9 jit_solution(4257405305976205954)
XLA Ops:
  0.7 2.5 dynamic-slice_bitcast_fusion
  4.3 2.6 collective-permute-start
  7.0 1.9 collective-permute-start.3
  8.8 1.0 fusion.4
  9.8 10.7 %collective-permute-done.3 = bf16[128,1792]{1,0:T(8,128)(2,1)S(1)} collective-permute-done((bf16[128,1792]{1,0:T(8,128)(2,1)}, bf16[128,1792]{1,0:T(8,128)(2,1)S(1)}, u32[]{:S(2)}, u32[]{:S(2)}) %collective-permute-start.3) | collective-permute-done | bytes 458784 | tf_op jit(solution)/shard_map/ppermute | solution.py:234
  20.5 8.4 %collective-permute-done.4 = bf16[128,1792]{1,0:T(8,128)(2,1)S(1)} collective-permute-done((bf16[128,1792]{1,0:T(8,128)(2,1)}, bf16[128,1792]{1,0:T(8,128)(2,1)S(1)}, u32[]{:S(2)}, u32[]{:S(2)}) %collective-permute-start.4) | collective-permute-done | bytes 458784 | tf_op jit(solution)/shard_map/ppermute | solution.py:234
  29.0 1.0 fusion.3
  30.1 0.8 collective-permute-done
  30.8 1.4 collective-permute-done.1
  32.2 1.6 collective-permute-start.5
  34.3 1.5 collective-permute-start.7
  35.8 1.7 pad_maximum_fusion.refs_1_
  37.4 19.6 %collective-permute-done.5 = bf16[128,4096]{1,0:T(8,128)(2,1)} collective-permute-done((bf16[128,4096]{1,0:T(8,128)(2,1)}, bf16[128,4096]{1,0:T(8,128)(2,1)}, u32[]{:S(2)}, u32[]{:S(2)}) %collective-permute-start.5) | collective-permute-done | bytes 1048608 | tf_op jit(solution)/shard_map/ppermute | solution.py:231
  57.0 1.3 collective-permute-done.6
  58.3 0.5 collective-permute-start.12
  58.8 0.6 dynamic_slice.21
  59.4 0.6 compare_select_fusion
  60.1 0.6 gather_fusion
  60.8 1.6 collective-permute-start.10
  62.4 1.6 collective-permute-start.8
  64.4 3.1 pad_maximum_fusion.1.refs_1_
  67.5 24.8 %shard_map.113.refs_9_.refs_0_ = bf16[2,512,1792]{2,1,0:T(8,128)(2,1)S(1)} custom-call(s32[9]{0:T(128)S(1)} %pad_add_fusion.refs_0_.slots_ref, bf16[128,4096]{1,0:T(8,128)(2,1)} %copy-done.3, bf16[128,4096]{1,0:T(8,128)(2,1)} %collective-permute-done.11.refs_2_, bf16[128,4096]{1,0:T(8,128)(2,1)} %collective-permute-done.7.refs_3_, ...), custom_call_target="tpu_custom_call" | custom-call | flops 16911433728 | bytes 29360128 | tf_op jit(solution)/shard_map/pallas_call | solution.py:315
  92.3 12.0 %collective-permute-done.8.refs_8_ = bf16[512,1792]{1,0:T(8,128)(2,1)S(1)} collective-permute-done((bf16[512,1792]{1,0:T(8,128)(2,1)}, bf16[512,1792]{1,0:T(8,128)(2,1)S(1)}, u32[]{:S(2)}, u32[]{:S(2)}) %collective-permute-start.8) | collective-permute-done | bytes 1835040 | tf_op jit(solution)/shard_map/ppermute | solution.py:231
  104.3 1.3 collective-permute-done.9.refs_7_
  105.6 2.8 collective-permute-done.10.refs_3_
  108.5 0.5 collective-permute-start.19
  109.0 1.5 collective-permute-start.17
  110.4 1.6 collective-permute-start.15
  112.6 1.6 collective-permute-start.13
  114.2 1.4 collective-permute-done.19.refs_4_
  115.6 1.5 collective-permute-start.14
  117.1 43.4 %shard_map.114 = (bf16[2,512,1792]{2,1,0:T(8,128)(2,1)S(1)}, bf16[2,512,1792]{2,1,0:T(8,128)(2,1)S(1)}) custom-call(s32[9]{0:T(128)S(1)} %pad_add_fusion.refs_0_.slots_ref, bf16[256,4096]{1,0:T(8,128)(2,1)} %copy-done.2, bf16[256,4096]{1,0:T(8,128)(2,1)} %copy-done.16, bf16[256,4096]{1,0:T(8,128)(2,1)} %copy-done.12, bf16[256,4096]{1,0:T(8,128)(2,1)} %copy-done.18, ...), custom_call_target="tpu_custom_call" | custom-call | flops 33822867456 | bytes 29360128 | tf_op jit(solution)/shard_map/pallas_call | solution.py:315
  160.5 14.3 %collective-permute-done.13 = bf16[128,4096]{1,0:T(8,128)(2,1)S(1)} collective-permute-done((bf16[128,4096]{1,0:T(8,128)(2,1)}, bf16[128,4096]{1,0:T(8,128)(2,1)S(1)}, u32[]{:S(2)}, u32[]{:S(2)}) %collective-permute-start.13) | collective-permute-done | bytes 1048608 | tf_op jit(solution)/shard_map/ppermute | solution.py:231
  174.8 1.3 collective-permute-done.14
  176.3 0.5 collective-permute-start.26
  176.9 0.6 copy-done.10
  177.6 0.6 collective-permute-start.24
  178.2 1.6 collective-permute-start.22
  180.3 2.6 collective-permute-done.25.refs_2_
  182.8 1.6 collective-permute-start.20
  184.4 0.6 collective-permute-start.21
  185.0 0.8 copy-done.14
  185.8 43.4 %shard_map.115 = (bf16[2,512,1792]{2,1,0:T(8,128)(2,1)S(1)}, bf16[2,512,1792]{2,1,0:T(8,128)(2,1)S(1)}) custom-call(s32[9]{0:T(128)S(1)} %pad_add_fusion.refs_0_.slots_ref, bf16[256,4096]{1,0:T(8,128)(2,1)} %pad_maximum_fusion.1.refs_1_, bf16[256,4096]{1,0:T(8,128)(2,1)} %copy-done.13, bf16[256,4096]{1,0:T(8,128)(2,1)} %copy-done.10, ...), custom_call_target="tpu_custom_call" | custom-call | flops 33822867456 | bytes 29360128 | tf_op jit(solution)/shard_map/pallas_call | solution.py:315
  229.1 1.5 collective-permute-done.20
  230.6 1.5 collective-permute-done.21
  232.2 0.5 collective-permute-start.31
  232.8 1.6 collective-permute-start.29
  234.4 1.5 collective-permute-start.27
  236.1 0.8 collective-permute-start.28
  236.9 2.5 collective-permute-done.31.refs_4_
  239.4 1.3 copy-done.17
  240.7 43.4 %shard_map.116 = (bf16[2,512,1792]{2,1,0:T(8,128)(2,1)S(1)}, bf16[2,512,1792]{2,1,0:T(8,128)(2,1)S(1)}) custom-call(s32[9]{0:T(128)S(1)} %pad_add_fusion.refs_0_.slots_ref, bf16[256,4096]{1,0:T(8,128)(2,1)} %copy-done.4, bf16[256,4096]{1,0:T(8,128)(2,1)} %copy-done.15, bf16[256,4096]{1,0:T(8,128)(2,1)} %copy-done.11, bf16[256,4096]{1,0:T(8,128)(2,1)} %copy-done.17, ...), custom_call_target="tpu_custom_call" | custom-call | flops 33822867456 | bytes 29360128 | tf_op jit(solution)/shard_map/pallas_call | solution.py:315
  284.8 2.1 collective-permute-done.32.refs_2_
  286.9 1.5 collective-permute-done.33.refs_4_
  288.5 1.0 copy-done.24
  289.5 37.4 %shard_map.117 = (bf16[2,512,1792]{2,1,0:T(8,128)(2,1)S(1)}, f32[8,128]{1,0:T(8,128)S(1)}) custom-call(s32[9]{0:T(128)S(1)} %pad_add_fusion.refs_0_.slots_ref, bf16[128,4096]{1,0:T(8,128)(2,1)} %copy-done.7, bf16[128,4096]{1,0:T(8,128)(2,1)} %copy-done.23, bf16[128,4096]{1,0:T(8,128)(2,1)} %copy-done.22, bf16[128,4096]{1,0:T(8,128)(2,1)} %copy-done.24, ...), custom_call_target="tpu_custom_call" | custom-call | flops 16911433728 | bytes 29360128 | tf_op jit(solution)/shard_map/pallas_call | solution.py:315
  327.1 1.0 collective-permute-done.34
  328.1 1.5 collective-permute-start.35
  329.7 2.0 collective-permute-done.35
  331.7 1.5 collective-permute-start.36
  333.2 2.1 collective-permute-done.36
  335.9 3.1 collective-permute-done.37
  339.4 4.1 %collective-permute-done.38 = f32[8,128]{1,0:T(8,128)S(1)} collective-permute-done((f32[8,128]{1,0:T(8,128)S(1)}, f32[8,128]{1,0:T(8,128)S(1)}, u32[]{:S(2)}, u32[]{:S(2)}) %collective-permute-start.38) | collective-permute-done | bytes 4128 | tf_op jit(solution)/shard_map/ppermute | solution.py:389
  343.4 8.1 %shard_map.118 = (f32[512,1792]{1,0:T(8,128)}, f32[512,1792]{1,0:T(8,128)}) custom-call(f32[8,128]{1,0:T(8,128)S(1)} %add.82.table_ref, f32[8,128]{1,0:T(8,128)S(1)} %broadcast_multiply_fusion.factors_ref, f32[1,128]{1,0:T(1,128)S(1)} %compare_select_fusion.3.factor_ref, s32[9]{0:T(128)S(1)} %pad_add_fusion.refs_0_.slots_ref, ...), custom_call_target="tpu_custom_call" | custom-call | tf_op jit(solution)/shard_map/pallas_call | solution.py:396
  (119 shorter events, 5.9 us)
Async XLA Ops:
  0.6 3.0 copy-start.1
  0.6 3.3 copy-start.9
  3.2 6.6 %collective-permute-start.2 = (bf16[128,1792]{1,0:T(8,128)(2,1)}, bf16[128,1792]{1,0:T(8,128)(2,1)S(1)}, u32[]{:S(2)}, u32[]{:S(2)}) collective-permute-start(bf16[128,1792]{1,0:T(8,128)(2,1)} %get-tuple-element.121), channel_id=1, source_target_pairs={{0,1},{1,0},{2,3},{3,2},{4,5},{5,4},{6,7},{7,6},{8,9},{9,8},{10,11... | collective-permute-start | bytes 1376264 | tf_op jit(solution)/shard_map/ppermute | solution.py:234
  4.3 54.1 %copy-start.3 = (bf16[128,4096]{1,0:T(8,128)(2,1)}, bf16[128,4096]{1,0:T(8,128)(2,1)S(1)}, u32[]{:S(2)}) copy-start(bf16[128,4096]{1,0:T(8,128)(2,1)S(1)} %fusion.2.refs_1_) | copy-start | bytes 3145732
  4.3 26.6 %collective-permute-start = (bf16[128,4096]{1,0:T(8,128)(2,1)S(1)}, bf16[128,4096]{1,0:T(8,128)(2,1)}, u32[]{:S(2)}, u32[]{:S(2)}) collective-permute-start(bf16[128,4096]{1,0:T(8,128)(2,1)S(1)} %fusion.2.refs_1_), channel_id=1, source_target_pairs={{0,4},{4,12},{8,0},{12,20},{16,8},{20,28},{24,16},{28,24},{1,5},{5... | collective-permute-start | bytes 3145736 | tf_op jit(solution)/shard_map/ppermute | solution.py:231
  6.8 25.4 %collective-permute-start.1 = (bf16[128,4096]{1,0:T(8,128)(2,1)S(1)}, bf16[128,4096]{1,0:T(8,128)(2,1)}, u32[]{:S(2)}, u32[]{:S(2)}) collective-permute-start(bf16[128,4096]{1,0:T(8,128)(2,1)S(1)} %fusion.2.refs_1_), channel_id=1, source_target_pairs={{0,8},{4,0},{8,16},{12,4},{16,24},{20,12},{24,28},{28,20},{1,9},{5... | collective-permute-start | bytes 3145736 | tf_op jit(solution)/shard_map/ppermute | solution.py:231
  7.0 13.6 %collective-permute-start.3 = (bf16[128,1792]{1,0:T(8,128)(2,1)}, bf16[128,1792]{1,0:T(8,128)(2,1)S(1)}, u32[]{:S(2)}, u32[]{:S(2)}) collective-permute-start(bf16[128,1792]{1,0:T(8,128)(2,1)} %get-tuple-element.122), channel_id=1, source_target_pairs={{0,2},{1,3},{2,0},{3,1},{4,6},{5,7},{6,4},{7,5},{8,10},{9,11},{10,... | collective-permute-start | bytes 1376264 | tf_op jit(solution)/shard_map/ppermute | solution.py:234
  8.8 20.1 %collective-permute-start.4 = (bf16[128,1792]{1,0:T(8,128)(2,1)}, bf16[128,1792]{1,0:T(8,128)(2,1)S(1)}, u32[]{:S(2)}, u32[]{:S(2)}) collective-permute-start(bf16[128,1792]{1,0:T(8,128)(2,1)} %get-tuple-element.120), channel_id=1, source_target_pairs={{0,3},{1,2},{2,1},{3,0},{4,7},{5,6},{6,5},{7,4},{8,11},{9,10},{10,... | collective-permute-start | bytes 1376264 | tf_op jit(solution)/shard_map/ppermute | solution.py:234
  30.0 4.3 %copy-start.8 = (bf16[512,1792]{1,0:T(8,128)(2,1)}, bf16[512,1792]{1,0:T(8,128)(2,1)S(1)}, u32[]{:S(2)}) copy-start(bf16[512,1792]{1,0:T(8,128)(2,1)S(1)} %slice_dynamic-update-slice_fusion.refs_7_) | copy-start | bytes 5505028
  30.0 28.8 %copy-start.30 = (s32[8]{0:T(128)S(1)}, s32[8]{0:T(128)}, u32[]{:S(2)}) copy-start(s32[8]{0:T(128)} %constant.61.clone) | copy-start | bytes 100
  30.0 29.4 %copy-start.29 = (s32[8]{0:T(128)S(1)}, s32[8]{0:T(128)}, u32[]{:S(2)}) copy-start(s32[8]{0:T(128)} %constant.65) | copy-start | bytes 100
  30.0 30.1 %copy-start = (s32[8]{0:T(128)S(1)}, s32[8]{0:T(128)}, u32[]{:S(2)}) copy-start(s32[8]{0:T(128)} %constant.60.clone) | copy-start | bytes 100
  32.2 24.8 %collective-permute-start.5 = (bf16[128,4096]{1,0:T(8,128)(2,1)}, bf16[128,4096]{1,0:T(8,128)(2,1)}, u32[]{:S(2)}, u32[]{:S(2)}) collective-permute-start(bf16[128,4096]{1,0:T(8,128)(2,1)} %collective-permute-done), channel_id=1, source_target_pairs={{0,4},{4,12},{8,0},{12,20},{16,8},{20,28},{24,16},{28,24},{1,5},{5... | collective-permute-start | bytes 3145736 | tf_op jit(solution)/shard_map/ppermute | solution.py:231
  33.8 24.5 %collective-permute-start.6 = (bf16[128,4096]{1,0:T(8,128)(2,1)}, bf16[128,4096]{1,0:T(8,128)(2,1)}, u32[]{:S(2)}, u32[]{:S(2)}) collective-permute-start(bf16[128,4096]{1,0:T(8,128)(2,1)} %collective-permute-done.1), channel_id=1, source_target_pairs={{0,8},{4,0},{8,16},{12,4},{16,24},{20,12},{24,28},{28,20},{1,9},{5... | collective-permute-start | bytes 3145736 | tf_op jit(solution)/shard_map/ppermute | solution.py:231
  34.3 24.1 %collective-permute-start.7 = (bf16[128,4096]{1,0:T(8,128)(2,1)S(1)}, bf16[128,4096]{1,0:T(8,128)(2,1)}, u32[]{:S(2)}, u32[]{:S(2)}) collective-permute-start(bf16[128,4096]{1,0:T(8,128)(2,1)S(1)} %fusion.2.refs_1_), channel_id=1, source_target_pairs={{0,2},{1,3},{2,0},{3,1},{4,6},{5,7},{6,4},{7,5},{8,10},{9,11},{10,... | collective-permute-start | bytes 3145736 | tf_op jit(solution)/shard_map/ppermute | solution.py:234
  37.4 71.0 %copy-start.2 = (bf16[256,4096]{1,0:T(8,128)(2,1)}, bf16[256,4096]{1,0:T(8,128)(2,1)S(1)}, u32[]{:S(2)}) copy-start(bf16[256,4096]{1,0:T(8,128)(2,1)S(1)} %pad_maximum_fusion.refs_1_) | copy-start | bytes 6291460
  58.3 9.2 %collective-permute-start.11 = (bf16[128,4096]{1,0:T(8,128)(2,1)S(1)}, bf16[128,4096]{1,0:T(8,128)(2,1)}, u32[]{:S(2)}, u32[]{:S(2)}) collective-permute-start(bf16[128,4096]{1,0:T(8,128)(2,1)S(1)} %fusion.2.refs_1_), channel_id=1, source_target_pairs={{0,1},{1,0},{2,3},{3,2},{4,5},{5,4},{6,7},{7,6},{8,9},{9,8},{10,11... | collective-permute-start | bytes 3145736 | tf_op jit(solution)/shard_map/ppermute | solution.py:234
  58.3 9.2 %collective-permute-start.12 = (bf16[128,4096]{1,0:T(8,128)(2,1)}, bf16[128,4096]{1,0:T(8,128)(2,1)}, u32[]{:S(2)}, u32[]{:S(2)}) collective-permute-start(bf16[128,4096]{1,0:T(8,128)(2,1)} %collective-permute-done.7.refs_3_), channel_id=1, source_target_pairs={{0,1},{1,0},{2,3},{3,2},{4,5},{5,4},{6,7},{7,6},{8,9},{9,8},{10,11... | collective-permute-start | bytes 3145736 | tf_op jit(solution)/shard_map/ppermute | solution.py:234
  60.8 47.7 %collective-permute-start.10 = (bf16[256,4096]{1,0:T(8,128)(2,1)S(1)}, bf16[256,4096]{1,0:T(8,128)(2,1)S(1)}, u32[]{:S(2)}, u32[]{:S(2)}) collective-permute-start(bf16[256,4096]{1,0:T(8,128)(2,1)S(1)} %pad_maximum_fusion.refs_1_), channel_id=1, source_target_pairs={{0,2},{1,3},{2,0},{3,1},{4,6},{5,7},{6,4},{7,5},{8,10},{9,11},{10,... | collective-permute-start | bytes 6291464 | tf_op jit(solution)/shard_map/ppermute | solution.py:234
  62.4 41.9 %collective-permute-start.8 = (bf16[512,1792]{1,0:T(8,128)(2,1)}, bf16[512,1792]{1,0:T(8,128)(2,1)S(1)}, u32[]{:S(2)}, u32[]{:S(2)}) collective-permute-start(bf16[512,1792]{1,0:T(8,128)(2,1)} %copy-done.8), channel_id=1, source_target_pairs={{0,4},{4,12},{8,0},{12,20},{16,8},{20,28},{24,16},{28,24},{1,5},{5... | collective-permute-start | bytes 5505032 | tf_op jit(solution)/shard_map/ppermute | solution.py:231
  64.0 41.6 %collective-permute-start.9 = (bf16[512,1792]{1,0:T(8,128)(2,1)}, bf16[512,1792]{1,0:T(8,128)(2,1)S(1)}, u32[]{:S(2)}, u32[]{:S(2)}) collective-permute-start(bf16[512,1792]{1,0:T(8,128)(2,1)} %copy-done.8), channel_id=1, source_target_pairs={{0,8},{4,0},{8,16},{12,4},{16,24},{20,12},{24,28},{28,20},{1,9},{5... | collective-permute-start | bytes 5505032 | tf_op jit(solution)/shard_map/ppermute | solution.py:231
  104.3 4.6 %copy-start.20 = (bf16[512,1792]{1,0:T(8,128)(2,1)}, bf16[512,1792]{1,0:T(8,128)(2,1)S(1)}, u32[]{:S(2)}) copy-start(bf16[512,1792]{1,0:T(8,128)(2,1)S(1)} %collective-permute-done.8.refs_8_) | copy-start | bytes 5505028
  105.6 2.8 copy-start.21
  108.4 8.7 %copy-start.12 = (bf16[256,4096]{1,0:T(8,128)(2,1)}, bf16[256,4096]{1,0:T(8,128)(2,1)S(1)}, u32[]{:S(2)}) copy-start(bf16[256,4096]{1,0:T(8,128)(2,1)S(1)} %collective-permute-done.10.refs_3_) | copy-start | bytes 6291460
  108.4 4.2 %collective-permute-start.18 = (bf16[256,4096]{1,0:T(8,128)(2,1)S(1)}, bf16[256,4096]{1,0:T(8,128)(2,1)S(1)}, u32[]{:S(2)}, u32[]{:S(2)}) collective-permute-start(bf16[256,4096]{1,0:T(8,128)(2,1)S(1)} %pad_maximum_fusion.refs_1_), channel_id=1, source_target_pairs={{0,1},{1,0},{2,3},{3,2},{4,5},{5,4},{6,7},{7,6},{8,9},{9,8},{10,11... | collective-permute-start | bytes 6291464 | tf_op jit(solution)/shard_map/ppermute | solution.py:234
  108.5 7.1 %collective-permute-start.19 = (bf16[256,4096]{1,0:T(8,128)(2,1)S(1)}, bf16[256,4096]{1,0:T(8,128)(2,1)S(1)}, u32[]{:S(2)}, u32[]{:S(2)}) collective-permute-start(bf16[256,4096]{1,0:T(8,128)(2,1)S(1)} %collective-permute-done.10.refs_3_), channel_id=1, source_target_pairs={{0,1},{1,0},{2,3},{3,2},{4,5},{5,4},{6,7},{7,6},{8,9},{9,8},{10,11... | collective-permute-start | bytes 6291464 | tf_op jit(solution)/shard_map/ppermute | solution.py:234
  109.0 67.2 %collective-permute-start.17 = (bf16[256,4096]{1,0:T(8,128)(2,1)}, bf16[256,4096]{1,0:T(8,128)(2,1)S(1)}, u32[]{:S(2)}, u32[]{:S(2)}) collective-permute-start(bf16[256,4096]{1,0:T(8,128)(2,1)} %pad_maximum_fusion.1.refs_1_), channel_id=1, source_target_pairs={{0,2},{1,3},{2,0},{3,1},{4,6},{5,7},{6,4},{7,5},{8,10},{9,11},{10,... | collective-permute-start | bytes 6291464 | tf_op jit(solution)/shard_map/ppermute | solution.py:234
  110.4 65.7 %collective-permute-start.15 = (bf16[512,1792]{1,0:T(8,128)(2,1)}, bf16[512,1792]{1,0:T(8,128)(2,1)S(1)}, u32[]{:S(2)}, u32[]{:S(2)}) collective-permute-start(bf16[512,1792]{1,0:T(8,128)(2,1)} %copy-done.20), channel_id=1, source_target_pairs={{0,4},{4,12},{8,0},{12,20},{16,8},{20,28},{24,16},{28,24},{1,5},{5... | collective-permute-start | bytes 5505032 | tf_op jit(solution)/shard_map/ppermute | solution.py:231
  112.0 64.1 %collective-permute-start.16 = (bf16[512,1792]{1,0:T(8,128)(2,1)}, bf16[512,1792]{1,0:T(8,128)(2,1)}, u32[]{:S(2)}, u32[]{:S(2)}) collective-permute-start(bf16[512,1792]{1,0:T(8,128)(2,1)} %copy-done.21), channel_id=1, source_target_pairs={{0,8},{4,0},{8,16},{12,4},{16,24},{20,12},{24,28},{28,20},{1,9},{5... | collective-permute-start | bytes 5505032 | tf_op jit(solution)/shard_map/ppermute | solution.py:231
  112.6 4.5 %copy-start.16 = (bf16[256,4096]{1,0:T(8,128)(2,1)}, bf16[256,4096]{1,0:T(8,128)(2,1)S(1)}, u32[]{:S(2)}) copy-start(bf16[256,4096]{1,0:T(8,128)(2,1)S(1)} %collective-permute-done.18.refs_2_) | copy-start | bytes 6291460
  112.6 62.2 %collective-permute-start.13 = (bf16[128,4096]{1,0:T(8,128)(2,1)}, bf16[128,4096]{1,0:T(8,128)(2,1)S(1)}, u32[]{:S(2)}, u32[]{:S(2)}) collective-permute-start(bf16[128,4096]{1,0:T(8,128)(2,1)} %collective-permute-done.5), channel_id=1, source_target_pairs={{0,4},{4,12},{8,0},{12,20},{16,8},{20,28},{24,16},{28,24},{1,5},{5... | collective-permute-start | bytes 3145736 | tf_op jit(solution)/shard_map/ppermute | solution.py:231
  115.6 60.5 %collective-permute-start.14 = (bf16[128,4096]{1,0:T(8,128)(2,1)}, bf16[128,4096]{1,0:T(8,128)(2,1)S(1)}, u32[]{:S(2)}, u32[]{:S(2)}) collective-permute-start(bf16[128,4096]{1,0:T(8,128)(2,1)} %collective-permute-done.6), channel_id=1, source_target_pairs={{0,8},{4,0},{8,16},{12,4},{16,24},{20,12},{24,28},{28,20},{1,9},{5... | collective-permute-start | bytes 3145736 | tf_op jit(solution)/shard_map/ppermute | solution.py:231
  176.1 2.1 copy-start.19
  176.2 6.7 %collective-permute-start.25 = (bf16[256,4096]{1,0:T(8,128)(2,1)}, bf16[256,4096]{1,0:T(8,128)(2,1)S(1)}, u32[]{:S(2)}, u32[]{:S(2)}) collective-permute-start(bf16[256,4096]{1,0:T(8,128)(2,1)} %pad_maximum_fusion.1.refs_1_), channel_id=1, source_target_pairs={{0,1},{1,0},{2,3},{3,2},{4,5},{5,4},{6,7},{7,6},{8,9},{9,8},{10,11... | collective-permute-start | bytes 6291464 | tf_op jit(solution)/shard_map/ppermute | solution.py:234
  176.3 8.2 %collective-permute-start.26 = (bf16[256,4096]{1,0:T(8,128)(2,1)S(1)}, bf16[256,4096]{1,0:T(8,128)(2,1)S(1)}, u32[]{:S(2)}, u32[]{:S(2)}) collective-permute-start(bf16[256,4096]{1,0:T(8,128)(2,1)S(1)} %collective-permute-done.17.refs_3_), channel_id=1, source_target_pairs={{0,1},{1,0},{2,3},{3,2},{4,5},{5,4},{6,7},{7,6},{8,9},{9,8},{10,11... | collective-permute-start | bytes 6291464 | tf_op jit(solution)/shard_map/ppermute | solution.py:234
  177.6 54.5 %copy-start.4 = (bf16[256,4096]{1,0:T(8,128)(2,1)}, bf16[256,4096]{1,0:T(8,128)(2,1)S(1)}, u32[]{:S(2)}) copy-start(bf16[256,4096]{1,0:T(8,128)(2,1)S(1)} %constant_dynamic-update-slice_fusion.refs_1_) | copy-start | bytes 6291460
  177.6 54.5 %collective-permute-start.24 = (bf16[256,4096]{1,0:T(8,128)(2,1)S(1)}, bf16[256,4096]{1,0:T(8,128)(2,1)S(1)}, u32[]{:S(2)}, u32[]{:S(2)}) collective-permute-start(bf16[256,4096]{1,0:T(8,128)(2,1)S(1)} %constant_dynamic-update-slice_fusion.refs_1_), channel_id=1, source_target_pairs={{0,2},{1,3},{2,0},{3,1},{4,6},{5,7},{6,4},{7,5},{8,10},{9,11},{10,... | collective-permute-start | bytes 6291464 | tf_op jit(solution)/shard_map/ppermute | solution.py:234
  178.2 53.9 %collective-permute-start.22 = (bf16[512,1792]{1,0:T(8,128)(2,1)S(1)}, bf16[512,1792]{1,0:T(8,128)(2,1)S(1)}, u32[]{:S(2)}, u32[]{:S(2)}) collective-permute-start(bf16[512,1792]{1,0:T(8,128)(2,1)S(1)} %collective-permute-done.15.refs_8_), channel_id=1, source_target_pairs={{0,4},{4,12},{8,0},{12,20},{16,8},{20,28},{24,16},{28,24},{1,5},{5... | collective-permute-start | bytes 5505032 | tf_op jit(solution)/shard_map/ppermute | solution.py:231
  179.8 52.3 %collective-permute-start.23 = (bf16[512,1792]{1,0:T(8,128)(2,1)}, bf16[512,1792]{1,0:T(8,128)(2,1)S(1)}, u32[]{:S(2)}, u32[]{:S(2)}) collective-permute-start(bf16[512,1792]{1,0:T(8,128)(2,1)} %collective-permute-done.16.refs_7_), channel_id=1, source_target_pairs={{0,8},{4,0},{8,16},{12,4},{16,24},{20,12},{24,28},{28,20},{1,9},{5... | collective-permute-start | bytes 5505032 | tf_op jit(solution)/shard_map/ppermute | solution.py:231
  182.8 2.2 copy-start.13
  182.8 47.8 %collective-permute-start.20 = (bf16[64,4096]{1,0:T(8,128)(2,1)S(1)}, bf16[64,4096]{1,0:T(8,128)(2,1)S(1)}, u32[]{:S(2)}, u32[]{:S(2)}) collective-permute-start(bf16[64,4096]{1,0:T(8,128)(2,1)S(1)} %slice.58), channel_id=1, source_target_pairs={{0,4},{4,12},{8,0},{12,20},{16,8},{20,28},{24,16},{28,24},{1,5},{5... | collective-permute-start | bytes 1572872 | tf_op jit(solution)/shard_map/ppermute | solution.py:231
  184.4 47.7 %collective-permute-start.21 = (bf16[64,4096]{1,0:T(8,128)(2,1)S(1)}, bf16[64,4096]{1,0:T(8,128)(2,1)S(1)}, u32[]{:S(2)}, u32[]{:S(2)}) collective-permute-start(bf16[64,4096]{1,0:T(8,128)(2,1)S(1)} %slice.59), channel_id=1, source_target_pairs={{0,8},{4,0},{8,16},{12,4},{16,24},{20,12},{24,28},{28,20},{1,9},{5... | collective-permute-start | bytes 1572872 | tf_op jit(solution)/shard_map/ppermute | solution.py:231
  232.1 3.9 %copy-start.5 = (bf16[512,1792]{1,0:T(8,128)(2,1)}, bf16[512,1792]{1,0:T(8,128)(2,1)S(1)}, u32[]{:S(2)}) copy-start(bf16[512,1792]{1,0:T(8,128)(2,1)S(1)} %collective-permute-done.22.refs_8_) | copy-start | bytes 5505028
  232.1 3.9 %copy-start.6 = (bf16[512,1792]{1,0:T(8,128)(2,1)}, bf16[512,1792]{1,0:T(8,128)(2,1)S(1)}, u32[]{:S(2)}) copy-start(bf16[512,1792]{1,0:T(8,128)(2,1)S(1)} %collective-permute-done.23.refs_7_) | copy-start | bytes 5505028
  232.1 3.9 %copy-start.11 = (bf16[256,4096]{1,0:T(8,128)(2,1)}, bf16[256,4096]{1,0:T(8,128)(2,1)S(1)}, u32[]{:S(2)}) copy-start(bf16[256,4096]{1,0:T(8,128)(2,1)S(1)} %collective-permute-done.24.refs_3_) | copy-start | bytes 6291460
  232.2 4.7 %collective-permute-start.30 = (bf16[256,4096]{1,0:T(8,128)(2,1)S(1)}, bf16[256,4096]{1,0:T(8,128)(2,1)S(1)}, u32[]{:S(2)}, u32[]{:S(2)}) collective-permute-start(bf16[256,4096]{1,0:T(8,128)(2,1)S(1)} %constant_dynamic-update-slice_fusion.refs_1_), channel_id=1, source_target_pairs={{0,1},{1,0},{2,3},{3,2},{4,5},{5,4},{6,7},{7,6},{8,9},{9,8},{10,11... | collective-permute-start | bytes 6291464 | tf_op jit(solution)/shard_map/ppermute | solution.py:234
  232.2 7.1 %collective-permute-start.31 = (bf16[256,4096]{1,0:T(8,128)(2,1)S(1)}, bf16[256,4096]{1,0:T(8,128)(2,1)S(1)}, u32[]{:S(2)}, u32[]{:S(2)}) collective-permute-start(bf16[256,4096]{1,0:T(8,128)(2,1)S(1)} %collective-permute-done.24.refs_3_), channel_id=1, source_target_pairs={{0,1},{1,0},{2,3},{3,2},{4,5},{5,4},{6,7},{7,6},{8,9},{9,8},{10,11... | collective-permute-start | bytes 6291464 | tf_op jit(solution)/shard_map/ppermute | solution.py:234
  232.8 51.3 %copy-start.7 = (bf16[128,4096]{1,0:T(8,128)(2,1)}, bf16[128,4096]{1,0:T(8,128)(2,1)S(1)}, u32[]{:S(2)}) copy-start(bf16[128,4096]{1,0:T(8,128)(2,1)S(1)} %constant_dynamic-update-slice_fusion.2.refs_1_) | copy-start | bytes 3145732
  232.8 51.3 %collective-permute-start.29 = (bf16[128,4096]{1,0:T(8,128)(2,1)S(1)}, bf16[128,4096]{1,0:T(8,128)(2,1)S(1)}, u32[]{:S(2)}, u32[]{:S(2)}) collective-permute-start(bf16[128,4096]{1,0:T(8,128)(2,1)S(1)} %constant_dynamic-update-slice_fusion.2.refs_1_), channel_id=1, source_target_pairs={{0,2},{1,3},{2,0},{3,1},{4,6},{5,7},{6,4},{7,5},{8,10},{9,11},{10,... | collective-permute-start | bytes 3145736 | tf_op jit(solution)/shard_map/ppermute | solution.py:234
  234.4 49.7 %collective-permute-start.27 = (bf16[256,1792]{1,0:T(8,128)(2,1)S(1)}, bf16[256,1792]{1,0:T(8,128)(2,1)S(1)}, u32[]{:S(2)}, u32[]{:S(2)}) collective-permute-start(bf16[256,1792]{1,0:T(8,128)(2,1)S(1)} %slice.60), channel_id=1, source_target_pairs={{0,4},{4,12},{8,0},{12,20},{16,8},{20,28},{24,16},{28,24},{1,5},{5... | collective-permute-start | bytes 2752520 | tf_op jit(solution)/shard_map/ppermute | solution.py:231
  236.1 48.1 %collective-permute-start.28 = (bf16[256,1792]{1,0:T(8,128)(2,1)S(1)}, bf16[256,1792]{1,0:T(8,128)(2,1)S(1)}, u32[]{:S(2)}, u32[]{:S(2)}) collective-permute-start(bf16[256,1792]{1,0:T(8,128)(2,1)S(1)} %slice.61), channel_id=1, source_target_pairs={{0,8},{4,0},{8,16},{12,4},{16,24},{20,12},{24,28},{28,20},{1,9},{5... | collective-permute-start | bytes 2752520 | tf_op jit(solution)/shard_map/ppermute | solution.py:231
  236.9 2.5 copy-start.15
  284.1 4.3 %copy-start.25 = (bf16[256,1792]{1,0:T(8,128)(2,1)}, bf16[256,1792]{1,0:T(8,128)(2,1)S(1)}, u32[]{:S(2)}) copy-start(bf16[256,1792]{1,0:T(8,128)(2,1)S(1)} %collective-permute-done.27.refs_8_) | copy-start | bytes 2752516
  284.1 4.3 %copy-start.26 = (bf16[256,1792]{1,0:T(8,128)(2,1)}, bf16[256,1792]{1,0:T(8,128)(2,1)S(1)}, u32[]{:S(2)}) copy-start(bf16[256,1792]{1,0:T(8,128)(2,1)S(1)} %collective-permute-done.28.refs_7_) | copy-start | bytes 2752516
  284.2 4.3 %copy-start.22 = (bf16[128,4096]{1,0:T(8,128)(2,1)}, bf16[128,4096]{1,0:T(8,128)(2,1)S(1)}, u32[]{:S(2)}) copy-start(bf16[128,4096]{1,0:T(8,128)(2,1)S(1)} %collective-permute-done.29.refs_3_) | copy-start | bytes 3145732
  284.2 42.9 %copy-start.27 = (f32[3]{0:T(128)S(1)}, f32[3]{0:T(128)}, u32[]{:S(2)}) copy-start(f32[3]{0:T(128)} %param.16) | copy-start | bytes 40
  284.2 45.4 %copy-start.28 = (s32[8]{0:T(128)S(1)}, s32[8]{0:T(128)}, u32[]{:S(2)}) copy-start(s32[8]{0:T(128)} %param.15) | copy-start | bytes 100
  284.2 2.7 collective-permute-start.32
  284.4 4.0 %collective-permute-start.33 = (bf16[128,4096]{1,0:T(8,128)(2,1)S(1)}, bf16[128,4096]{1,0:T(8,128)(2,1)S(1)}, u32[]{:S(2)}, u32[]{:S(2)}) collective-permute-start(bf16[128,4096]{1,0:T(8,128)(2,1)S(1)} %collective-permute-done.29.refs_3_), channel_id=1, source_target_pairs={{0,1},{1,0},{2,3},{3,2},{4,5},{5,4},{6,7},{7,6},{8,9},{9,8},{10,11... | collective-permute-start | bytes 3145736 | tf_op jit(solution)/shard_map/ppermute | solution.py:234
  326.9 1.2 collective-permute-start.34
  328.1 3.6 %collective-permute-start.35 = (f32[8,128]{1,0:T(8,128)S(1)}, f32[8,128]{1,0:T(8,128)S(1)}, u32[]{:S(2)}, u32[]{:S(2)}) collective-permute-start(f32[8,128]{1,0:T(8,128)S(1)} %add.78), channel_id=1, source_target_pairs={{0,2},{1,3},{2,0},{3,1},{4,6},{5,7},{6,4},{7,5},{8,10},{9,11},{10,... | collective-permute-start | bytes 12296 | tf_op jit(solution)/shard_map/ppermute | solution.py:389
  331.7 3.6 %collective-permute-start.36 = (f32[8,128]{1,0:T(8,128)S(1)}, f32[8,128]{1,0:T(8,128)S(1)}, u32[]{:S(2)}, u32[]{:S(2)}) collective-permute-start(f32[8,128]{1,0:T(8,128)S(1)} %add.79), channel_id=1, source_target_pairs={{0,4},{1,5},{2,6},{3,7},{4,0},{5,1},{6,2},{7,3},{8,12},{9,13},{10,... | collective-permute-start | bytes 12296 | tf_op jit(solution)/shard_map/ppermute | solution.py:389
  335.3 3.6 %collective-permute-start.37 = (f32[8,128]{1,0:T(8,128)S(1)}, f32[8,128]{1,0:T(8,128)S(1)}, u32[]{:S(2)}, u32[]{:S(2)}) collective-permute-start(f32[8,128]{1,0:T(8,128)S(1)} %add.80), channel_id=1, source_target_pairs={{0,8},{1,9},{2,10},{3,11},{4,12},{5,13},{6,14},{7,15},{8,0},{9,1},... | collective-permute-start | bytes 12296 | tf_op jit(solution)/shard_map/ppermute | solution.py:389
  338.9 4.5 %collective-permute-start.38 = (f32[8,128]{1,0:T(8,128)S(1)}, f32[8,128]{1,0:T(8,128)S(1)}, u32[]{:S(2)}, u32[]{:S(2)}) collective-permute-start(f32[8,128]{1,0:T(8,128)S(1)} %add.81), channel_id=1, source_target_pairs={{0,16},{1,17},{2,18},{3,19},{4,20},{5,21},{6,22},{7,23},{8,24},{9,... | collective-permute-start | bytes 12296 | tf_op jit(solution)/shard_map/ppermute | solution.py:389
  (6 other events, 8.1 us)
